TPU v7x, 32 devices: a whole 2x2x4 slice. The times are simulated.
32 devices in a mesh: dp: 8 (over z, x), fsdp: 4 (over y, core).
Axes of the slice: x: 2, y: 2, z: 4, core: 2. Of those that a mesh axis runs over, the one named last changes fastest.
Arguments:
- patches: bfloat16 [128, 153, 768], P(('dp', 'fsdp')), may hold values from -6 to 6
- counts: int32 [128], P(('dp', 'fsdp')), may hold values from 26 to 153, as said below
- positions: int32 [128, 153], P(('dp', 'fsdp')), may hold values from 0 to 255, as said below
- ln1_gain: bfloat16 [768], P(('dp', 'fsdp')), may hold values from 0.5 to 1.5
- ln1_bias: bfloat16 [768], P(('dp', 'fsdp')), may hold values from -1 to 1
- qkv_weight: bfloat16 [768, 2304], P(('dp', 'fsdp')), may hold values from -0.21875 to 0.21875
- qv_bias: bfloat16 [1536], P(('dp', 'fsdp')), may hold values from -1.5 to 1.5
- out_weight: bfloat16 [768, 768], P(('dp', 'fsdp')), may hold values from -0.625 to 0.625
- out_bias: bfloat16 [768], P(('dp', 'fsdp')), may hold values from -1 to 1
- ln2_gain: bfloat16 [768], P(('dp', 'fsdp')), may hold values from 0.5 to 1.5
- ln2_bias: bfloat16 [768], P(('dp', 'fsdp')), may hold values from -1 to 1
- fc1_weight: bfloat16 [768, 3072], P(('dp', 'fsdp')), may hold values from -0.21875 to 0.21875
- fc1_bias: bfloat16 [3072], P(('dp', 'fsdp')), may hold values from -1.5 to 1.5
- fc2_weight: bfloat16 [3072, 768], P(('dp', 'fsdp')), may hold values from -0.109375 to 0.109375
- fc2_bias: bfloat16 [768], P(('dp', 'fsdp')), may hold values from -1 to 1
- cotangent: bfloat16 [128, 153, 768], P(('dp', 'fsdp')), may hold values from -6 to 6
Outputs:
- output: bfloat16 [128, 153, 768], P(('dp', 'fsdp'))
- input_grad: bfloat16 [128, 153, 768], P(('dp', 'fsdp'))
- ln1_gain_grad: float32 [768], P(('dp', 'fsdp'))
- ln1_bias_grad: float32 [768], P(('dp', 'fsdp'))
- qkv_weight_grad: float32 [768, 2304], P(('dp', 'fsdp'))
- qv_bias_grad: float32 [1536], P(('dp', 'fsdp'))
- out_weight_grad: float32 [768, 768], P(('dp', 'fsdp'))
- out_bias_grad: float32 [768], P(('dp', 'fsdp'))
- ln2_gain_grad: float32 [768], P(('dp', 'fsdp'))
- ln2_bias_grad: float32 [768], P(('dp', 'fsdp'))
- fc1_weight_grad: float32 [768, 3072], P(('dp', 'fsdp'))
- fc1_bias_grad: float32 [3072], P(('dp', 'fsdp'))
- fc2_weight_grad: float32 [3072, 768], P(('dp', 'fsdp'))
- fc2_bias_grad: float32 [768], P(('dp', 'fsdp'))
Inputs may be any that keep to these rules, and one draw needn't show every extreme that they name: `counts`: rows at and beyond an image's count are padding; some image has exactly 153. `positions`: row index times 16 plus column index of the patch on the image's grid, distinct within an image; padding rows hold some grid index too.
All inputs are finite; a program needn't handle non-finite values.
Results may differ from a plain program's by a relative error of at most 0.012.
Values may be sent and summed in bfloat16 or wider, within the bound.
No kernel may reach another device: no remote copies, remote signals or barrier semaphores. Data moves between devices by JAX's collectives and lax.ppermute only.
A program may use at most 192 MiB of HBM per device.

v0:
```python
import math

import jax
import jax.numpy as jnp
import numpy as np
from jax import lax
from jax.experimental import pallas as pl
from jax.experimental.pallas import tpu as pltpu
from jax.sharding import PartitionSpec as P

HEADS = 12
SIDE = 16
EPSILON = 1e-06
AXES = ("dp", "fsdp")
FAR = 1e30
CHIPS = 16
BLOCK = 384
SMALL, LARGE = (32, 96), (112, 128)
MIB = 1024 * 1024

BF = jnp.bfloat16
F32 = jnp.float32


def power_slopes(number):
    first_slope = 2.0 ** (-8.0 / number)
    return [first_slope ** (index + 1) for index in range(number)]


def slope_list(heads_total):
    lower_power = 2 ** int(math.floor(math.log2(heads_total)))
    return (
        power_slopes(lower_power) + power_slopes(2 * lower_power)[0::2][: heads_total - lower_power]
    )


SLOPES = [float(np.float32(slope)) for slope in slope_list(HEADS)]


def dot(left, right, left_dim=1, right_dim=0):
    return lax.dot_general(
        left, right, (((left_dim,), (right_dim,)), ((), ())), preferred_element_type=F32
    )


def normed_rows(values):
    centered = values - jnp.mean(values, axis=-1, keepdims=True)
    scale = lax.rsqrt(jnp.mean(centered * centered, axis=-1, keepdims=True) + EPSILON)
    return centered * scale, scale


def norm_back(grad_normed, normed, scale):
    centered_mean = jnp.mean(grad_normed, axis=-1, keepdims=True)
    projected_mean = jnp.mean(grad_normed * normed, axis=-1, keepdims=True)
    return scale * (grad_normed - centered_mean - normed * projected_mean)


def row_of(vectors_ref, index):
    return jnp.concatenate(
        [vectors_ref[0, index : index + 1, :], vectors_ref[1, index : index + 1, :]], axis=1
    )


def gelu_parts(hidden):
    cumulative = 0.5 + 0.5 * lax.erf(hidden * math.sqrt(0.5))
    bell = jnp.exp(-0.5 * hidden * hidden)
    return cumulative, cumulative + hidden * bell * (1.0 / math.sqrt(2.0 * math.pi))


def share_kernel(place, qkv_ref, out_ref, fc1_ref, *refs):
    smalls, (mine_ref, theirs_ref, lines_ref) = refs[:-3], refs[-3:]
    for target, core in ((mine_ref, place[48]), (theirs_ref, 1 - place[48])):
        starts = [(qkv_ref, 2 * BLOCK * part + BLOCK * core) for part in range(3)]
        starts.append((out_ref, BLOCK * core))
        starts += [(fc1_ref, 4 * BLOCK * core + BLOCK * part) for part in range(4)]
        for block, (source, start) in enumerate(starts):
            target[block] = source[:, pl.ds(pl.multiple_of(start, 128), BLOCK)]
    device = place[49]
    lines = []
    for small in smalls:
        count = small.shape[0]
        line = small[...].astype(F32).reshape(1, count)
        line = jnp.concatenate([line, jnp.zeros((1, BLOCK - count), F32)], axis=1)
        lines.append(pltpu.roll(line, lax.rem(device, BLOCK // count) * count, 1))
    lines_ref[...] = jnp.concatenate(lines + [jnp.zeros((8, BLOCK), F32)], axis=0).astype(BF)


def pair_kernel(place, mine_ref, got_ref, lines_ref, fc2_ref, a_ref, b1_ref, b2_ref):
    swap = place[48] == 1
    for block in range(8):
        mine, got = mine_ref[block].astype(F32), got_ref[block].astype(F32)
        rows = jnp.concatenate([jnp.where(swap, got, mine), jnp.where(swap, mine, got)], axis=0)
        if block < 3:
            a_ref[48 * block : 48 * (block + 1), :] = rows.astype(BF)
        elif block == 3:
            b2_ref[192:240, :] = rows.astype(BF)
        else:
            b1_ref[48 * (block - 4) : 48 * (block - 3), :] = rows.astype(BF)
    b2_ref[0:96, :] = fc2_ref[:, :BLOCK]
    b2_ref[96:192, :] = fc2_ref[:, BLOCK:]
    a_ref[144:160, :] = lines_ref[...]


def each_piece(place, table, sources, work):
    core = place[48]
    for number, source in enumerate(sources):
        half = core if number < 2 else 1 - core

        def bring(index, _, source=source, number=number, half=half):
            work(source, index, place[table + number * 8 + index], half)
            return 0

        lax.fori_loop(0, 8, bring, 0)


def bring_out_weight(place, sources, wo, sem, table):
    def work(source, index, chip, half):
        spot = pl.ds(pl.multiple_of(chip * 48, 16), 48)
        pltpu.make_async_copy(source.at[index, pl.ds(192, 48)], wo.at[half, spot], sem).start()

    each_piece(place, table, sources, work)


def bring_qkv_weight(place, sources, side, wq, sem, part_of=None):
    for first, here in ((0, place[48] == side), (2, place[48] != side)):

        @pl.when(here)
        def _(first=first):
            for number in (first, first + 1):

                def bring(index, _, source=sources[number], number=number):
                    spot = pl.ds(pl.multiple_of(place[number * 8 + index] * 48, 16), 48)
                    for part in range(3):
                        pltpu.make_async_copy(
                            source.at[index, pl.ds(48 * part, 48)],
                            wq.at[spot, pl.ds(BLOCK * part, BLOCK)] if part_of is None else wq.at[part, spot],
                            sem if part_of is None else part_of.at[part],
                        ).start()
                    return 0

                lax.fori_loop(0, 8, bring, 0)


def wait_all(buffer, sem):
    pltpu.make_async_copy(buffer, buffer, sem).wait()


def two_heads(pair_rows, low_half):
    nothing = jnp.zeros_like(pair_rows)
    return jnp.concatenate(
        [jnp.where(low_half, pair_rows, nothing), jnp.where(low_half, nothing, pair_rows)], axis=0
    )


def first_kernel(
    place, own0, own1, other0, other1, rows_ref, far_ref,
    vec_ref, fcb_ref, h1_turned, qkv_ref, att_ref, wq_out0, wq_out1,
    wq, h1, qvb, small, sems,
):
    sources = (own0, own1, other0, other1)

    def work(source, index, chip, half):
        pltpu.make_async_copy(
            source.at[index, pl.ds(144, 16)], small.at[2 * chip + half], sems.at[2]
        ).start()

    each_piece(place, 0, sources, work)
    for half in range(2):
        bring_qkv_weight(place, sources, half, wq.at[half], sems.at[half])
    normed, _ = normed_rows(rows_ref[...].astype(F32))
    wait_all(small, sems.at[2])
    spread = small[...].astype(F32)
    vec_ref[...] = jnp.sum(spread.reshape(2, 16, 16, BLOCK), axis=1)
    qvb[...] = jnp.sum(spread.reshape(4, 8, 16, BLOCK), axis=1)
    lines = jnp.sum(spread.reshape(8, 4, 16, BLOCK), axis=1)
    for block in range(4):
        fcb_ref[block] = jnp.concatenate([lines[2 * block, 7:8], lines[2 * block + 1, 7:8]], axis=1)
    low = (normed * row_of(vec_ref, 0) + row_of(vec_ref, 1)).astype(BF)
    h1[...] = low
    h1_turned[...] = low.T

    def one_side(side, _):
        wait_all(wq.at[side], sems.at[side])
        for half, target in enumerate((wq_out0, wq_out1)):

            @pl.when(side == half)
            def _(half=half, target=target):
                pltpu.make_async_copy(wq.at[half], target, sems.at[3 + half]).start()

        bias = jnp.concatenate(
            [qvb[side, 6:7, :], jnp.zeros((1, BLOCK), F32), qvb[2 + side, 6:7, :]], axis=1
        )
        qkv_ref[side] = (dot(h1[...], wq[side]) + bias).astype(BF)
        return 0

    lax.fori_loop(0, 2, one_side, 0)
    length = far_ref.shape[1]
    low_half = lax.broadcasted_iota(jnp.int32, (length, 128), 1) < 64

    def one_image(image, _):
        here = pl.ds(pl.multiple_of(image * length, 32), length)
        far = far_ref[image]
        for pair in range(HEADS // 2):
            side, at = pair // 3, 128 * (pair % 3)
            queries = two_heads(qkv_ref[side, here, at : at + 128] * jnp.asarray(0.125, BF), low_half)
            key_rows = qkv_ref[side, here, BLOCK + at : BLOCK + at + 128]
            values = qkv_ref[side, here, 2 * BLOCK + at : 2 * BLOCK + at + 128]
            both = dot(queries, key_rows, 1, 1)
            probs = []
            for head in range(2):
                scores = both[length * head : length * (head + 1)] - SLOPES[2 * pair + head] * far
                shifted = jnp.exp(scores - jnp.max(scores, axis=-1, keepdims=True))
                share = shifted * (1.0 / jnp.sum(shifted, axis=-1, keepdims=True))
                probs.append(share.astype(BF))
            result = dot(jnp.concatenate(probs, axis=0), values)
            att_ref[here, 128 * pair : 128 * (pair + 1)] = jnp.where(
                low_half, result[:length], result[length:]
            ).astype(BF)
        return 0

    lax.fori_loop(0, far_ref.shape[0], one_image, 0)
    wait_all(wq_out0, sems.at[3])
    wait_all(wq_out1, sems.at[4])


def at_slot(target, slot, work):
    if not isinstance(target, tuple):
        work(target, slot)
        return

    @pl.when(slot >= 8)
    def _():
        work(target[0], slot - 8)

    @pl.when(slot < 8)
    def _():
        work(target[1], slot)


def give_rows(place, tables, total, keep_ref, send_ref, extra=None, lanes=slice(None)):
    for group in range(1 if extra is None else 4):
        below = None if extra is None else extra(group)

        def one_chip(index, _, group=group, below=below):
            chip = 4 * group + index
            for which, target in enumerate((keep_ref, send_ref)):
                owner = place[48] if which == 0 else 1 - place[48]
                share = total[pl.ds(pl.multiple_of(48 * chip + 24 * owner, 8), 24), :]
                if below is not None:
                    share = jnp.concatenate([share, below], axis=0)

                def put(ref, slot, share=share):
                    ref[slot, :, lanes] = share.astype(BF)

                at_slot(target, place[tables[which] + chip], put)
            return 0

        lax.fori_loop(0, CHIPS if extra is None else 4, one_chip, 0)


def stack_rows(rows):
    blank = jnp.zeros_like(next(row for row in rows if row is not None))
    rows = [blank if row is None else row for row in rows]
    return jnp.concatenate(rows + [blank] * (8 - len(rows)), axis=0)


def sum_rows(values):
    return jnp.sum(values.astype(F32), axis=0, keepdims=True)


def mlp_kernel(
    place, counts, a0, a1, a2, a3, b0, b1, b2, b3, att_far, rows_far, gout_far, vec_ref, fcb_ref,
    out_ref, glow_ref, keep1_ref, send1_ref, sums_ref, fcg, keep2, upper2, lower2, wo_out,
    w1, w2, wo, att_ref, rows_ref, gout_ref, h2, h2_turned, normed, total, gh2, product1, product2,
    stage, scales, sems1, sems2, sems,
):
    step = pl.program_id(0)
    wide = 2 * BLOCK
    core, z = place[48], place[50]
    block_of = lambda step: lax.rem(z + 4 - step, 4)
    block = block_of(step)
    gain = row_of(vec_ref, 3)
    loads = [
        pltpu.make_async_copy(source, target, sems.at[3 + index])
        for index, (source, target) in enumerate(
            ((att_far, att_ref), (rows_far, rows_ref), (gout_far, gout_ref))
        )
    ]

    @pl.when(step == 0)
    def _():
        bring_out_weight(place, (b0, b1, b2, b3), wo, sems.at[2], 144)
        loads[0].start()
        loads[1].start()
        loads[2].start()

        def one_block(later, _):
            column = block_of(later)
            for first, here in ((0, column // 2 == core), (2, column // 2 != core)):

                @pl.when(here)
                def _(first=first):
                    for number in (first, first + 1):

                        def bring(index, _, source=(a0, a1, a2, a3)[number], number=number):
                            spot = pl.ds(pl.multiple_of(place[64 + number * 8 + index] * 48, 16), 48)
                            for part in range(2):
                                start = pl.multiple_of(lax.rem(column, 2) * 96 + 48 * part, 16)
                                pltpu.make_async_copy(
                                    source.at[index, pl.ds(start, 48)],
                                    w1.at[column, spot, pl.ds(BLOCK * part, BLOCK)],
                                    sems1.at[column],
                                ).start()
                            return 0

                        lax.fori_loop(0, 8, bring, 0)

            for number, source in enumerate((b0, b1, b2, b3)):
                half = core if number < 2 else 1 - core
                for index in (later, jnp.where(later < 2, 4 + later, 9 - later)):
                    chip = place[144 + number * 8 + index]
                    spot = pl.ds(pl.multiple_of(chip * 192 + half * 96, 16), 96)
                    for part in range(2):
                        pltpu.make_async_copy(
                            source.at[index, pl.ds(96 * part, 96)],
                            w2.at[spot, pl.ds(BLOCK * part, BLOCK)],
                            sems2.at[column],
                        ).start()
            return 0

        lax.fori_loop(0, 4, one_block, 0)
        wait_all(wo, sems.at[2])
        pltpu.make_async_copy(wo, wo_out, sems.at[2]).start()
        bias = row_of(vec_ref, 2)
        loads[0].wait()
        loads[1].wait()
        for part in range(2):
            lanes = slice(BLOCK * part, BLOCK * (part + 1))
            total[:, lanes] = rows_ref[:, lanes].astype(F32) + dot(att_ref[...], wo[part]) + bias[:, lanes]
        normal, scale = normed_rows(total[...])
        normed[...] = normal
        scales[...] = jnp.broadcast_to(scale, scales.shape)
        low = (normal * gain + row_of(vec_ref, 4)).astype(BF)
        h2[...] = low
        h2_turned[...] = low.T
        total[...] += row_of(vec_ref, 5)
        gh2[...] = jnp.zeros_like(gh2)
        loads[2].wait()

    wait_all(w1.at[block], sems1.at[block])
    hidden = dot(h2[...], w1[block]) + fcb_ref[block]
    rows_of = pl.ds(pl.multiple_of(block * wide, wide), wide)
    wait_all(w2.at[rows_of], sems2.at[block])
    gactivated = dot(gout_ref[...], w2[rows_of, :], 1, 1)
    cumulative, slope = gelu_parts(hidden)
    activated = (hidden * cumulative).astype(BF)
    ghidden = (gactivated * slope).astype(BF)
    product1[...] = dot(h2_turned[...], ghidden)
    product2[...] = dot(activated, gout_ref[...], 0, 0)
    total[...] += dot(activated, w2[rows_of, :])
    gh2[...] += dot(ghidden, w1[block], 1, 1)
    fcg[block] = stack_rows([None, None, None, sum_rows(ghidden)])
    give_rows(place, LARGE, product1, keep1_ref, send1_ref)
    for pair in range(4):
        chip = 4 * block + pair
        for which, target in enumerate((keep2, (upper2, lower2))):
            owner = place[48] if which == 0 else 1 - place[48]
            start = pl.multiple_of(192 * pair + 96 * owner, 8)
            stage[which, chip] = product2[pl.ds(start, 96), :].astype(BF)

            def send(ref, slot, which=which, chip=chip):
                sem = sems.at[1 if ref is upper2 else 6 if ref is lower2 else 0]
                pltpu.make_async_copy(stage.at[which, chip], ref.at[slot], sem).start()

            at_slot(target, place[LARGE[which] + chip], send)

    @pl.when(step == pl.num_programs(0) - 1)
    def _():
        length = out_ref.shape[0] // 4
        row_index = lax.broadcasted_iota(jnp.int32, (length, 1), 0)
        for image in range(4):
            rows = slice(length * image, length * (image + 1))
            value = total[rows, :]
            out_ref[rows, :] = jnp.where(row_index < counts[image], value, 0.0).astype(BF)
        whole = gh2[...]
        gout = gout_ref[...].astype(F32)
        gresid = gout + norm_back(whole * gain, normed[...], scales[:, 0:1])
        low = gresid.astype(BF)
        glow_ref[...] = low
        sums_ref[...] = stack_rows(
            [sum_rows(whole * normed[...]), sum_rows(whole), sum_rows(gout), None, sum_rows(low)]
        )
        wait_all(wo, sems.at[2])
        wait_all(keep2, sems.at[0])
        wait_all(upper2, sems.at[1])
        wait_all(lower2, sems.at[6])


def attention_back_kernel(side, wo, qkv_ref, far_ref, glow_ref, gqkv_ref):
    low = glow_ref[...]
    mine = slice(BLOCK * side, BLOCK * (side + 1))
    gatt = (
        dot(low[:, :BLOCK], wo[0, mine, :], 1, 1) + dot(low[:, BLOCK:], wo[1, mine, :], 1, 1)
    ).astype(BF)
    length = low.shape[0]
    low_half = lax.broadcasted_iota(jnp.int32, (length, 128), 1) < 64
    far = far_ref[0]
    for pair in range(3):
        at = 128 * pair
        queries = qkv_ref[0, :, at : at + 128] * jnp.asarray(0.125, BF)
        key_rows = two_heads(qkv_ref[0, :, BLOCK + at : BLOCK + at + 128], low_half)
        values = two_heads(qkv_ref[0, :, 2 * BLOCK + at : 2 * BLOCK + at + 128], low_half)
        grads = gatt[:, at : at + 128]
        both = dot(key_rows, queries, 1, 1)
        gboth = dot(values, grads, 1, 1)
        probs, gscores = [], []
        for head in range(2):
            rows = slice(length * head, length * (head + 1))
            scores = both[rows] - SLOPES[6 * side + 2 * pair + head] * far
            shifted = jnp.exp(scores - jnp.max(scores, axis=0, keepdims=True))
            share = shifted * (1.0 / jnp.sum(shifted, axis=0, keepdims=True))
            weighted = share * gboth[rows]
            probs.append(share.astype(BF))
            inner = jnp.sum(weighted, axis=0, keepdims=True)
            gscores.append((weighted - share * inner).astype(BF))
        probs, gscores = jnp.concatenate(probs, axis=0), jnp.concatenate(gscores, axis=0)
        gvalues = dot(probs, grads)
        gkeys = dot(gscores, queries)
        gqkv_ref[:, at : at + 128] = (dot(gscores, key_rows, 0, 0) * 0.125).astype(BF)
        for which, result in ((1, gkeys), (2, gvalues)):
            gqkv_ref[:, which * BLOCK + at : which * BLOCK + at + 128] = jnp.where(
                low_half, result[:length], result[length:]
            ).astype(BF)


def qkv_grad_kernel(
    place, h1_turned, gqkv_ref, wq_ref, att_ref, glow_ref, gh1_ref, sums_ref, keep_ref, upper_ref, lower_ref,
    product, product_out,
):
    third, wide = gqkv_ref.shape[1], glow_ref.shape[1]
    product[...] = dot(h1_turned[...], gqkv_ref[...])
    product_out[...] = dot(att_ref[...], glow_ref[...], 0, 0)
    gh1_ref[...] = dot(gqkv_ref[...], wq_ref[...], 1, 1)
    sums_ref[...] = sum_rows(gqkv_ref[...])
    send = upper_ref, lower_ref
    give_rows(place, SMALL, product, keep_ref, send, lanes=slice(0, third))
    give_rows(place, SMALL, product_out, keep_ref, send, lanes=slice(third, third + wide))


def input_kernel(
    place, h1_turned, gqkv_ref, wq_ref, before_ref, mlp_ref, fcg_ref, rows_ref, vec_ref, glow_ref, gh1_ref,
    ginput_ref, keep_ref, upper_ref, lower_ref, product,
):
    product[...] = dot(h1_turned[...], gqkv_ref[...])
    sums = sum_rows(gqkv_ref[...])
    gradient = gh1_ref[...] + dot(gqkv_ref[...], wq_ref[...], 1, 1)
    normed, scale = normed_rows(rows_ref[...].astype(F32))
    ginput_ref[...] = (
        glow_ref[...].astype(F32) + norm_back(gradient * row_of(vec_ref, 0), normed, scale)
    ).astype(BF)
    gain, shift = sum_rows(gradient * normed), sum_rows(gradient)
    first, last = slice(0, BLOCK), slice(2 * BLOCK, 3 * BLOCK)
    biases = before_ref[:, first], sums[:, first], before_ref[:, last], sums[:, last]

    def below(group):
        lanes = slice(BLOCK * (group // 2), BLOCK * (group // 2 + 1))
        own = stack_rows([gain[:, lanes], shift[:, lanes], biases[group]])
        return jnp.concatenate([mlp_ref[...] + fcg_ref[group], own], axis=1)

    give_rows(place, SMALL, product, keep_ref, (upper_ref, lower_ref), below)


def add_up(parts):
    return sum(part.astype(F32) for part in parts)


def give_vector(target, line, device):
    count, columns = target.shape[0], line.shape[1]
    start = lax.rem(device, columns // count) * count
    moved = pltpu.roll(line, lax.rem(columns - start, columns), 1)
    target[...] = moved[:, :count].reshape(count)


def last_kernel(place, *refs):
    sources, (qkv_out, out_out), smalls = refs[:12], refs[12:14], refs[14:]
    total_a = add_up([source[0] for source in sources[:6]])
    total_c = add_up([source[0] for source in sources[6:]])
    for part in range(3):
        lanes = slice(BLOCK * part, BLOCK * (part + 1))
        qkv_out[:, 2 * BLOCK * part : 2 * BLOCK * part + BLOCK] = total_a[:, lanes]
        qkv_out[:, 2 * BLOCK * part + BLOCK : 2 * BLOCK * (part + 1)] = total_c[:24, lanes]
    out_out[...] = total_a[:, 3 * BLOCK :]
    device = place[49]
    for line, target in enumerate(smalls[:3]):
        give_vector(target, total_c[24 + line : 25 + line, 2 * BLOCK :], device)
    for line, target in enumerate(smalls[3:]):
        give_vector(target, total_c[24 + line : 25 + line, : 2 * BLOCK], device)


def after(value, *others):
    return lax.optimization_barrier((value,) + others)[0]


class Links:
    def __init__(self, depth):
        self.depth = depth

        def table(move):
            pairs = []
            for z in range(depth):
                for x in range(2):
                    for y in range(2):
                        for c in range(2):
                            nz, nx, ny, nc = move(z, x, y, c)
                            source = (z * 2 + x) * 4 + y * 2 + c
                            pairs.append((source, ((nz % depth) * 2 + nx) * 4 + ny * 2 + nc))
            return pairs

        self.ups = {step: table(lambda z, x, y, c: (z + step, x, y, c)) for step in (1, 2, 3)}
        self.first = table(lambda z, x, y, c: (z, x, 1 - y, c) if c else (z, 1 - x, y, c))
        self.second = table(lambda z, x, y, c: (z, 1 - x, y, c) if c else (z, x, 1 - y, c))
        self.across = table(lambda z, x, y, c: (z, 1 - x, 1 - y, c))
        self.cores = table(lambda z, x, y, c: (z, x, y, 1 - c))
        self.near = table(lambda z, x, y, c: (z ^ 1, x, y, c))
        self.far = table(lambda z, x, y, c: (z ^ 2, x, y, c))

    def move(self, value, pairs):
        return lax.ppermute(value, AXES, pairs)

    def spots(self):
        dp, fsdp = lax.axis_index("dp"), lax.axis_index("fsdp")
        z, x, y, core = dp // 2, dp % 2, fsdp // 2, fsdp % 2

        def chip(c, flip1, flip2, step):
            flip_x = jnp.where(c == 0, flip1, flip2)
            flip_y = jnp.where(c == 0, flip2, flip1)
            return (((z - step) % self.depth) * 2 + (x ^ flip_x)) * 2 + (y ^ flip_y)

        index = jnp.arange(32, dtype=jnp.int32)
        whose = jnp.where(index < 16, core, 1 - core)
        flip2 = (index // 8) % 2
        z_first = chip(whose, (index // 4) % 2, flip2, index % 4)
        x_first = chip(whose, index % 2, (index // 2) % 2, (index // 4) % 4)
        chips = jnp.arange(16, dtype=jnp.int32)
        turn_x, turn_y = ((chips // 2) % 2) ^ x, (chips % 2) ^ y
        far_z = (chips // 4) ^ z
        near, wide_step = far_z % 2, far_z // 2

        def slots(order):
            turns = {"x": turn_x, "y": turn_y, "near": near, "far": wide_step}
            return sum(turns[name] * weight for name, weight in zip(order, (8, 4, 2, 1)))

        others = jnp.stack([core, dp * 4 + fsdp, z]).astype(jnp.int32)
        rest = jnp.concatenate([others, jnp.zeros((13,), jnp.int32)])
        tables = []
        for orders in (
            (("y", "x", "near", "far"), ("x", "y", "near", "far")),
            (("y", "near", "x", "far"), ("x", "near", "y", "far")),
        ):
            both = [slots(order) for order in orders]
            tables += [jnp.where(core == 0, both[0], both[1]), jnp.where(core == 0, both[1], both[0])]
        swapped = jnp.where(index % 8 >= 6, 9 - index % 8, index % 4)
        swapped = chip(whose, (index // 4) % 2, flip2, swapped)
        parts = [z_first, tables[0], rest, x_first] + tables[1:] + [swapped]
        return jnp.concatenate(parts).astype(jnp.int32)

    def gather(self, piece_a, piece_b1, piece_b2, inputs, prepare):
        hold = lax.optimization_barrier
        up = lambda value, step: self.move(value, self.ups[step])
        a_one, a_three, b1_two = hold((up(piece_a, 1), up(piece_a, 3), self.move(piece_b1, self.first)))
        b1_two = jnp.stack([piece_b1, b1_two])
        a_two, b1_four = hold((up(a_one, 1), self.move(b1_two, self.second)))
        a_four = jnp.stack([piece_a, a_one, a_two, a_three])
        b1_four = jnp.concatenate([b1_two, b1_four])
        piece_b2 = after(piece_b2, a_two)
        a_rest, b2_one, b2_three = hold((self.move(a_four, self.first), up(piece_b2, 1), up(piece_b2, 3)))
        early = prepare(*after(inputs, a_rest))
        a_eight = jnp.concatenate([a_four, a_rest])
        b2_rest = self.move(jnp.stack([piece_b2, b2_one, b2_three]), self.first)
        a_other, b2_two, b1_one, b2_rest, early = hold(
            (self.move(a_eight, self.second), up(b2_one, 1), up(after(b1_four, a_rest), 1), b2_rest, early)
        )
        b2_seven = jnp.concatenate([jnp.stack([piece_b2, b2_one, b2_two, b2_three]), b2_rest])
        a = self.finish(a_eight, a_other)
        b1 = b1_four, b1_one, up(b1_one, 1), up(b1_four, 3)
        b2_last, b2_across = self.move(b2_two[None], self.first), self.move(b2_two[None], self.across)
        return a, b1, (b2_seven, b2_last, self.move(b2_seven, self.second), b2_across), early

    def gather_end(self, b1, b2, done):
        b1_four, b1_one, b1_two, b1_three = b1
        b2_seven, b2_last, other_seven, other_last = b2
        b2_last, done = lax.optimization_barrier((b2_last, done))
        b2_mine, b1_mine = jnp.concatenate([b2_seven, b2_last]), jnp.concatenate([b1_four, b1_one])
        b2_theirs, b1_theirs = self.move(b2_mine, self.cores), self.move(b1_mine, self.cores)
        b1_two, b1_three, other_seven, other_last, done = lax.optimization_barrier(
            (b1_two, b1_three, other_seven, other_last, done)
        )
        b2_rest, b1_rest = jnp.concatenate([other_seven, other_last]), jnp.concatenate([b1_two, b1_three])
        b1 = b1_mine, b1_rest, b1_theirs, self.move(b1_rest, self.cores)
        return done, b1, (b2_mine, b2_rest, b2_theirs, self.move(b2_rest, self.cores))

    def finish(self, eight, rest):
        return (eight, rest, self.move(eight, self.cores), self.move(rest, self.cores))

    def fold(self, state):
        left = 32 >> (len(state) - 1)
        return add_up([part[left // 2 : left] for part in state]).astype(BF)

def full_pieces(full, blocks):
    split = full.reshape((CHIPS, 48) + full.shape[1:])
    split = split.transpose(3, 0, 2, 1, 4) if full.shape[1] == blocks else split.transpose(2, 0, 3, 1, 4)
    return split.reshape(2 * CHIPS, blocks * 48, BLOCK)


STILL = [
    16 * core + ((-step % 4) * 2 + (flip2 if core else flip1)) * 2 + (flip1 if core else flip2)
    for core in range(2)
    for flip2 in range(2)
    for flip1 in range(2)
    for step in range(4)
]


STILL_LAST = [STILL[8 * array + index] for array in range(4) for index in (0, 1, 2, 3, 4, 5, 7, 6)]


def eights(pieces, order=None):
    if order is not None:
        pieces = jnp.stack([pieces[index] for index in order])
    return tuple(pieces[8 * index : 8 * (index + 1)] for index in range(4))


def placed(vector, device, per_row):
    start = (device % per_row) * vector.shape[0]
    return lax.dynamic_update_slice(jnp.zeros((BLOCK,), vector.dtype), vector, (start,))


def shards(
    mesh_shape,
    patches,
    counts,
    positions,
    ln1_gain,
    ln1_bias,
    qkv_weight,
    qv_bias,
    out_weight,
    out_bias,
    ln2_gain,
    ln2_bias,
    fc1_weight,
    fc1_bias,
    fc2_weight,
    fc2_bias,
    cotangent,
):
    images, length, width = patches.shape
    padded = (length + 31) // 32 * 32
    rows = images * padded
    hidden_width = fc1_weight.shape[1]
    devices = mesh_shape["dp"] * mesh_shape["fsdp"]
    by_hand = devices == 2 * CHIPS and mesh_shape["fsdp"] == 4
    small_parts = (ln1_gain, ln1_bias, out_bias, ln2_gain, ln2_bias, fc2_bias, qv_bias, fc1_bias)

    smem = pl.BlockSpec(memory_space=pltpu.SMEM)
    vmem = pl.BlockSpec(memory_space=pltpu.VMEM)
    anywhere = pl.BlockSpec(memory_space=pltpu.HBM)
    struct = jax.ShapeDtypeStruct

    def prepare(patches, counts, positions, cotangent):
        row_index = jnp.arange(padded, dtype=jnp.int32)
        is_live = row_index[None, :] < counts[:, None]
        pad_rows = ((0, 0), (0, padded - length), (0, 0))
        rows_in = jnp.pad(patches, pad_rows).reshape(rows, width)
        gout = jnp.where(is_live[:, :, None], jnp.pad(cotangent, pad_rows), 0).reshape(rows, width)
        spots = jnp.pad(positions, pad_rows[:2])
        grid_rows = (spots // SIDE).astype(F32)
        grid_cols = (spots % SIDE).astype(F32)
        row_delta = grid_rows[:, :, None] - grid_rows[:, None, :]
        col_delta = grid_cols[:, :, None] - grid_cols[:, None, :]
        distance = jnp.sqrt(row_delta * row_delta + col_delta * col_delta)
        far = jnp.where(is_live[:, None, :], distance, FAR)
        far_turned = jnp.where(is_live[:, :, None], distance, FAR)
        return rows_in, gout, far, far_turned

    if by_hand:
        links = Links(mesh_shape["dp"] // 2)
        place = links.spots()
        core = place[48]
        share = struct((8, 24, BLOCK), BF)
        mine, theirs, lines = pl.pallas_call(
            share_kernel,
            out_shape=(share, share, struct((16, BLOCK), BF)),
            in_specs=[smem] + [vmem] * 11,
            out_specs=(vmem,) * 3,
            name="share",
        )(place, qkv_weight, out_weight, fc1_weight, *small_parts)
        got = links.move(theirs, links.cores)
        pieces = pl.pallas_call(
            pair_kernel,
            out_shape=tuple(struct((height, BLOCK), BF) for height in (160, 192, 240)),
            in_specs=[smem] + [vmem] * 4,
            out_specs=(vmem,) * 3,
            name="pair",
        )(place, mine, got, lines, fc2_weight)
    else:
        links = None
        place = jnp.concatenate(
            [
                jnp.array([chip % CHIPS for chip in STILL], jnp.int32),
                jnp.arange(16, dtype=jnp.int32),
                jnp.zeros((16,), jnp.int32),
                jnp.arange(80, dtype=jnp.int32) % 16,
                jnp.array([chip % CHIPS for chip in STILL_LAST], jnp.int32),
            ]
        )
        whole = [lax.all_gather(part, AXES, axis=0, tiled=True) for part in small_parts]
        lines = []
        for part in whole:
            share = part.shape[0] // 32
            chunks = part.reshape(32, share)
            lines.append(
                jnp.stack([placed(chunks[index], index, BLOCK // share) for index in range(32)])
            )
        lines = jnp.concatenate([jnp.stack(lines, axis=1), jnp.zeros((32, 8, BLOCK), BF)], axis=1)
        lines = lines.reshape(CHIPS, 2, 16, BLOCK).transpose(1, 0, 2, 3).reshape(32, 16, BLOCK)
        whole_qkv = lax.all_gather(qkv_weight, AXES, axis=0, tiled=True)
        whole_out = lax.all_gather(out_weight, AXES, axis=0, tiled=True)
        whole_fc1 = lax.all_gather(fc1_weight, AXES, axis=0, tiled=True)
        whole_fc2 = lax.all_gather(fc2_weight, AXES, axis=0, tiled=True)
        split = whole_fc2.reshape(CHIPS, 2, 96, 2, BLOCK).transpose(1, 0, 3, 2, 4).reshape(32, 192, BLOCK)
        gathered_a = eights(
            jnp.concatenate([full_pieces(whole_qkv.reshape(width, 3, 2, BLOCK), 3), lines], axis=1), STILL
        )
        gathered_b1 = eights(full_pieces(whole_fc1.reshape(width, 2, 4, BLOCK), 4))
        split = whole_fc2.reshape(CHIPS, 2, 96, 2, BLOCK).transpose(1, 0, 3, 2, 4).reshape(32, 192, BLOCK)
        gathered_b2 = eights(
            jnp.concatenate([split, full_pieces(whole_out.reshape(width, 1, 2, BLOCK), 1)], axis=1), STILL_LAST
        )

    if by_hand:
        gathered_a, on_b1, on_b2, early = links.gather(*pieces, (patches, counts, positions, cotangent), prepare)
    else:
        early = prepare(patches, counts, positions, cotangent)
    rows_in, gout, far, far_turned = early

    def call(kernel, operands, out_shape, out_specs, in_specs, flops, mib, vmem_mib, grid, scratch=(), name=None):
        return pl.pallas_call(
            kernel,
            grid=grid,
            out_shape=out_shape,
            in_specs=in_specs,
            out_specs=out_specs,
            scratch_shapes=list(scratch),
            compiler_params=pltpu.CompilerParams(vmem_limit_bytes=vmem_mib * MIB),
            cost_estimate=pl.CostEstimate(
                flops=1, bytes_accessed=1, transcendentals=0
            ),
            name=name,
        )(*operands)

    image_rows = lambda columns: pl.BlockSpec((padded, columns), lambda image: (image, 0))
    image_far = pl.BlockSpec((1, padded, padded), lambda image: (image, 0, 0))
    fixed = lambda *shape: pl.BlockSpec(shape, lambda step: (0,) * len(shape))
    step_rows = lambda columns: pl.BlockSpec((rows, columns), lambda step: (0, step))
    shares = lambda height, columns: struct((CHIPS, height, columns), BF)
    buffer, flag = pltpu.VMEM, pltpu.SemaphoreType.DMA
    low_rows, wide_rows = struct((rows, width), BF), struct((rows, width), F32)
    wide = 2 * BLOCK
    steps = hidden_width // wide
    third = 3 * BLOCK

    def join(value, *others):
        return after(value, *others) if by_hand else value

    vec, fcb, h1_turned, qkv, att, wq_0, wq_1 = pl.pallas_call(
        first_kernel,
        out_shape=(
            struct((2, 16, BLOCK), F32), struct((steps, 1, wide), F32), struct((width, rows), BF),
            struct((2, rows, third), BF), low_rows, struct((width, third), BF), struct((width, third), BF),
        ),
        in_specs=[smem] + [anywhere] * 4 + [vmem] * 2,
        out_specs=(vmem,) * 5 + (anywhere,) * 2,
        scratch_shapes=[
            buffer((2, width, third), BF), buffer((rows, width), BF), buffer((4, 16, BLOCK), F32),
            buffer((32, 16, BLOCK), BF), flag((5,)),
        ],
        compiler_params=pltpu.CompilerParams(vmem_limit_bytes=30 * MIB),
        cost_estimate=pl.CostEstimate(flops=1, bytes_accessed=1, transcendentals=0),
        name="first",
    )(place, *gathered_a, rows_in, far)
    if by_hand:
        att, gathered_b1, gathered_b2 = links.gather_end(on_b1, on_b2, att)

    step_shares = lambda height, columns: pl.BlockSpec((CHIPS, height, columns), lambda step: (0, 0, step))
    still = lambda *shape: pl.BlockSpec(shape, lambda step, place: (0,) * len(shape))
    turned_shares = pl.BlockSpec(
        (CHIPS, 24, wide), lambda step, place: (0, 0, lax.rem(place[50] + 4 - step, 4))
    )
    low_buffer, wide_buffer = buffer((rows, width), BF), buffer((rows, width), F32)
    out, glow, keep_1, send_1, sums, fcg, keep_2, upper_2, lower_2, wo = pl.pallas_call(
        mlp_kernel,
        grid_spec=pltpu.PrefetchScalarGridSpec(
            num_scalar_prefetch=1,
            grid=(steps,),
            in_specs=[smem] + [anywhere] * 11 + [still(2, 16, BLOCK), still(steps, 1, wide)],
            out_specs=(still(rows, width),) * 2
            + (turned_shares,) * 2
            + (still(8, wide), still(steps, 8, wide))
            + (anywhere,) * 4,
            scratch_shapes=[
                buffer((steps, width, wide), BF), buffer((hidden_width, width), BF), buffer((2, width, BLOCK), BF),
                low_buffer, low_buffer, low_buffer, low_buffer, buffer((width, rows), BF),
                wide_buffer, wide_buffer, wide_buffer, buffer((width, wide), F32), buffer((width, wide), F32),
                buffer((2, CHIPS, 96, wide), BF), buffer((rows, 128), F32), flag((steps,)), flag((steps,)), flag((7,)),
            ],
        ),
        out_shape=(low_rows, low_rows)
        + (shares(24, hidden_width),) * 2
        + (struct((8, wide), F32), struct((steps, 8, wide), F32))
        + (shares(96, wide),)
        + (struct((8, 96, wide), BF),) * 2
        + (struct((2, width, BLOCK), BF),),
        compiler_params=pltpu.CompilerParams(vmem_limit_bytes=60 * MIB),
        cost_estimate=pl.CostEstimate(flops=1, bytes_accessed=1, transcendentals=0),
        name="mlp",
    )(place, counts, *gathered_b1, *gathered_b2, att, rows_in, gout, vec, fcb)

    if by_hand:
        state_2 = keep_2, links.move(upper_2, links.cores)

    def attention_back(side, gradient):
        return call(
            lambda *refs: attention_back_kernel(side, *refs),
            (wo, qkv, far_turned, gradient),
            struct((rows, third), BF),
            image_rows(third),
            [
                fixed(2, width, BLOCK), pl.BlockSpec((1, padded, third), lambda image: (side, image, 0)),
                image_far, image_rows(width),
            ],
            8 * rows * 256 * width,
            8,
            20,
            grid=(images,),
            name="attention_back",
        )

    part_2 = glow
    if by_hand:
        part_2 = add_up([keep_2[8:], state_2[1]]).astype(BF)
        lower_2, send_1 = after((lower_2, send_1), part_2)
        state_2 = keep_2, links.move(lower_2, links.cores), links.move(part_2, links.second)
        state_1 = keep_1, links.move(send_1, links.cores)
    gqkv_0 = attention_back(0, join(glow, part_2))
    if by_hand:
        state_1, gqkv_0 = lax.optimization_barrier((state_1, gqkv_0))
        state_1 += (links.move(links.fold(state_1), links.second),)

    def grad_call(kernel, operands, out_shape, scratch, name):
        return pl.pallas_call(
            kernel,
            out_shape=out_shape,
            in_specs=[smem] + [vmem] * (len(operands) - 1),
            out_specs=(vmem,) * len(out_shape),
            scratch_shapes=list(scratch),
            compiler_params=pltpu.CompilerParams(vmem_limit_bytes=28 * MIB),
            cost_estimate=pl.CostEstimate(flops=1, bytes_accessed=1, transcendentals=0),
            name=name,
        )(*operands)

    half_shares = lambda height, columns: (struct((8, height, columns), BF),) * 2
    gh1, sums_0, keep_a, upper_a, lower_a = grad_call(
        qkv_grad_kernel,
        (place, h1_turned, gqkv_0, wq_0, att, glow),
        (wide_rows, struct((1, third), F32), shares(24, third + wide)) + half_shares(24, third + wide),
        (buffer((width, third), F32), buffer((width, wide), F32)),
        "qkv_grad",
    )
    parts = gh1
    if by_hand:
        got_a = links.move(upper_a, links.cores)
        state_2, got_a, gh1 = lax.optimization_barrier((state_2, got_a, gh1))
        parts = links.fold(state_2), add_up([keep_a[8:], got_a]).astype(BF)
        state_2 += (links.move(parts[0], links.near),)
        lower_a = after(lower_a, parts)
        state_a = keep_a, links.move(lower_a, links.cores), links.move(parts[1], links.second)

    gqkv_1 = attention_back(1, join(glow, gh1, parts))
    ginput, keep_c, upper_c, lower_c = grad_call(
        input_kernel,
        (place, h1_turned, gqkv_1, wq_1, sums_0, sums, fcg, rows_in, vec, glow, gh1),
        (low_rows, shares(32, third)) + half_shares(32, third),
        (buffer((width, third), F32),),
        "input_grad",
    )

    def cut(value):
        return value.reshape(images, padded, width)[:, :length]

    if by_hand:
        fold, move = links.fold, links.move

        state_c = keep_c, move(upper_c, links.cores)
        rest_c = move(after(lower_c, keep_c), links.cores)
        state_1 = after(state_1, keep_c)
        part = fold(state_1)
        state_1 += (move(part, links.near),)
        keep_c, got_c = after(state_c, part)
        part = add_up([keep_c[8:], got_c]).astype(BF)
        state_c = keep_c, rest_c, move(part, links.second)
        state_2, state_a, out, ginput = after((state_2, state_a, out, ginput), part)
        out, ginput = cut(out), cut(ginput)
        state_2, state_a, out, ginput = after((state_2, state_a, out, ginput))
        parts = fold(state_2), fold(state_a)
        state_2 += (move(parts[0], links.first),)
        state_a += (move(parts[1], links.first),)
        part = fold(after(state_c, parts))
        state_c += (move(part, links.first),)
        state_1, out, ginput = after((state_1, out, ginput), part)
        part = fold(state_1)
        state_1 += (move(part, links.first),)
        state_2 = after(state_2, part)
        part = fold(state_2)
        state_2 += (move(part, links.far),)
        state_a = after(state_a, part)
        part = fold(state_a)
        state_a += (move(part, links.near),)
        part = fold(after(state_c, part))
        state_c += (move(part, links.near),)
        state_1 = after(state_1, part)
        part = fold(state_1)
        state_1 += (move(part, links.far),)
        state_a = after(state_a, part)
        part = fold(state_a)
        state_a += (move(part, links.far),)
        part = fold(after(state_c, part))
        state_c += (move(part, links.far),)
        state_2 = after(state_2, part)
        mine_2 = add_up([part[0] for part in state_2])
        state_1 = after(state_1, mine_2)
        mine_1 = add_up([part[0] for part in state_1])
        own_slot = lambda part: pl.BlockSpec((1,) + part.shape[1:], lambda step: (0, 0, 0))
        heights, counts_out = ((24, 3 * width), (24, width)), (24, 24, 48, 24, 24, 24, 96, 24)
        (
            qkv_grad, out_grad, ln1_gain_grad, ln1_bias_grad, qv_bias_grad,
            ln2_gain_grad, ln2_bias_grad, fc2_bias_grad, fc1_bias_grad, out_bias_grad,
        ) = pl.pallas_call(
            last_kernel,
            grid=(1,),
            out_shape=tuple(struct(shape, F32) for shape in heights + tuple((count,) for count in counts_out)),
            in_specs=[smem] + [own_slot(part) for part in state_a + state_c],
            out_specs=tuple(fixed(*shape) for shape in heights)
            + tuple(pl.BlockSpec((count,), lambda step: (0,)) for count in counts_out),
            compiler_params=pltpu.CompilerParams(vmem_limit_bytes=30 * MIB),
            name="last",
        )(place, *state_a, *state_c)
        return (
            out, ginput, ln1_gain_grad, ln1_bias_grad, qkv_grad, qv_bias_grad, out_grad, out_bias_grad,
            ln2_gain_grad, ln2_bias_grad, mine_1, fc1_bias_grad, mine_2, fc2_bias_grad,
        )

    both_a, both_c, both_1, both_2 = (
        jnp.stack(pair, axis=1).astype(F32)
        for pair in (
            (keep_a, jnp.concatenate([lower_a, upper_a])),
            (keep_c, jnp.concatenate([lower_c, upper_c])),
            (keep_1, send_1),
            (keep_2, jnp.concatenate([lower_2, upper_2])),
        )
    )
    heads = jnp.stack(
        [both.reshape(CHIPS, 2, 24, 3, BLOCK) for both in (both_a[..., :third], both_c[:, :, :24])], axis=4
    )

    def vector(lines, count):
        columns = lines.shape[-1]
        return lines.reshape(32 * count // columns, -1, columns)[:, 0].reshape(-1)

    small_c, small_2 = both_c[:, :, 24:, 2 * BLOCK :], both_c[:, :, 24:, : 2 * BLOCK]
    totals = (
        vector(small_c[:, :, 0], 24),
        vector(small_c[:, :, 1], 24),
        heads.reshape(width, 3 * width),
        vector(small_c[:, :, 2], 48),
        both_a[..., third:].reshape(width, width),
        vector(small_2[:, :, 4], 24),
        vector(small_2[:, :, 0], 24),
        vector(small_2[:, :, 1], 24),
        both_1.reshape(width, hidden_width),
        vector(small_2[:, :, 3], 96),
        both_2.reshape(hidden_width, width),
        vector(small_2[:, :, 2], 24),
    )
    return (cut(out), cut(ginput)) + tuple(
        lax.psum_scatter(total, AXES, scatter_dimension=0, tiled=True) for total in totals
    )


def solution(mesh):
    rows = P(AXES, None, None)
    table = P(AXES, None)
    line = P(AXES)
    in_specs = (
        rows, line, table, line, line, table, line, table, line, line, line, table, line, table, line, rows,
    )
    out_specs = (
        rows, rows, line, line, table, line, table, line, line, line, table, line, table, line,
    )
    mesh_shape = dict(mesh.shape)

    def body(*arrays):
        return shards(mesh_shape, *arrays)

    return jax.shard_map(body, mesh=mesh, in_specs=in_specs, out_specs=out_specs, check_vma=False)
```

profile of v0, /device:TPU:0, one launch (start us, length us, event | category | flops | bytes accessed | tf_op | source)
XLA Modules:
  0.0 219.5 jit_solution(1584410123503918301)
XLA Ops:
  1.5 1.8 share.1
  3.7 1.2 collective-permute-done.got_ref
  5.6 1.9 pair.1
  7.5 2.9 %collective-permute-start.3 = (bf16[192,384]{1,0:T(8,128)(2,1)}, bf16[192,384]{1,0:T(8,128)(2,1)S(1)}, u32[]{:S(2)}, u32[]{:S(2)}) collective-permute-start(bf16[192,384]{1,0:T(8,128)(2,1)} %get-tuple-element.174), channel_id=1, source_target_pairs={{0,4},{1,3},{2,6},{3,1},{4,0},{5,7},{6,2},{7,5},{8,12},{9,11},{10,... | collective-permute-start | bytes 442376 | tf_op jit(solution)/shard_map/ppermute | solution.py:528
  10.3 3.6 %collective-permute-start.2 = (bf16[160,384]{1,0:T(8,128)(2,1)}, bf16[160,384]{1,0:T(8,128)(2,1)S(1)}, u32[]{:S(2)}, u32[]{:S(2)}) collective-permute-start(bf16[160,384]{1,0:T(8,128)(2,1)} %get-tuple-element.175), channel_id=1, source_target_pairs={{0,24},{1,25},{2,26},{3,27},{4,28},{5,29},{6,30},{7,31},{8,0},{9,1... | collective-permute-start | bytes 368648 | tf_op jit(solution)/shard_map/ppermute | solution.py:528
  13.9 4.0 %collective-permute-done.2 = bf16[160,384]{1,0:T(8,128)(2,1)S(1)} collective-permute-done((bf16[160,384]{1,0:T(8,128)(2,1)}, bf16[160,384]{1,0:T(8,128)(2,1)S(1)}, u32[]{:S(2)}, u32[]{:S(2)}) %collective-permute-start.2) | collective-permute-done | bytes 122912 | tf_op jit(solution)/shard_map/ppermute | solution.py:528
  18.0 2.8 %collective-permute-done.1 = bf16[160,384]{1,0:T(8,128)(2,1)S(1)} collective-permute-done((bf16[160,384]{1,0:T(8,128)(2,1)}, bf16[160,384]{1,0:T(8,128)(2,1)S(1)}, u32[]{:S(2)}, u32[]{:S(2)}) %collective-permute-start.1) | collective-permute-done | bytes 122912 | tf_op jit(solution)/shard_map/ppermute | solution.py:528
  20.8 1.0 pad_maximum_fusion.4
  21.8 1.6 collective-permute-start.5
  24.5 6.6 %collective-permute-done.4 = bf16[160,384]{1,0:T(8,128)(2,1)S(1)} collective-permute-done((bf16[160,384]{1,0:T(8,128)(2,1)S(1)}, bf16[160,384]{1,0:T(8,128)(2,1)S(1)}, u32[]{:S(2)}, u32[]{:S(2)}) %collective-permute-start.4) | collective-permute-done | bytes 122912 | tf_op jit(solution)/shard_map/ppermute | solution.py:528
  31.1 2.0 collective-permute-start.7
  33.1 1.0 pad_maximum_fusion.3
  36.4 4.4 %collective-permute-done.8 = bf16[240,384]{1,0:T(8,128)(2,1)S(1)} collective-permute-done((bf16[240,384]{1,0:T(8,128)(2,1)}, bf16[240,384]{1,0:T(8,128)(2,1)S(1)}, u32[]{:S(2)}, u32[]{:S(2)}) %collective-permute-start.8) | collective-permute-done | bytes 184352 | tf_op jit(solution)/shard_map/ppermute | solution.py:528
  40.8 2.3 %collective-permute-done.6 = bf16[4,160,384]{2,1,0:T(8,128)(2,1)} collective-permute-done((bf16[4,160,384]{2,1,0:T(8,128)(2,1)S(1)}, bf16[4,160,384]{2,1,0:T(8,128)(2,1)}, u32[]{:S(2)}, u32[]{:S(2)}) %collective-permute-start.6) | collective-permute-done | bytes 491552 | tf_op jit(solution)/shard_map/ppermute | solution.py:528
  43.4 1.2 constant_dynamic-update-slice_fusion.own0
  44.6 1.6 collective-permute-start.9
  46.2 1.0 pad_maximum_fusion.2
  47.2 2.7 %collective-permute-start.12 = (bf16[3,240,384]{2,1,0:T(8,128)(2,1)S(1)}, bf16[3,240,384]{2,1,0:T(8,128)(2,1)S(1)}, u32[]{:S(2)}, u32[]{:S(2)}) collective-permute-start(bf16[3,240,384]{2,1,0:T(8,128)(2,1)S(1)} %pad_maximum_fusion.2), channel_id=1, source_target_pairs={{0,4},{1,3},{2,6},{3,1},{4,0},{5,7},{6,2},{7,5},{8,12},{9,11},{10,... | collective-permute-start | bytes 1658888 | tf_op jit(solution)/shard_map/ppermute | solution.py:528
  49.8 1.9 pad_select_fusion
  51.7 1.1 copy.32
  54.1 1.2 fusion
  55.3 1.0 constant_dynamic-update-slice_fusion.16
  56.3 4.9 %collective-permute-done.12 = bf16[3,240,384]{2,1,0:T(8,128)(2,1)S(1)} collective-permute-done((bf16[3,240,384]{2,1,0:T(8,128)(2,1)S(1)}, bf16[3,240,384]{2,1,0:T(8,128)(2,1)S(1)}, u32[]{:S(2)}, u32[]{:S(2)}) %collective-permute-start.12) | collective-permute-done | bytes 552992 | tf_op jit(solution)/shard_map/ppermute | solution.py:528
  61.2 1.3 collective-permute-done.11
  62.9 1.7 collective-permute-start.15
  65.1 1.5 collective-permute-start.14
  67.2 1.5 collective-permute-start.17
  68.7 1.2 collective-permute-start.16
  69.9 1.2 copy-done.14
  71.1 13.4 %first.1 = (f32[2,16,384]{2,1,0:T(8,128)S(1)}, f32[4,1,768]{2,1,0:T(1,128)S(1)}, bf16[768,640]{1,0:T(8,128)(2,1)S(1)}, bf16[2,640,1152]{2,1,0:T(8,128)(2,1)S(1)}...) custom-call(s32[176]{0:T(256)S(1)} %copy-done.18, ...), custom_call_target="tpu_custom_call" | custom-call | flops 1 | bytes 1 | tf_op jit(solution)/shard_map/first/pallas_call | solution.py:776
  84.5 1.2 copy-done.9
  85.7 1.2 copy-done.11
  87.1 5.9 %collective-permute-done.14 = bf16[4,192,384]{2,1,0:T(8,128)(2,1)S(1)} collective-permute-done((bf16[4,192,384]{2,1,0:T(8,128)(2,1)S(1)}, bf16[4,192,384]{2,1,0:T(8,128)(2,1)S(1)}, u32[]{:S(2)}, u32[]{:S(2)}) %collective-permute-start.14) | collective-permute-done | bytes 589856 | tf_op jit(solution)/shard_map/ppermute | solution.py:528
  94.5 3.7 %collective-permute-done.20.a2 = bf16[8,192,384]{2,1,0:T(8,128)(2,1)S(1)} collective-permute-done((bf16[8,192,384]{2,1,0:T(8,128)(2,1)S(1)}, bf16[8,192,384]{2,1,0:T(8,128)(2,1)S(1)}, u32[]{:S(2)}, u32[]{:S(2)}) %collective-permute-start.20) | collective-permute-done | bytes 1179680 | tf_op jit(solution)/shard_map/ppermute | solution.py:528
  98.3 1.7 collective-permute-done.21.a3
  101.5 35.0 %mlp.1 = (bf16[640,768]{1,0:T(8,128)(2,1)}, bf16[640,768]{1,0:T(8,128)(2,1)}, bf16[16,24,3072]{2,1,0:T(8,128)(2,1)}, bf16[16,24,3072]{2,1,0:T(8,128)(2,1)}, f32[...) custom-call(s32[176]{0:T(256)} %concatenate.28.place, ...), custom_call_target="tpu_custom_call" | custom-call | flops 1 | bytes 1 | tf_op jit(solution)/shard_map/mlp/pallas_call | solution.py:801
  136.7 2.9 %collective-permute-done.24 = bf16[8,96,768]{2,1,0:T(8,128)(2,1)S(1)} collective-permute-done((bf16[8,96,768]{2,1,0:T(8,128)(2,1)}, bf16[8,96,768]{2,1,0:T(8,128)(2,1)S(1)}, u32[]{:S(2)}, u32[]{:S(2)}) %collective-permute-start.24) | collective-permute-done | bytes 1179680 | tf_op jit(solution)/shard_map/ppermute | solution.py:528
  139.6 1.7 add_convert_fusion.1
  141.9 1.6 collective-permute-start.28
  143.5 6.5 %attention_back.2.gqkv_ref = bf16[640,1152]{1,0:T(8,128)(2,1)S(1)} custom-call(bf16[2,768,384]{2,1,0:T(8,128)(2,1)S(1)} %copy-done.4, bf16[2,640,1152]{2,1,0:T(8,128)(2,1)S(1)} %get-tuple-element.215.refs_1_, f32[4,160,160]{2,1,0:T(8,128)S(1)} %copy-done.3, bf16[640,768]{1,0:T(8,128)(2,1)S(1)} %copy-done), custom_call_target="tpu_custom_call" | custom-call | flops 1 | bytes 1 | tf_op jit(solution)/shard_map/attention_back/pallas_call | solution.py:748
  150.1 5.5 %qkv_grad.1 = (f32[640,768]{1,0:T(8,128)S(1)}, f32[1,1152]{1,0:T(1,128)S(1)}, bf16[16,24,1920]{2,1,0:T(8,128)(2,1)S(1)}, bf16[8,24,1920]{2,1,0:T(8,128)(2,1)S(1)}, bf16[8,24,1920]{2,1,0:T(8,128)(2,1)S(1)}) custom-call(s32[176]{0:T(256)S(1)} %copy-done.19, bf16[768,640]{1,0:T(8,128)(2,1)S(1)} %copy-done.6, bf16[640,1152]{1,0:T(8,128)(2,1)S(1)} %attention_back.2.gqkv_ref, ...), custom_call_target="tpu_custom_call" | custom-call | flops 1 | bytes 1 | tf_op jit(solution)/shard_map/qkv_grad/pallas_call | solution.py:861
  156.1 1.3 collective-permute-start.26
  158.3 1.6 collective-permute-start.31
  160.2 1.8 collective-permute-start.33
  162.0 6.5 %attention_back.3.gqkv_ref = bf16[640,1152]{1,0:T(8,128)(2,1)S(1)} custom-call(bf16[2,768,384]{2,1,0:T(8,128)(2,1)S(1)} %copy-done.4, bf16[2,640,1152]{2,1,0:T(8,128)(2,1)S(1)} %get-tuple-element.215.refs_1_, f32[4,160,160]{2,1,0:T(8,128)S(1)} %copy-done.3, bf16[640,768]{1,0:T(8,128)(2,1)S(1)} %copy-done), custom_call_target="tpu_custom_call" | custom-call | flops 1 | bytes 1 | tf_op jit(solution)/shard_map/attention_back/pallas_call | solution.py:748
  168.6 5.3 %input_grad.1 = (bf16[640,768]{1,0:T(8,128)(2,1)S(1)}, bf16[16,32,1152]{2,1,0:T(8,128)(2,1)S(1)}, bf16[8,32,1152]{2,1,0:T(8,128)(2,1)S(1)}, bf16[8,32,1152]{2,1,0:T(8,128)(2,1)S(1)}) custom-call(s32[176]{0:T(256)S(1)} %copy-done.19, bf16[768,640]{1,0:T(8,128)(2,1)S(1)} %copy-done.6, bf16[640,1152]{1,0:T(8,128)(2,1)S(1)} %attention_back.3.gqkv_ref, ...), custom_call_target="tpu_custom_call" | custom-call | flops 1 | bytes 1 | tf_op jit(solution)/shard_map/input_grad/pallas_call | solution.py:861
  174.8 2.0 collective-permute-done.34
  177.9 2.4 %collective-permute-done.33.refs_2_ = bf16[8,24,1920]{2,1,0:T(8,128)(2,1)S(1)} collective-permute-done((bf16[8,24,1920]{2,1,0:T(8,128)(2,1)S(1)}, bf16[8,24,1920]{2,1,0:T(8,128)(2,1)S(1)}, u32[]{:S(2)}, u32[]{:S(2)}) %collective-permute-start.33) | collective-permute-done | bytes 737312 | tf_op jit(solution)/shard_map/ppermute | solution.py:528
  180.3 1.7 copy.35
  182.0 1.7 copy.36
  183.8 1.5 collective-permute-start.38
  186.1 2.2 collective-permute-done.36.refs_8_
  188.4 1.5 collective-permute-start.41
  189.9 2.3 %collective-permute-done.30 = bf16[4,24,3072]{2,1,0:T(8,128)(2,1)S(1)} collective-permute-done((bf16[4,24,3072]{2,1,0:T(8,128)(2,1)S(1)}, bf16[4,24,3072]{2,1,0:T(8,128)(2,1)S(1)}, u32[]{:S(2)}, u32[]{:S(2)}) %collective-permute-start.30) | collective-permute-done | bytes 589856 | tf_op jit(solution)/shard_map/ppermute | solution.py:528
  192.4 1.6 collective-permute-start.40
  194.8 1.7 collective-permute-start.39
  196.5 1.2 collective-permute-done.41.refs_9_
  197.8 1.8 collective-permute-start.43
  199.6 1.3 collective-permute-done.40
  200.9 1.4 collective-permute-start.45
  202.3 1.8 collective-permute-done.39.refs_4_
  205.2 3.7 %collective-permute-done.43.refs_10_ = bf16[2,32,1152]{2,1,0:T(8,128)(2,1)S(1)} collective-permute-done((bf16[2,32,1152]{2,1,0:T(8,128)(2,1)S(1)}, bf16[2,32,1152]{2,1,0:T(8,128)(2,1)S(1)}, u32[]{:S(2)}, u32[]{:S(2)}) %collective-permute-start.43) | collective-permute-done | bytes 147488 | tf_op jit(solution)/shard_map/ppermute | solution.py:528
  210.2 5.1 %collective-permute-done.45 = bf16[1,24,3072]{2,1,0:T(8,128)(2,1)S(1)} collective-permute-done((bf16[1,24,3072]{2,1,0:T(8,128)(2,1)S(1)}, bf16[1,24,3072]{2,1,0:T(8,128)(2,1)S(1)}, u32[]{:S(2)}, u32[]{:S(2)}) %collective-permute-start.45) | collective-permute-done | bytes 147488 | tf_op jit(solution)/shard_map/ppermute | solution.py:528
  217.9 1.4 last.1
  (187 shorter events, 22.6 us)
Async XLA Ops:
  3.3 1.7 collective-permute-start
  7.5 27.3 %copy-start.32 = (bf16[192,384]{1,0:T(8,128)(2,1)S(1)}, bf16[192,384]{1,0:T(8,128)(2,1)}, u32[]{:S(2)}) copy-start(bf16[192,384]{1,0:T(8,128)(2,1)} %get-tuple-element.174) | copy-start | bytes 442372
  7.5 13.3 %collective-permute-start.3 = (bf16[192,384]{1,0:T(8,128)(2,1)}, bf16[192,384]{1,0:T(8,128)(2,1)S(1)}, u32[]{:S(2)}, u32[]{:S(2)}) collective-permute-start(bf16[192,384]{1,0:T(8,128)(2,1)} %get-tuple-element.174), channel_id=1, source_target_pairs={{0,4},{1,3},{2,6},{3,1},{4,0},{5,7},{6,2},{7,5},{8,12},{9,11},{10,... | collective-permute-start | bytes 442376 | tf_op jit(solution)/shard_map/ppermute | solution.py:528
  10.3 7.6 %collective-permute-start.2 = (bf16[160,384]{1,0:T(8,128)(2,1)}, bf16[160,384]{1,0:T(8,128)(2,1)S(1)}, u32[]{:S(2)}, u32[]{:S(2)}) collective-permute-start(bf16[160,384]{1,0:T(8,128)(2,1)} %get-tuple-element.175), channel_id=1, source_target_pairs={{0,24},{1,25},{2,26},{3,27},{4,28},{5,29},{6,30},{7,31},{8,0},{9,1... | collective-permute-start | bytes 368648 | tf_op jit(solution)/shard_map/ppermute | solution.py:528
  13.9 6.9 %collective-permute-start.1 = (bf16[160,384]{1,0:T(8,128)(2,1)}, bf16[160,384]{1,0:T(8,128)(2,1)S(1)}, u32[]{:S(2)}, u32[]{:S(2)}) collective-permute-start(bf16[160,384]{1,0:T(8,128)(2,1)} %get-tuple-element.175), channel_id=1, source_target_pairs={{0,8},{1,9},{2,10},{3,11},{4,12},{5,13},{6,14},{7,15},{8,16},{9,17... | collective-permute-start | bytes 368648 | tf_op jit(solution)/shard_map/ppermute | solution.py:528
  20.8 13.9 %copy-start.33 = (bf16[192,384]{1,0:T(8,128)(2,1)}, bf16[192,384]{1,0:T(8,128)(2,1)S(1)}, u32[]{:S(2)}) copy-start(bf16[192,384]{1,0:T(8,128)(2,1)S(1)} %collective-permute-done.3) | copy-start | bytes 442372
  21.8 9.2 %collective-permute-start.5 = (bf16[2,192,384]{2,1,0:T(8,128)(2,1)S(1)}, bf16[2,192,384]{2,1,0:T(8,128)(2,1)S(1)}, u32[]{:S(2)}, u32[]{:S(2)}) collective-permute-start(bf16[2,192,384]{2,1,0:T(8,128)(2,1)S(1)} %pad_maximum_fusion.4), channel_id=1, source_target_pairs={{0,2},{1,5},{2,0},{3,7},{4,6},{5,1},{6,4},{7,3},{8,10},{9,13},{10,... | collective-permute-start | bytes 884744 | tf_op jit(solution)/shard_map/ppermute | solution.py:528
  24.3 11.3 %copy-start.41 = (bf16[240,384]{1,0:T(8,128)(2,1)S(1)}, bf16[240,384]{1,0:T(8,128)(2,1)}, u32[]{:S(2)}) copy-start(bf16[240,384]{1,0:T(8,128)(2,1)} %get-tuple-element.182) | copy-start | bytes 552964
  24.3 6.7 %collective-permute-start.4 = (bf16[160,384]{1,0:T(8,128)(2,1)S(1)}, bf16[160,384]{1,0:T(8,128)(2,1)S(1)}, u32[]{:S(2)}, u32[]{:S(2)}) collective-permute-start(bf16[160,384]{1,0:T(8,128)(2,1)S(1)} %collective-permute-done.1), channel_id=1, source_target_pairs={{0,8},{1,9},{2,10},{3,11},{4,12},{5,13},{6,14},{7,15},{8,16},{9,17... | collective-permute-start | bytes 368648 | tf_op jit(solution)/shard_map/ppermute | solution.py:528
  31.1 9.7 %collective-permute-start.8 = (bf16[240,384]{1,0:T(8,128)(2,1)}, bf16[240,384]{1,0:T(8,128)(2,1)S(1)}, u32[]{:S(2)}, u32[]{:S(2)}) collective-permute-start(bf16[240,384]{1,0:T(8,128)(2,1)} %get-tuple-element.182), channel_id=1, source_target_pairs={{0,24},{1,25},{2,26},{3,27},{4,28},{5,29},{6,30},{7,31},{8,0},{9,1... | collective-permute-start | bytes 552968 | tf_op jit(solution)/shard_map/ppermute | solution.py:528
  31.1 9.7 %collective-permute-start.7 = (bf16[240,384]{1,0:T(8,128)(2,1)}, bf16[240,384]{1,0:T(8,128)(2,1)}, u32[]{:S(2)}, u32[]{:S(2)}) collective-permute-start(bf16[240,384]{1,0:T(8,128)(2,1)} %get-tuple-element.182), channel_id=1, source_target_pairs={{0,8},{1,9},{2,10},{3,11},{4,12},{5,13},{6,14},{7,15},{8,16},{9,17... | collective-permute-start | bytes 552968 | tf_op jit(solution)/shard_map/ppermute | solution.py:528
  34.1 9.0 %copy-start.46 = (s32[4]{0:T(128)S(1)}, s32[4]{0:T(128)}, u32[]{:S(2)}) copy-start(s32[4]{0:T(128)} %counts.1) | copy-start | bytes 52
  34.1 9.0 %collective-permute-start.6 = (bf16[4,160,384]{2,1,0:T(8,128)(2,1)S(1)}, bf16[4,160,384]{2,1,0:T(8,128)(2,1)}, u32[]{:S(2)}, u32[]{:S(2)}) collective-permute-start(bf16[4,160,384]{2,1,0:T(8,128)(2,1)S(1)} %pad_maximum_fusion.3), channel_id=1, source_target_pairs={{0,4},{1,3},{2,6},{3,1},{4,0},{5,7},{6,2},{7,5},{8,12},{9,11},{10,... | collective-permute-start | bytes 1474568 | tf_op jit(solution)/shard_map/ppermute | solution.py:528
  43.3 13.0 %collective-permute-start.10 = (bf16[240,384]{1,0:T(8,128)(2,1)}, bf16[240,384]{1,0:T(8,128)(2,1)S(1)}, u32[]{:S(2)}, u32[]{:S(2)}) collective-permute-start(bf16[240,384]{1,0:T(8,128)(2,1)} %collective-permute-done.7), channel_id=1, source_target_pairs={{0,8},{1,9},{2,10},{3,11},{4,12},{5,13},{6,14},{7,15},{8,16},{9,17... | collective-permute-start | bytes 552968 | tf_op jit(solution)/shard_map/ppermute | solution.py:528
  44.6 20.0 %copy-start.13 = (bf16[8,160,384]{2,1,0:T(8,128)(2,1)}, bf16[8,160,384]{2,1,0:T(8,128)(2,1)S(1)}, u32[]{:S(2)}) copy-start(bf16[8,160,384]{2,1,0:T(8,128)(2,1)S(1)} %constant_dynamic-update-slice_fusion.own0) | copy-start | bytes 2949124
  44.6 18.0 %collective-permute-start.9 = (bf16[8,160,384]{2,1,0:T(8,128)(2,1)S(1)}, bf16[8,160,384]{2,1,0:T(8,128)(2,1)S(1)}, u32[]{:S(2)}, u32[]{:S(2)}) collective-permute-start(bf16[8,160,384]{2,1,0:T(8,128)(2,1)S(1)} %constant_dynamic-update-slice_fusion.own0), channel_id=1, source_target_pairs={{0,2},{1,5},{2,0},{3,7},{4,6},{5,1},{6,4},{7,3},{8,10},{9,13},{10,... | collective-permute-start | bytes 2949128 | tf_op jit(solution)/shard_map/ppermute | solution.py:528
  47.2 14.0 %collective-permute-start.12 = (bf16[3,240,384]{2,1,0:T(8,128)(2,1)S(1)}, bf16[3,240,384]{2,1,0:T(8,128)(2,1)S(1)}, u32[]{:S(2)}, u32[]{:S(2)}) collective-permute-start(bf16[3,240,384]{2,1,0:T(8,128)(2,1)S(1)} %pad_maximum_fusion.2), channel_id=1, source_target_pairs={{0,4},{1,3},{2,6},{3,1},{4,0},{5,7},{6,2},{7,5},{8,12},{9,11},{10,... | collective-permute-start | bytes 1658888 | tf_op jit(solution)/shard_map/ppermute | solution.py:528
  49.8 12.7 %collective-permute-start.11 = (bf16[4,192,384]{2,1,0:T(8,128)(2,1)S(1)}, bf16[4,192,384]{2,1,0:T(8,128)(2,1)S(1)}, u32[]{:S(2)}, u32[]{:S(2)}) collective-permute-start(bf16[4,192,384]{2,1,0:T(8,128)(2,1)S(1)} %copy-done.42), channel_id=1, source_target_pairs={{0,8},{1,9},{2,10},{3,11},{4,12},{5,13},{6,14},{7,15},{8,16},{9,17... | collective-permute-start | bytes 1769480 | tf_op jit(solution)/shard_map/ppermute | solution.py:528
  54.1 15.8 %copy-start.1 = (bf16[4,160,768]{2,1,0:T(8,128)(2,1)}, bf16[4,160,768]{2,1,0:T(8,128)(2,1)S(1)}, u32[]{:S(2)}) copy-start(bf16[4,160,768]{2,1,0:T(8,128)(2,1)S(1)} %pad.11.clone) | copy-start | bytes 2949124
  62.5 7.3 %copy-start.18 = (s32[176]{0:T(256)S(1)}, s32[176]{0:T(256)}, u32[]{:S(2)}) copy-start(s32[176]{0:T(256)} %concatenate.28.place) | copy-start | bytes 2116
  62.9 30.1 %collective-permute-start.15 = (bf16[7,240,384]{2,1,0:T(8,128)(2,1)S(1)}, bf16[7,240,384]{2,1,0:T(8,128)(2,1)S(1)}, u32[]{:S(2)}, u32[]{:S(2)}) collective-permute-start(bf16[7,240,384]{2,1,0:T(8,128)(2,1)S(1)} %get-tuple-element.329), channel_id=1, source_target_pairs={{0,2},{1,5},{2,0},{3,7},{4,6},{5,1},{6,4},{7,3},{8,10},{9,13},{10,... | collective-permute-start | bytes 3870728 | tf_op jit(solution)/shard_map/ppermute | solution.py:528
  64.6 2.6 %collective-permute-start.18 = (bf16[8,160,384]{2,1,0:T(8,128)(2,1)S(1)}, bf16[8,160,384]{2,1,0:T(8,128)(2,1)S(1)}, u32[]{:S(2)}, u32[]{:S(2)}) collective-permute-start(bf16[8,160,384]{2,1,0:T(8,128)(2,1)S(1)} %constant_dynamic-update-slice_fusion.own0), channel_id=1, source_target_pairs={{0,1},{1,0},{2,3},{3,2},{4,5},{5,4},{6,7},{7,6},{8,9},{9,8},{10,11... | collective-permute-start | bytes 2949128 | tf_op jit(solution)/shard_map/ppermute | solution.py:528
  64.6 4.1 %collective-permute-start.19 = (bf16[8,160,384]{2,1,0:T(8,128)(2,1)S(1)}, bf16[8,160,384]{2,1,0:T(8,128)(2,1)S(1)}, u32[]{:S(2)}, u32[]{:S(2)}) collective-permute-start(bf16[8,160,384]{2,1,0:T(8,128)(2,1)S(1)} %collective-permute-done.9.own1), channel_id=1, source_target_pairs={{0,1},{1,0},{2,3},{3,2},{4,5},{5,4},{6,7},{7,6},{8,9},{9,8},{10,11... | collective-permute-start | bytes 2949128 | tf_op jit(solution)/shard_map/ppermute | solution.py:528
  65.1 27.9 %collective-permute-start.14 = (bf16[4,192,384]{2,1,0:T(8,128)(2,1)S(1)}, bf16[4,192,384]{2,1,0:T(8,128)(2,1)S(1)}, u32[]{:S(2)}, u32[]{:S(2)}) collective-permute-start(bf16[4,192,384]{2,1,0:T(8,128)(2,1)S(1)} %copy-done.42), channel_id=1, source_target_pairs={{0,24},{1,25},{2,26},{3,27},{4,28},{5,29},{6,30},{7,31},{8,0},{9,1... | collective-permute-start | bytes 1769480 | tf_op jit(solution)/shard_map/ppermute | solution.py:528
  66.6 26.4 %collective-permute-start.13 = (bf16[4,192,384]{2,1,0:T(8,128)(2,1)S(1)}, bf16[4,192,384]{2,1,0:T(8,128)(2,1)S(1)}, u32[]{:S(2)}, u32[]{:S(2)}) collective-permute-start(bf16[4,192,384]{2,1,0:T(8,128)(2,1)S(1)} %collective-permute-done.11), channel_id=1, source_target_pairs={{0,8},{1,9},{2,10},{3,11},{4,12},{5,13},{6,14},{7,15},{8,16},{9,17... | collective-permute-start | bytes 1769480 | tf_op jit(solution)/shard_map/ppermute | solution.py:528
  67.2 19.8 %collective-permute-start.17 = (bf16[1,240,384]{2,1,0:T(8,128)(2,1)S(1)}, bf16[1,240,384]{2,1,0:T(8,128)(2,1)S(1)}, u32[]{:S(2)}, u32[]{:S(2)}) collective-permute-start(bf16[1,240,384]{2,1,0:T(8,128)(2,1)S(1)} %bitcast.53), channel_id=1, source_target_pairs={{0,4},{1,3},{2,6},{3,1},{4,0},{5,7},{6,2},{7,5},{8,12},{9,11},{10,... | collective-permute-start | bytes 552968 | tf_op jit(solution)/shard_map/ppermute | solution.py:528
  68.7 24.3 %collective-permute-start.16 = (bf16[1,240,384]{2,1,0:T(8,128)(2,1)S(1)}, bf16[1,240,384]{2,1,0:T(8,128)(2,1)S(1)}, u32[]{:S(2)}, u32[]{:S(2)}) collective-permute-start(bf16[1,240,384]{2,1,0:T(8,128)(2,1)S(1)} %bitcast.54), channel_id=1, source_target_pairs={{0,6},{1,7},{2,4},{3,5},{4,2},{5,3},{6,0},{7,1},{8,14},{9,15},{10,... | collective-permute-start | bytes 552968 | tf_op jit(solution)/shard_map/ppermute | solution.py:528
  71.1 15.9 %copy-start.28 = (bf16[8,240,384]{2,1,0:T(8,128)(2,1)S(1)}, bf16[8,240,384]{2,1,0:T(8,128)(2,1)}, u32[]{:S(2)}) copy-start(bf16[8,240,384]{2,1,0:T(8,128)(2,1)} %copy-done.27) | copy-start | bytes 4423684
  87.0 13.0 %copy-start.29 = (bf16[8,240,384]{2,1,0:T(8,128)(2,1)}, bf16[8,240,384]{2,1,0:T(8,128)(2,1)S(1)}, u32[]{:S(2)}) copy-start(bf16[8,240,384]{2,1,0:T(8,128)(2,1)S(1)} %constant_dynamic-update-slice_fusion.12.b0) | copy-start | bytes 4423684
  87.0 11.2 %collective-permute-start.22 = (bf16[8,240,384]{2,1,0:T(8,128)(2,1)S(1)}, bf16[8,240,384]{2,1,0:T(8,128)(2,1)S(1)}, u32[]{:S(2)}, u32[]{:S(2)}) collective-permute-start(bf16[8,240,384]{2,1,0:T(8,128)(2,1)S(1)} %constant_dynamic-update-slice_fusion.12.b0), channel_id=1, source_target_pairs={{0,1},{1,0},{2,3},{3,2},{4,5},{5,4},{6,7},{7,6},{8,9},{9,8},{10,11... | collective-permute-start | bytes 4423688 | tf_op jit(solution)/shard_map/ppermute | solution.py:528
  93.2 6.7 %collective-permute-start.23 = (bf16[8,240,384]{2,1,0:T(8,128)(2,1)S(1)}, bf16[8,240,384]{2,1,0:T(8,128)(2,1)S(1)}, u32[]{:S(2)}, u32[]{:S(2)}) collective-permute-start(bf16[8,240,384]{2,1,0:T(8,128)(2,1)S(1)} %constant_dynamic-update-slice_fusion.18.b1), channel_id=1, source_target_pairs={{0,1},{1,0},{2,3},{3,2},{4,5},{5,4},{6,7},{7,6},{8,9},{9,8},{10,11... | collective-permute-start | bytes 4423688 | tf_op jit(solution)/shard_map/ppermute | solution.py:528
  93.5 4.8 %collective-permute-start.20 = (bf16[8,192,384]{2,1,0:T(8,128)(2,1)S(1)}, bf16[8,192,384]{2,1,0:T(8,128)(2,1)S(1)}, u32[]{:S(2)}, u32[]{:S(2)}) collective-permute-start(bf16[8,192,384]{2,1,0:T(8,128)(2,1)S(1)} %pad_maximum_fusion.a0), channel_id=1, source_target_pairs={{0,1},{1,0},{2,3},{3,2},{4,5},{5,4},{6,7},{7,6},{8,9},{9,8},{10,11... | collective-permute-start | bytes 3538952 | tf_op jit(solution)/shard_map/ppermute | solution.py:528
  94.5 5.5 %collective-permute-start.21 = (bf16[8,192,384]{2,1,0:T(8,128)(2,1)S(1)}, bf16[8,192,384]{2,1,0:T(8,128)(2,1)S(1)}, u32[]{:S(2)}, u32[]{:S(2)}) collective-permute-start(bf16[8,192,384]{2,1,0:T(8,128)(2,1)S(1)} %constant_dynamic-update-slice_fusion.10.a1), channel_id=1, source_target_pairs={{0,1},{1,0},{2,3},{3,2},{4,5},{5,4},{6,7},{7,6},{8,9},{9,8},{10,11... | collective-permute-start | bytes 3538952 | tf_op jit(solution)/shard_map/ppermute | solution.py:528
  136.5 3.1 %collective-permute-start.24 = (bf16[8,96,768]{2,1,0:T(8,128)(2,1)}, bf16[8,96,768]{2,1,0:T(8,128)(2,1)S(1)}, u32[]{:S(2)}, u32[]{:S(2)}) collective-permute-start(bf16[8,96,768]{2,1,0:T(8,128)(2,1)} %get-tuple-element.212), channel_id=1, source_target_pairs={{0,1},{1,0},{2,3},{3,2},{4,5},{5,4},{6,7},{7,6},{8,9},{9,8},{10,11... | collective-permute-start | bytes 3538952 | tf_op jit(solution)/shard_map/ppermute | solution.py:528
  141.3 8.7 %collective-permute-start.25 = (bf16[16,24,3072]{2,1,0:T(8,128)(2,1)}, bf16[16,24,3072]{2,1,0:T(8,128)(2,1)S(1)}, u32[]{:S(2)}, u32[]{:S(2)}) collective-permute-start(bf16[16,24,3072]{2,1,0:T(8,128)(2,1)} %get-tuple-element.213), channel_id=1, source_target_pairs={{0,1},{1,0},{2,3},{3,2},{4,5},{5,4},{6,7},{7,6},{8,9},{9,8},{10,11... | collective-permute-start | bytes 7077896 | tf_op jit(solution)/shard_map/ppermute | solution.py:528
  141.5 16.0 %collective-permute-start.27 = (bf16[8,96,768]{2,1,0:T(8,128)(2,1)}, bf16[8,96,768]{2,1,0:T(8,128)(2,1)S(1)}, u32[]{:S(2)}, u32[]{:S(2)}) collective-permute-start(bf16[8,96,768]{2,1,0:T(8,128)(2,1)} %get-tuple-element.222), channel_id=1, source_target_pairs={{0,1},{1,0},{2,3},{3,2},{4,5},{5,4},{6,7},{7,6},{8,9},{9,8},{10,11... | collective-permute-start | bytes 3538952 | tf_op jit(solution)/shard_map/ppermute | solution.py:528
  141.9 16.2 %collective-permute-start.28 = (bf16[8,96,768]{2,1,0:T(8,128)(2,1)S(1)}, bf16[8,96,768]{2,1,0:T(8,128)(2,1)S(1)}, u32[]{:S(2)}, u32[]{:S(2)}) collective-permute-start(bf16[8,96,768]{2,1,0:T(8,128)(2,1)S(1)} %add_convert_fusion.1), channel_id=1, source_target_pairs={{0,2},{1,5},{2,0},{3,7},{4,6},{5,1},{6,4},{7,3},{8,10},{9,13},{10,... | collective-permute-start | bytes 3538952 | tf_op jit(solution)/shard_map/ppermute | solution.py:528
  143.5 6.6 %copy-start.8 = (bf16[640,768]{1,0:T(8,128)(2,1)S(1)}, bf16[640,768]{1,0:T(8,128)(2,1)}, u32[]{:S(2)}) copy-start(bf16[640,768]{1,0:T(8,128)(2,1)} %copy-done.7) | copy-start | bytes 2949124
  143.5 6.6 %copy-start.12 = (bf16[768,1152]{1,0:T(8,128)(2,1)S(1)}, bf16[768,1152]{1,0:T(8,128)(2,1)}, u32[]{:S(2)}) copy-start(bf16[768,1152]{1,0:T(8,128)(2,1)} %copy-done.11) | copy-start | bytes 5308420
  143.5 6.6 %copy-start.19 = (s32[176]{0:T(256)S(1)}, s32[176]{0:T(256)}, u32[]{:S(2)}) copy-start(s32[176]{0:T(256)} %concatenate.28.place) | copy-start | bytes 2116
  155.6 2.5 %collective-permute-start.29 = (bf16[8,24,1920]{2,1,0:T(8,128)(2,1)S(1)}, bf16[8,24,1920]{2,1,0:T(8,128)(2,1)S(1)}, u32[]{:S(2)}, u32[]{:S(2)}) collective-permute-start(bf16[8,24,1920]{2,1,0:T(8,128)(2,1)S(1)} %get-tuple-element.225), channel_id=1, source_target_pairs={{0,1},{1,0},{2,3},{3,2},{4,5},{5,4},{6,7},{7,6},{8,9},{9,8},{10,11... | collective-permute-start | bytes 2211848 | tf_op jit(solution)/shard_map/ppermute | solution.py:528
  156.1 18.4 %collective-permute-start.26 = (bf16[8,24,3072]{2,1,0:T(8,128)(2,1)S(1)}, bf16[8,24,3072]{2,1,0:T(8,128)(2,1)S(1)}, u32[]{:S(2)}, u32[]{:S(2)}) collective-permute-start(bf16[8,24,3072]{2,1,0:T(8,128)(2,1)S(1)} %add_convert_fusion), channel_id=1, source_target_pairs={{0,2},{1,5},{2,0},{3,7},{4,6},{5,1},{6,4},{7,3},{8,10},{9,13},{10,... | collective-permute-start | bytes 3538952 | tf_op jit(solution)/shard_map/ppermute | solution.py:528
  158.3 18.9 %collective-permute-start.31 = (bf16[4,96,768]{2,1,0:T(8,128)(2,1)S(1)}, bf16[4,96,768]{2,1,0:T(8,128)(2,1)S(1)}, u32[]{:S(2)}, u32[]{:S(2)}) collective-permute-start(bf16[4,96,768]{2,1,0:T(8,128)(2,1)S(1)} %add_convert_fusion.5), channel_id=1, source_target_pairs={{0,8},{1,9},{2,10},{3,11},{4,12},{5,13},{6,14},{7,15},{8,0},{9,1},... | collective-permute-start | bytes 1769480 | tf_op jit(solution)/shard_map/ppermute | solution.py:528
  160.2 8.4 %copy-start.2 = (bf16[4,160,768]{2,1,0:T(8,128)(2,1)S(1)}, bf16[4,160,768]{2,1,0:T(8,128)(2,1)}, u32[]{:S(2)}) copy-start(bf16[4,160,768]{2,1,0:T(8,128)(2,1)} %copy-done.1) | copy-start | bytes 2949124
  160.2 8.4 %copy-start.10 = (bf16[768,1152]{1,0:T(8,128)(2,1)S(1)}, bf16[768,1152]{1,0:T(8,128)(2,1)}, u32[]{:S(2)}) copy-start(bf16[768,1152]{1,0:T(8,128)(2,1)} %copy-done.9) | copy-start | bytes 5308420
  160.2 8.4 %copy-start.16 = (f32[2,16,384]{2,1,0:T(8,128)S(1)}, f32[2,16,384]{2,1,0:T(8,128)}, u32[]{:S(2)}) copy-start(f32[2,16,384]{2,1,0:T(8,128)} %copy-done.15) | copy-start | bytes 147460
  160.2 8.4 %copy-start.17 = (f32[4,8,768]{2,1,0:T(8,128)S(1)}, f32[4,8,768]{2,1,0:T(8,128)}, u32[]{:S(2)}) copy-start(f32[4,8,768]{2,1,0:T(8,128)} %get-tuple-element.237.fcg_ref) | copy-start | bytes 294916
  160.2 8.4 %copy-start.20 = (f32[8,768]{1,0:T(8,128)S(1)}, f32[8,768]{1,0:T(8,128)}, u32[]{:S(2)}) copy-start(f32[8,768]{1,0:T(8,128)} %get-tuple-element.236.mlp_ref) | copy-start | bytes 73732
  160.2 20.1 %collective-permute-start.33 = (bf16[8,24,1920]{2,1,0:T(8,128)(2,1)S(1)}, bf16[8,24,1920]{2,1,0:T(8,128)(2,1)S(1)}, u32[]{:S(2)}, u32[]{:S(2)}) collective-permute-start(bf16[8,24,1920]{2,1,0:T(8,128)(2,1)S(1)} %add_convert_fusion.2), channel_id=1, source_target_pairs={{0,2},{1,5},{2,0},{3,7},{4,6},{5,1},{6,4},{7,3},{8,10},{9,13},{10,... | collective-permute-start | bytes 2211848 | tf_op jit(solution)/shard_map/ppermute | solution.py:528
  173.9 12.2 %collective-permute-start.35 = (bf16[8,32,1152]{2,1,0:T(8,128)(2,1)S(1)}, bf16[8,32,1152]{2,1,0:T(8,128)(2,1)S(1)}, u32[]{:S(2)}, u32[]{:S(2)}) collective-permute-start(bf16[8,32,1152]{2,1,0:T(8,128)(2,1)S(1)} %get-tuple-element.261), channel_id=1, source_target_pairs={{0,1},{1,0},{2,3},{3,2},{4,5},{5,4},{6,7},{7,6},{8,9},{9,8},{10,11... | collective-permute-start | bytes 1769480 | tf_op jit(solution)/shard_map/ppermute | solution.py:528
  174.0 2.8 %collective-permute-start.34 = (bf16[8,32,1152]{2,1,0:T(8,128)(2,1)S(1)}, bf16[8,32,1152]{2,1,0:T(8,128)(2,1)S(1)}, u32[]{:S(2)}, u32[]{:S(2)}) collective-permute-start(bf16[8,32,1152]{2,1,0:T(8,128)(2,1)S(1)} %get-tuple-element.246), channel_id=1, source_target_pairs={{0,1},{1,0},{2,3},{3,2},{4,5},{5,4},{6,7},{7,6},{8,9},{9,8},{10,11... | collective-permute-start | bytes 1769480 | tf_op jit(solution)/shard_map/ppermute | solution.py:528
  174.5 3.4 %collective-permute-start.32 = (bf16[8,24,1920]{2,1,0:T(8,128)(2,1)S(1)}, bf16[8,24,1920]{2,1,0:T(8,128)(2,1)S(1)}, u32[]{:S(2)}, u32[]{:S(2)}) collective-permute-start(bf16[8,24,1920]{2,1,0:T(8,128)(2,1)S(1)} %get-tuple-element.243), channel_id=1, source_target_pairs={{0,1},{1,0},{2,3},{3,2},{4,5},{5,4},{6,7},{7,6},{8,9},{9,8},{10,11... | collective-permute-start | bytes 2211848 | tf_op jit(solution)/shard_map/ppermute | solution.py:528
  176.8 15.4 %collective-permute-start.30 = (bf16[4,24,3072]{2,1,0:T(8,128)(2,1)S(1)}, bf16[4,24,3072]{2,1,0:T(8,128)(2,1)S(1)}, u32[]{:S(2)}, u32[]{:S(2)}) collective-permute-start(bf16[4,24,3072]{2,1,0:T(8,128)(2,1)S(1)} %add_convert_fusion.4), channel_id=1, source_target_pairs={{0,8},{1,9},{2,10},{3,11},{4,12},{5,13},{6,14},{7,15},{8,0},{9,1},... | collective-permute-start | bytes 1769480 | tf_op jit(solution)/shard_map/ppermute | solution.py:528
  177.3 11.0 %collective-permute-start.36 = (bf16[8,32,1152]{2,1,0:T(8,128)(2,1)S(1)}, bf16[8,32,1152]{2,1,0:T(8,128)(2,1)S(1)}, u32[]{:S(2)}, u32[]{:S(2)}) collective-permute-start(bf16[8,32,1152]{2,1,0:T(8,128)(2,1)S(1)} %add_convert_fusion.3), channel_id=1, source_target_pairs={{0,2},{1,5},{2,0},{3,7},{4,6},{5,1},{6,4},{7,3},{8,10},{9,13},{10,... | collective-permute-start | bytes 1769480 | tf_op jit(solution)/shard_map/ppermute | solution.py:528
  183.8 10.1 %collective-permute-start.38 = (bf16[2,96,768]{2,1,0:T(8,128)(2,1)S(1)}, bf16[2,96,768]{2,1,0:T(8,128)(2,1)S(1)}, u32[]{:S(2)}, u32[]{:S(2)}) collective-permute-start(bf16[2,96,768]{2,1,0:T(8,128)(2,1)S(1)} %add_convert_fusion.9), channel_id=1, source_target_pairs={{0,4},{1,3},{2,6},{3,1},{4,0},{5,7},{6,2},{7,5},{8,12},{9,11},{10,... | collective-permute-start | bytes 884744 | tf_op jit(solution)/shard_map/ppermute | solution.py:528
  185.4 9.2 %collective-permute-start.37 = (bf16[4,24,1920]{2,1,0:T(8,128)(2,1)S(1)}, bf16[4,24,1920]{2,1,0:T(8,128)(2,1)S(1)}, u32[]{:S(2)}, u32[]{:S(2)}) collective-permute-start(bf16[4,24,1920]{2,1,0:T(8,128)(2,1)S(1)} %add_convert_fusion.6), channel_id=1, source_target_pairs={{0,4},{1,3},{2,6},{3,1},{4,0},{5,7},{6,2},{7,5},{8,12},{9,11},{10,... | collective-permute-start | bytes 1105928 | tf_op jit(solution)/shard_map/ppermute | solution.py:528
  188.4 9.3 %collective-permute-start.41 = (bf16[4,32,1152]{2,1,0:T(8,128)(2,1)S(1)}, bf16[4,32,1152]{2,1,0:T(8,128)(2,1)S(1)}, u32[]{:S(2)}, u32[]{:S(2)}) collective-permute-start(bf16[4,32,1152]{2,1,0:T(8,128)(2,1)S(1)} %add_convert_fusion.8), channel_id=1, source_target_pairs={{0,4},{1,3},{2,6},{3,1},{4,0},{5,7},{6,2},{7,5},{8,12},{9,11},{10,... | collective-permute-start | bytes 884744 | tf_op jit(solution)/shard_map/ppermute | solution.py:528
  192.4 8.5 %collective-permute-start.40 = (bf16[2,24,3072]{2,1,0:T(8,128)(2,1)S(1)}, bf16[2,24,3072]{2,1,0:T(8,128)(2,1)S(1)}, u32[]{:S(2)}, u32[]{:S(2)}) collective-permute-start(bf16[2,24,3072]{2,1,0:T(8,128)(2,1)S(1)} %add_convert_fusion.7), channel_id=1, source_target_pairs={{0,4},{1,3},{2,6},{3,1},{4,0},{5,7},{6,2},{7,5},{8,12},{9,11},{10,... | collective-permute-start | bytes 884744 | tf_op jit(solution)/shard_map/ppermute | solution.py:528
  194.0 15.4 %collective-permute-start.46 = (bf16[1,96,768]{2,1,0:T(8,128)(2,1)S(1)}, bf16[1,96,768]{2,1,0:T(8,128)(2,1)S(1)}, u32[]{:S(2)}, u32[]{:S(2)}) collective-permute-start(bf16[1,96,768]{2,1,0:T(8,128)(2,1)S(1)} %add_convert_fusion.13), channel_id=1, source_target_pairs={{0,16},{1,17},{2,18},{3,19},{4,20},{5,21},{6,22},{7,23},{8,24},{9,... | collective-permute-start | bytes 442376 | tf_op jit(solution)/shard_map/ppermute | solution.py:528
  194.8 9.3 %collective-permute-start.39 = (bf16[2,24,1920]{2,1,0:T(8,128)(2,1)S(1)}, bf16[2,24,1920]{2,1,0:T(8,128)(2,1)S(1)}, u32[]{:S(2)}, u32[]{:S(2)}) collective-permute-start(bf16[2,24,1920]{2,1,0:T(8,128)(2,1)S(1)} %add_convert_fusion.10), channel_id=1, source_target_pairs={{0,8},{1,9},{2,10},{3,11},{4,12},{5,13},{6,14},{7,15},{8,0},{9,1},... | collective-permute-start | bytes 552968 | tf_op jit(solution)/shard_map/ppermute | solution.py:528
  197.8 11.1 %collective-permute-start.43 = (bf16[2,32,1152]{2,1,0:T(8,128)(2,1)S(1)}, bf16[2,32,1152]{2,1,0:T(8,128)(2,1)S(1)}, u32[]{:S(2)}, u32[]{:S(2)}) collective-permute-start(bf16[2,32,1152]{2,1,0:T(8,128)(2,1)S(1)} %add_convert_fusion.12), channel_id=1, source_target_pairs={{0,8},{1,9},{2,10},{3,11},{4,12},{5,13},{6,14},{7,15},{8,0},{9,1},... | collective-permute-start | bytes 442376 | tf_op jit(solution)/shard_map/ppermute | solution.py:528
  200.9 14.4 %collective-permute-start.45 = (bf16[1,24,3072]{2,1,0:T(8,128)(2,1)S(1)}, bf16[1,24,3072]{2,1,0:T(8,128)(2,1)S(1)}, u32[]{:S(2)}, u32[]{:S(2)}) collective-permute-start(bf16[1,24,3072]{2,1,0:T(8,128)(2,1)S(1)} %add_convert_fusion.11), channel_id=1, source_target_pairs={{0,16},{1,17},{2,18},{3,19},{4,20},{5,21},{6,22},{7,23},{8,24},{9,... | collective-permute-start | bytes 442376 | tf_op jit(solution)/shard_map/ppermute | solution.py:528
  204.2 12.9 %collective-permute-start.42 = (bf16[1,24,1920]{2,1,0:T(8,128)(2,1)S(1)}, bf16[1,24,1920]{2,1,0:T(8,128)(2,1)S(1)}, u32[]{:S(2)}, u32[]{:S(2)}) collective-permute-start(bf16[1,24,1920]{2,1,0:T(8,128)(2,1)S(1)} %add_convert_fusion.14), channel_id=1, source_target_pairs={{0,16},{1,17},{2,18},{3,19},{4,20},{5,21},{6,22},{7,23},{8,24},{9,... | collective-permute-start | bytes 276488 | tf_op jit(solution)/shard_map/ppermute | solution.py:528
  208.9 9.0 %collective-permute-start.44 = (bf16[1,32,1152]{2,1,0:T(8,128)(2,1)S(1)}, bf16[1,32,1152]{2,1,0:T(8,128)(2,1)S(1)}, u32[]{:S(2)}, u32[]{:S(2)}) collective-permute-start(bf16[1,32,1152]{2,1,0:T(8,128)(2,1)S(1)} %add_convert_fusion.15), channel_id=1, source_target_pairs={{0,16},{1,17},{2,18},{3,19},{4,20},{5,21},{6,22},{7,23},{8,24},{9,... | collective-permute-start | bytes 221192 | tf_op jit(solution)/shard_map/ppermute | solution.py:528
  (30 other events, 113.0 us)
where the time goes:
time: 220 us
  Pallas kernels  77.4 us (35%)
  waiting for transfers between devices  66.4 us (30%)
  starting transfers between devices  44 us (20%)
  local copies, waits for them, and re-layouts  17.1 us (8%)
  other arithmetic  13 us (6%)
    ppermute x47, waiting for transfers between devices, move(): return lax.ppermute(value, AXES, pairs)  66.4 us
    ppermute x47, starting transfers between devices, move(): return lax.ppermute(value, AXES, pairs)  44 us
    pallas_call x1, Pallas kernels, shards(): pl.pallas_call(mlp_kernel, grid_spec=pltpu.PrefetchScalarGridSpec(num_sca...  35 us
    pallas_call x1, Pallas kernels, shards(): pl.pallas_call(first_kernel, out_shape=(struct((2, 16, BLOCK), F32), stru...  13.4 us
    pallas_call x2, Pallas kernels, call(): pl.pallas_call(kernel, grid=grid, out_shape=out_shape, in_specs=in_specs,...  13.1 us
    pallas_call x2, Pallas kernels, grad_call(): pl.pallas_call(kernel, out_shape=out_shape, in_specs=[smem] + [vmem] * (l...  10.8 us
    unnamed x106, local copies, waits for them, and re-layouts  10.5 us
  transfers between devices with their start and end apart: 47, of which 25 were waited for; matrix products, arithmetic and copies ran while one was open for 9% of the time, Pallas kernels for 17%

commit v1 on v0

--- a/solution.py
+++ b/solution.py
@@ -821,7 +821,7 @@
         + (shares(96, wide),)
         + (struct((8, 96, wide), BF),) * 2
         + (struct((2, width, BLOCK), BF),),
-        compiler_params=pltpu.CompilerParams(vmem_limit_bytes=60 * MIB),
+        compiler_params=pltpu.CompilerParams(vmem_limit_bytes=52 * MIB),
         cost_estimate=pl.CostEstimate(flops=1, bytes_accessed=1, transcendentals=0),
         name="mlp",
     )(place, counts, *gathered_b1, *gathered_b2, att, rows_in, gout, vec, fcb)

time: 220 us -> 218 us (level)
  waiting for transfers between devices: 66.4 us -> 72 us
  other arithmetic: 13 us -> 9.2 us
  local copies, waits for them, and re-layouts: 17.1 us -> 13.4 us
    ppermute x47, waiting for transfers between devices: 66.4 us -> 72 us  [move(): return lax.ppermute(value, AXES, pairs)]
    unnamed x106 -> x76, local copies, waits for them, and re-layouts: 10.5 us -> 6.85 us
  transfers between devices with their start and end apart: 47 -> 47, of which waited for: 25 -> 24; matrix products, arithmetic and copies ran while one was open for 9% -> 7% of each run, Pallas kernels for 17% -> 17%
where the time goes in v1:
time: 218 us
  Pallas kernels  76.6 us (35%)
  waiting for transfers between devices  72 us (33%)
  starting transfers between devices  44.8 us (21%)
  local copies, waits for them, and re-layouts  13.4 us (6%)
  other arithmetic  9.2 us (4%)
    ppermute x47, waiting for transfers between devices, move(): return lax.ppermute(value, AXES, pairs)  72 us
    ppermute x47, starting transfers between devices, move(): return lax.ppermute(value, AXES, pairs)  44.8 us
    pallas_call x1, Pallas kernels, shards(): pl.pallas_call(mlp_kernel, grid_spec=pltpu.PrefetchScalarGridSpec(num_sca...  34.2 us
    pallas_call x1, Pallas kernels, shards(): pl.pallas_call(first_kernel, out_shape=(struct((2, 16, BLOCK), F32), stru...  13.4 us
    pallas_call x2, Pallas kernels, call(): pl.pallas_call(kernel, grid=grid, out_shape=out_shape, in_specs=in_specs,...  13 us
    pallas_call x2, Pallas kernels, grad_call(): pl.pallas_call(kernel, out_shape=out_shape, in_specs=[smem] + [vmem] * (l...  10.8 us
    unnamed x76, local copies, waits for them, and re-layouts  6.85 us
  transfers between devices with their start and end apart: 47, of which 24 were waited for; matrix products, arithmetic and copies ran while one was open for 7% of the time, Pallas kernels for 17%

profile of v1, /device:TPU:0, one launch (start us, length us, event | category | flops | bytes accessed | tf_op | source)
XLA Modules:
  0.0 217.5 jit_solution(7699240344264513598)
XLA Ops:
  1.4 1.8 share.1
  3.7 1.2 collective-permute-done.got_ref
  5.6 1.9 pair.1
  7.4 2.9 %collective-permute-start.3 = (bf16[192,384]{1,0:T(8,128)(2,1)}, bf16[192,384]{1,0:T(8,128)(2,1)S(1)}, u32[]{:S(2)}, u32[]{:S(2)}) collective-permute-start(bf16[192,384]{1,0:T(8,128)(2,1)} %get-tuple-element.174), channel_id=1, source_target_pairs={{0,4},{1,3},{2,6},{3,1},{4,0},{5,7},{6,2},{7,5},{8,12},{9,11},{10,... | collective-permute-start | bytes 442376 | tf_op jit(solution)/shard_map/ppermute | solution.py:528
  10.3 3.6 %collective-permute-start.2 = (bf16[160,384]{1,0:T(8,128)(2,1)}, bf16[160,384]{1,0:T(8,128)(2,1)S(1)}, u32[]{:S(2)}, u32[]{:S(2)}) collective-permute-start(bf16[160,384]{1,0:T(8,128)(2,1)} %get-tuple-element.175), channel_id=1, source_target_pairs={{0,24},{1,25},{2,26},{3,27},{4,28},{5,29},{6,30},{7,31},{8,0},{9,1... | collective-permute-start | bytes 368648 | tf_op jit(solution)/shard_map/ppermute | solution.py:528
  13.9 4.0 %collective-permute-done.2 = bf16[160,384]{1,0:T(8,128)(2,1)S(1)} collective-permute-done((bf16[160,384]{1,0:T(8,128)(2,1)}, bf16[160,384]{1,0:T(8,128)(2,1)S(1)}, u32[]{:S(2)}, u32[]{:S(2)}) %collective-permute-start.2) | collective-permute-done | bytes 122912 | tf_op jit(solution)/shard_map/ppermute | solution.py:528
  17.9 2.8 %collective-permute-done.1 = bf16[160,384]{1,0:T(8,128)(2,1)S(1)} collective-permute-done((bf16[160,384]{1,0:T(8,128)(2,1)}, bf16[160,384]{1,0:T(8,128)(2,1)S(1)}, u32[]{:S(2)}, u32[]{:S(2)}) %collective-permute-start.1) | collective-permute-done | bytes 122912 | tf_op jit(solution)/shard_map/ppermute | solution.py:528
  20.8 1.0 pad_maximum_fusion.4
  21.8 1.6 collective-permute-start.5
  23.4 0.9 constant_dynamic-update-slice_fusion.4
  24.4 6.6 %collective-permute-done.4 = bf16[160,384]{1,0:T(8,128)(2,1)S(1)} collective-permute-done((bf16[160,384]{1,0:T(8,128)(2,1)S(1)}, bf16[160,384]{1,0:T(8,128)(2,1)S(1)}, u32[]{:S(2)}, u32[]{:S(2)}) %collective-permute-start.4) | collective-permute-done | bytes 122912 | tf_op jit(solution)/shard_map/ppermute | solution.py:528
  31.0 2.0 collective-permute-start.7
  33.1 1.0 pad_maximum_fusion.3
  34.8 0.8 constant_dynamic-update-slice_fusion.17
  35.6 5.1 %collective-permute-done.8 = bf16[240,384]{1,0:T(8,128)(2,1)S(1)} collective-permute-done((bf16[240,384]{1,0:T(8,128)(2,1)}, bf16[240,384]{1,0:T(8,128)(2,1)S(1)}, u32[]{:S(2)}, u32[]{:S(2)}) %collective-permute-start.8) | collective-permute-done | bytes 184352 | tf_op jit(solution)/shard_map/ppermute | solution.py:528
  40.7 2.3 %collective-permute-done.6 = bf16[4,160,384]{2,1,0:T(8,128)(2,1)} collective-permute-done((bf16[4,160,384]{2,1,0:T(8,128)(2,1)S(1)}, bf16[4,160,384]{2,1,0:T(8,128)(2,1)}, u32[]{:S(2)}, u32[]{:S(2)}) %collective-permute-start.6) | collective-permute-done | bytes 491552 | tf_op jit(solution)/shard_map/ppermute | solution.py:528
  43.3 1.1 constant_dynamic-update-slice_fusion.own0
  44.5 1.6 collective-permute-start.9
  46.1 2.7 %collective-permute-start.12 = (bf16[3,240,384]{2,1,0:T(8,128)(2,1)S(1)}, bf16[3,240,384]{2,1,0:T(8,128)(2,1)S(1)}, u32[]{:S(2)}, u32[]{:S(2)}) collective-permute-start(bf16[3,240,384]{2,1,0:T(8,128)(2,1)S(1)} %pad_maximum_fusion.2), channel_id=1, source_target_pairs={{0,4},{1,3},{2,6},{3,1},{4,0},{5,7},{6,2},{7,5},{8,12},{9,11},{10,... | collective-permute-start | bytes 1658888 | tf_op jit(solution)/shard_map/ppermute | solution.py:528
  49.5 1.1 copy.32
  53.4 7.8 %collective-permute-done.12 = bf16[3,240,384]{2,1,0:T(8,128)(2,1)S(1)} collective-permute-done((bf16[3,240,384]{2,1,0:T(8,128)(2,1)S(1)}, bf16[3,240,384]{2,1,0:T(8,128)(2,1)S(1)}, u32[]{:S(2)}, u32[]{:S(2)}) %collective-permute-start.12) | collective-permute-done | bytes 552992 | tf_op jit(solution)/shard_map/ppermute | solution.py:528
  61.6 1.7 collective-permute-start.15
  63.9 1.5 collective-permute-start.14
  65.9 1.7 collective-permute-start.17
  67.7 1.2 collective-permute-start.16
  68.9 13.4 %first.1 = (f32[2,16,384]{2,1,0:T(8,128)S(1)}, f32[4,1,768]{2,1,0:T(1,128)S(1)}, bf16[768,640]{1,0:T(8,128)(2,1)S(1)}, bf16[2,640,1152]{2,1,0:T(8,128)(2,1)S(1)}...) custom-call(s32[176]{0:T(256)S(1)} %copy-done.6, ...), custom_call_target="tpu_custom_call" | custom-call | flops 1 | bytes 1 | tf_op jit(solution)/shard_map/first/pallas_call | solution.py:776
  82.5 9.3 %collective-permute-done.13 = bf16[4,192,384]{2,1,0:T(8,128)(2,1)S(1)} collective-permute-done((bf16[4,192,384]{2,1,0:T(8,128)(2,1)S(1)}, bf16[4,192,384]{2,1,0:T(8,128)(2,1)S(1)}, u32[]{:S(2)}, u32[]{:S(2)}) %collective-permute-start.13) | collective-permute-done | bytes 589856 | tf_op jit(solution)/shard_map/ppermute | solution.py:528
  93.3 3.7 %collective-permute-done.20.a2 = bf16[8,192,384]{2,1,0:T(8,128)(2,1)S(1)} collective-permute-done((bf16[8,192,384]{2,1,0:T(8,128)(2,1)S(1)}, bf16[8,192,384]{2,1,0:T(8,128)(2,1)S(1)}, u32[]{:S(2)}, u32[]{:S(2)}) %collective-permute-start.20) | collective-permute-done | bytes 1179680 | tf_op jit(solution)/shard_map/ppermute | solution.py:528
  97.0 1.7 collective-permute-done.21.a3
  98.8 1.0 copy-done.22
  100.2 34.2 %mlp.1 = (bf16[640,768]{1,0:T(8,128)(2,1)S(1)}, bf16[640,768]{1,0:T(8,128)(2,1)}, bf16[16,24,3072]{2,1,0:T(8,128)(2,1)}, bf16[16,24,3072]{2,1,0:T(8,128)(2,1)}, ...) custom-call(s32[176]{0:T(256)S(1)} %copy-done.6, ...), custom_call_target="tpu_custom_call" | custom-call | flops 1 | bytes 1 | tf_op jit(solution)/shard_map/mlp/pallas_call | solution.py:801
  134.6 2.9 %collective-permute-done.24 = bf16[8,96,768]{2,1,0:T(8,128)(2,1)S(1)} collective-permute-done((bf16[8,96,768]{2,1,0:T(8,128)(2,1)}, bf16[8,96,768]{2,1,0:T(8,128)(2,1)S(1)}, u32[]{:S(2)}, u32[]{:S(2)}) %collective-permute-start.24) | collective-permute-done | bytes 1179680 | tf_op jit(solution)/shard_map/ppermute | solution.py:528
  137.6 1.7 add_convert_fusion.1
  139.9 1.7 collective-permute-start.28
  141.6 6.5 %attention_back.2.gqkv_ref = bf16[640,1152]{1,0:T(8,128)(2,1)S(1)} custom-call(bf16[2,768,384]{2,1,0:T(8,128)(2,1)S(1)} %copy-done.3, bf16[2,640,1152]{2,1,0:T(8,128)(2,1)S(1)} %get-tuple-element.215.refs_1_, f32[4,160,160]{2,1,0:T(8,128)S(1)} %get-tuple-element.216.refs_2_, bf16[640,768]{1,0:T(8,128)(2,1)S(1)} %copy-done), custom_call_target="tpu_custom_call" | custom-call | flops 1 | bytes 1 | tf_op jit(solution)/shard_map/attention_back/pallas_call | solution.py:748
  148.2 5.5 %qkv_grad.1 = (f32[640,768]{1,0:T(8,128)S(1)}, f32[1,1152]{1,0:T(1,128)S(1)}, bf16[16,24,1920]{2,1,0:T(8,128)(2,1)S(1)}, bf16[8,24,1920]{2,1,0:T(8,128)(2,1)S(1)}, bf16[8,24,1920]{2,1,0:T(8,128)(2,1)S(1)}) custom-call(s32[176]{0:T(256)S(1)} %copy-done.6, bf16[768,640]{1,0:T(8,128)(2,1)S(1)} %get-tuple-element.221.h1_turned, ...), custom_call_target="tpu_custom_call" | custom-call | flops 1 | bytes 1 | tf_op jit(solution)/shard_map/qkv_grad/pallas_call | solution.py:861
  154.3 1.3 collective-permute-start.26
  156.3 1.5 collective-permute-start.31
  158.0 1.8 collective-permute-start.33
  159.8 6.5 %attention_back.3.gqkv_ref = bf16[640,1152]{1,0:T(8,128)(2,1)S(1)} custom-call(bf16[2,768,384]{2,1,0:T(8,128)(2,1)S(1)} %copy-done.3, bf16[2,640,1152]{2,1,0:T(8,128)(2,1)S(1)} %get-tuple-element.215.refs_1_, f32[4,160,160]{2,1,0:T(8,128)S(1)} %get-tuple-element.216.refs_2_, bf16[640,768]{1,0:T(8,128)(2,1)S(1)} %copy-done), custom_call_target="tpu_custom_call" | custom-call | flops 1 | bytes 1 | tf_op jit(solution)/shard_map/attention_back/pallas_call | solution.py:748
  166.4 5.3 %input_grad.1 = (bf16[640,768]{1,0:T(8,128)(2,1)S(1)}, bf16[16,32,1152]{2,1,0:T(8,128)(2,1)S(1)}, bf16[8,32,1152]{2,1,0:T(8,128)(2,1)S(1)}, bf16[8,32,1152]{2,1,0:T(8,128)(2,1)S(1)}) custom-call(s32[176]{0:T(256)S(1)} %copy-done.6, bf16[768,640]{1,0:T(8,128)(2,1)S(1)} %get-tuple-element.221.h1_turned, bf16[640,1152]{1,0:T(8,128)(2,1)S(1)} %attention_back.3.gqkv_ref, ...), custom_call_target="tpu_custom_call" | custom-call | flops 1 | bytes 1 | tf_op jit(solution)/shard_map/input_grad/pallas_call | solution.py:861
  172.5 2.0 collective-permute-done.34
  175.7 2.8 %collective-permute-done.33.refs_2_ = bf16[8,24,1920]{2,1,0:T(8,128)(2,1)S(1)} collective-permute-done((bf16[8,24,1920]{2,1,0:T(8,128)(2,1)S(1)}, bf16[8,24,1920]{2,1,0:T(8,128)(2,1)S(1)}, u32[]{:S(2)}, u32[]{:S(2)}) %collective-permute-start.33) | collective-permute-done | bytes 737312 | tf_op jit(solution)/shard_map/ppermute | solution.py:528
  178.4 1.7 copy.35
  180.1 1.7 copy.36
  181.9 1.5 collective-permute-start.38
  184.2 2.1 collective-permute-done.36.refs_8_
  186.4 1.5 collective-permute-start.41
  187.9 2.0 collective-permute-done.30
  190.1 1.8 collective-permute-start.40
  192.8 1.6 collective-permute-start.39
  194.5 1.3 collective-permute-done.41.refs_9_
  195.9 1.7 collective-permute-start.43
  197.6 1.4 collective-permute-done.40
  199.1 1.3 collective-permute-start.45
  200.4 1.6 collective-permute-done.39.refs_4_
  202.1 1.2 collective-permute-start.42
  203.2 3.4 %collective-permute-done.43.refs_10_ = bf16[2,32,1152]{2,1,0:T(8,128)(2,1)S(1)} collective-permute-done((bf16[2,32,1152]{2,1,0:T(8,128)(2,1)S(1)}, bf16[2,32,1152]{2,1,0:T(8,128)(2,1)S(1)}, u32[]{:S(2)}, u32[]{:S(2)}) %collective-permute-start.43) | collective-permute-done | bytes 147488 | tf_op jit(solution)/shard_map/ppermute | solution.py:528
  207.2 0.8 add_bitcast_fusion.1
  208.0 5.4 %collective-permute-done.45 = bf16[1,24,3072]{2,1,0:T(8,128)(2,1)S(1)} collective-permute-done((bf16[1,24,3072]{2,1,0:T(8,128)(2,1)S(1)}, bf16[1,24,3072]{2,1,0:T(8,128)(2,1)S(1)}, u32[]{:S(2)}, u32[]{:S(2)}) %collective-permute-start.45) | collective-permute-done | bytes 147488 | tf_op jit(solution)/shard_map/ppermute | solution.py:528
  213.4 0.8 add_bitcast_fusion
  214.3 0.9 collective-permute-done.42.refs_5_
  215.1 0.8 collective-permute-done.44.refs_11_
  215.9 1.4 last.1
  (157 shorter events, 17.1 us)
Async XLA Ops:
  3.2 1.7 collective-permute-start
  7.4 27.2 %copy-start.17 = (bf16[192,384]{1,0:T(8,128)(2,1)S(1)}, bf16[192,384]{1,0:T(8,128)(2,1)}, u32[]{:S(2)}) copy-start(bf16[192,384]{1,0:T(8,128)(2,1)} %get-tuple-element.174) | copy-start | bytes 442372
  7.4 13.3 %collective-permute-start.3 = (bf16[192,384]{1,0:T(8,128)(2,1)}, bf16[192,384]{1,0:T(8,128)(2,1)S(1)}, u32[]{:S(2)}, u32[]{:S(2)}) collective-permute-start(bf16[192,384]{1,0:T(8,128)(2,1)} %get-tuple-element.174), channel_id=1, source_target_pairs={{0,4},{1,3},{2,6},{3,1},{4,0},{5,7},{6,2},{7,5},{8,12},{9,11},{10,... | collective-permute-start | bytes 442376 | tf_op jit(solution)/shard_map/ppermute | solution.py:528
  10.3 7.6 %collective-permute-start.2 = (bf16[160,384]{1,0:T(8,128)(2,1)}, bf16[160,384]{1,0:T(8,128)(2,1)S(1)}, u32[]{:S(2)}, u32[]{:S(2)}) collective-permute-start(bf16[160,384]{1,0:T(8,128)(2,1)} %get-tuple-element.175), channel_id=1, source_target_pairs={{0,24},{1,25},{2,26},{3,27},{4,28},{5,29},{6,30},{7,31},{8,0},{9,1... | collective-permute-start | bytes 368648 | tf_op jit(solution)/shard_map/ppermute | solution.py:528
  13.9 6.9 %collective-permute-start.1 = (bf16[160,384]{1,0:T(8,128)(2,1)}, bf16[160,384]{1,0:T(8,128)(2,1)S(1)}, u32[]{:S(2)}, u32[]{:S(2)}) collective-permute-start(bf16[160,384]{1,0:T(8,128)(2,1)} %get-tuple-element.175), channel_id=1, source_target_pairs={{0,8},{1,9},{2,10},{3,11},{4,12},{5,13},{6,14},{7,15},{8,16},{9,17... | collective-permute-start | bytes 368648 | tf_op jit(solution)/shard_map/ppermute | solution.py:528
  20.8 14.0 %copy-start.19 = (bf16[192,384]{1,0:T(8,128)(2,1)}, bf16[192,384]{1,0:T(8,128)(2,1)S(1)}, u32[]{:S(2)}) copy-start(bf16[192,384]{1,0:T(8,128)(2,1)S(1)} %collective-permute-done.3) | copy-start | bytes 442372
  21.8 9.2 %collective-permute-start.5 = (bf16[2,192,384]{2,1,0:T(8,128)(2,1)S(1)}, bf16[2,192,384]{2,1,0:T(8,128)(2,1)S(1)}, u32[]{:S(2)}, u32[]{:S(2)}) collective-permute-start(bf16[2,192,384]{2,1,0:T(8,128)(2,1)S(1)} %pad_maximum_fusion.4), channel_id=1, source_target_pairs={{0,2},{1,5},{2,0},{3,7},{4,6},{5,1},{6,4},{7,3},{8,10},{9,13},{10,... | collective-permute-start | bytes 884744 | tf_op jit(solution)/shard_map/ppermute | solution.py:528
  24.3 10.5 %copy-start.27 = (bf16[240,384]{1,0:T(8,128)(2,1)S(1)}, bf16[240,384]{1,0:T(8,128)(2,1)}, u32[]{:S(2)}) copy-start(bf16[240,384]{1,0:T(8,128)(2,1)} %get-tuple-element.182) | copy-start | bytes 552964
  24.3 6.7 %collective-permute-start.4 = (bf16[160,384]{1,0:T(8,128)(2,1)S(1)}, bf16[160,384]{1,0:T(8,128)(2,1)S(1)}, u32[]{:S(2)}, u32[]{:S(2)}) collective-permute-start(bf16[160,384]{1,0:T(8,128)(2,1)S(1)} %collective-permute-done.1), channel_id=1, source_target_pairs={{0,8},{1,9},{2,10},{3,11},{4,12},{5,13},{6,14},{7,15},{8,16},{9,17... | collective-permute-start | bytes 368648 | tf_op jit(solution)/shard_map/ppermute | solution.py:528
  31.0 9.7 %collective-permute-start.8 = (bf16[240,384]{1,0:T(8,128)(2,1)}, bf16[240,384]{1,0:T(8,128)(2,1)S(1)}, u32[]{:S(2)}, u32[]{:S(2)}) collective-permute-start(bf16[240,384]{1,0:T(8,128)(2,1)} %get-tuple-element.182), channel_id=1, source_target_pairs={{0,24},{1,25},{2,26},{3,27},{4,28},{5,29},{6,30},{7,31},{8,0},{9,1... | collective-permute-start | bytes 552968 | tf_op jit(solution)/shard_map/ppermute | solution.py:528
  31.0 9.7 %collective-permute-start.7 = (bf16[240,384]{1,0:T(8,128)(2,1)}, bf16[240,384]{1,0:T(8,128)(2,1)S(1)}, u32[]{:S(2)}, u32[]{:S(2)}) collective-permute-start(bf16[240,384]{1,0:T(8,128)(2,1)} %get-tuple-element.182), channel_id=1, source_target_pairs={{0,8},{1,9},{2,10},{3,11},{4,12},{5,13},{6,14},{7,15},{8,16},{9,17... | collective-permute-start | bytes 552968 | tf_op jit(solution)/shard_map/ppermute | solution.py:528
  34.0 9.0 %copy-start.7 = (s32[4]{0:T(128)S(1)}, s32[4]{0:T(128)}, u32[]{:S(2)}) copy-start(s32[4]{0:T(128)} %counts.1) | copy-start | bytes 52
  34.1 9.0 %collective-permute-start.6 = (bf16[4,160,384]{2,1,0:T(8,128)(2,1)S(1)}, bf16[4,160,384]{2,1,0:T(8,128)(2,1)}, u32[]{:S(2)}, u32[]{:S(2)}) collective-permute-start(bf16[4,160,384]{2,1,0:T(8,128)(2,1)S(1)} %pad_maximum_fusion.3), channel_id=1, source_target_pairs={{0,4},{1,3},{2,6},{3,1},{4,0},{5,7},{6,2},{7,5},{8,12},{9,11},{10,... | collective-permute-start | bytes 1474568 | tf_op jit(solution)/shard_map/ppermute | solution.py:528
  35.6 13.2 %copy-start.25 = (bf16[4,153,768]{2,0,1:T(4,128)(2,1)S(1)}, bf16[4,153,768]{2,0,1:T(4,128)(2,1)}, u32[]{:S(2)}) copy-start(bf16[4,153,768]{2,0,1:T(4,128)(2,1)} %param.31) | copy-start | bytes 2820100
  43.3 10.1 %collective-permute-start.10 = (bf16[240,384]{1,0:T(8,128)(2,1)S(1)}, bf16[240,384]{1,0:T(8,128)(2,1)S(1)}, u32[]{:S(2)}, u32[]{:S(2)}) collective-permute-start(bf16[240,384]{1,0:T(8,128)(2,1)S(1)} %collective-permute-done.7), channel_id=1, source_target_pairs={{0,8},{1,9},{2,10},{3,11},{4,12},{5,13},{6,14},{7,15},{8,16},{9,17... | collective-permute-start | bytes 552968 | tf_op jit(solution)/shard_map/ppermute | solution.py:528
  44.5 16.8 %collective-permute-start.9 = (bf16[8,160,384]{2,1,0:T(8,128)(2,1)S(1)}, bf16[8,160,384]{2,1,0:T(8,128)(2,1)S(1)}, u32[]{:S(2)}, u32[]{:S(2)}) collective-permute-start(bf16[8,160,384]{2,1,0:T(8,128)(2,1)S(1)} %constant_dynamic-update-slice_fusion.own0), channel_id=1, source_target_pairs={{0,2},{1,5},{2,0},{3,7},{4,6},{5,1},{6,4},{7,3},{8,10},{9,13},{10,... | collective-permute-start | bytes 2949128 | tf_op jit(solution)/shard_map/ppermute | solution.py:528
  46.1 15.0 %collective-permute-start.12 = (bf16[3,240,384]{2,1,0:T(8,128)(2,1)S(1)}, bf16[3,240,384]{2,1,0:T(8,128)(2,1)S(1)}, u32[]{:S(2)}, u32[]{:S(2)}) collective-permute-start(bf16[3,240,384]{2,1,0:T(8,128)(2,1)S(1)} %pad_maximum_fusion.2), channel_id=1, source_target_pairs={{0,4},{1,3},{2,6},{3,1},{4,0},{5,7},{6,2},{7,5},{8,12},{9,11},{10,... | collective-permute-start | bytes 1658888 | tf_op jit(solution)/shard_map/ppermute | solution.py:528
  48.8 12.5 %collective-permute-start.11 = (bf16[4,192,384]{2,1,0:T(8,128)(2,1)S(1)}, bf16[4,192,384]{2,1,0:T(8,128)(2,1)S(1)}, u32[]{:S(2)}, u32[]{:S(2)}) collective-permute-start(bf16[4,192,384]{2,1,0:T(8,128)(2,1)S(1)} %pad_maximum_fusion.1), channel_id=1, source_target_pairs={{0,8},{1,9},{2,10},{3,11},{4,12},{5,13},{6,14},{7,15},{8,16},{9,17... | collective-permute-start | bytes 1769480 | tf_op jit(solution)/shard_map/ppermute | solution.py:528
  51.8 17.1 %copy-start.1 = (bf16[4,160,768]{2,1,0:T(8,128)(2,1)}, bf16[4,160,768]{2,1,0:T(8,128)(2,1)S(1)}, u32[]{:S(2)}) copy-start(bf16[4,160,768]{2,1,0:T(8,128)(2,1)S(1)} %pad.11.clone) | copy-start | bytes 2949124
  61.3 7.6 %copy-start.6 = (s32[176]{0:T(256)S(1)}, s32[176]{0:T(256)}, u32[]{:S(2)}) copy-start(s32[176]{0:T(256)} %concatenate.28.place) | copy-start | bytes 2116
  61.6 30.2 %collective-permute-start.15 = (bf16[7,240,384]{2,1,0:T(8,128)(2,1)S(1)}, bf16[7,240,384]{2,1,0:T(8,128)(2,1)S(1)}, u32[]{:S(2)}, u32[]{:S(2)}) collective-permute-start(bf16[7,240,384]{2,1,0:T(8,128)(2,1)S(1)} %get-tuple-element.329), channel_id=1, source_target_pairs={{0,2},{1,5},{2,0},{3,7},{4,6},{5,1},{6,4},{7,3},{8,10},{9,13},{10,... | collective-permute-start | bytes 3870728 | tf_op jit(solution)/shard_map/ppermute | solution.py:528
  63.4 2.6 %collective-permute-start.18 = (bf16[8,160,384]{2,1,0:T(8,128)(2,1)S(1)}, bf16[8,160,384]{2,1,0:T(8,128)(2,1)S(1)}, u32[]{:S(2)}, u32[]{:S(2)}) collective-permute-start(bf16[8,160,384]{2,1,0:T(8,128)(2,1)S(1)} %constant_dynamic-update-slice_fusion.own0), channel_id=1, source_target_pairs={{0,1},{1,0},{2,3},{3,2},{4,5},{5,4},{6,7},{7,6},{8,9},{9,8},{10,11... | collective-permute-start | bytes 2949128 | tf_op jit(solution)/shard_map/ppermute | solution.py:528
  63.4 4.3 %collective-permute-start.19 = (bf16[8,160,384]{2,1,0:T(8,128)(2,1)S(1)}, bf16[8,160,384]{2,1,0:T(8,128)(2,1)S(1)}, u32[]{:S(2)}, u32[]{:S(2)}) collective-permute-start(bf16[8,160,384]{2,1,0:T(8,128)(2,1)S(1)} %collective-permute-done.9.own1), channel_id=1, source_target_pairs={{0,1},{1,0},{2,3},{3,2},{4,5},{5,4},{6,7},{7,6},{8,9},{9,8},{10,11... | collective-permute-start | bytes 2949128 | tf_op jit(solution)/shard_map/ppermute | solution.py:528
  63.9 18.6 %collective-permute-start.14 = (bf16[4,192,384]{2,1,0:T(8,128)(2,1)S(1)}, bf16[4,192,384]{2,1,0:T(8,128)(2,1)S(1)}, u32[]{:S(2)}, u32[]{:S(2)}) collective-permute-start(bf16[4,192,384]{2,1,0:T(8,128)(2,1)S(1)} %pad_maximum_fusion.1), channel_id=1, source_target_pairs={{0,24},{1,25},{2,26},{3,27},{4,28},{5,29},{6,30},{7,31},{8,0},{9,1... | collective-permute-start | bytes 1769480 | tf_op jit(solution)/shard_map/ppermute | solution.py:528
  65.3 26.5 %collective-permute-start.13 = (bf16[4,192,384]{2,1,0:T(8,128)(2,1)S(1)}, bf16[4,192,384]{2,1,0:T(8,128)(2,1)S(1)}, u32[]{:S(2)}, u32[]{:S(2)}) collective-permute-start(bf16[4,192,384]{2,1,0:T(8,128)(2,1)S(1)} %collective-permute-done.11), channel_id=1, source_target_pairs={{0,8},{1,9},{2,10},{3,11},{4,12},{5,13},{6,14},{7,15},{8,16},{9,17... | collective-permute-start | bytes 1769480 | tf_op jit(solution)/shard_map/ppermute | solution.py:528
  65.9 16.3 %collective-permute-start.17 = (bf16[1,240,384]{2,1,0:T(8,128)(2,1)S(1)}, bf16[1,240,384]{2,1,0:T(8,128)(2,1)S(1)}, u32[]{:S(2)}, u32[]{:S(2)}) collective-permute-start(bf16[1,240,384]{2,1,0:T(8,128)(2,1)S(1)} %bitcast.54), channel_id=1, source_target_pairs={{0,4},{1,3},{2,6},{3,1},{4,0},{5,7},{6,2},{7,5},{8,12},{9,11},{10,... | collective-permute-start | bytes 552968 | tf_op jit(solution)/shard_map/ppermute | solution.py:528
  67.7 14.8 %collective-permute-start.16 = (bf16[1,240,384]{2,1,0:T(8,128)(2,1)S(1)}, bf16[1,240,384]{2,1,0:T(8,128)(2,1)S(1)}, u32[]{:S(2)}, u32[]{:S(2)}) collective-permute-start(bf16[1,240,384]{2,1,0:T(8,128)(2,1)S(1)} %bitcast.55), channel_id=1, source_target_pairs={{0,6},{1,7},{2,4},{3,5},{4,2},{5,3},{6,0},{7,1},{8,14},{9,15},{10,... | collective-permute-start | bytes 552968 | tf_op jit(solution)/shard_map/ppermute | solution.py:528
  82.3 9.7 %copy-start.4 = (bf16[640,768]{1,0:T(8,128)(2,1)}, bf16[640,768]{1,0:T(8,128)(2,1)S(1)}, u32[]{:S(2)}) copy-start(bf16[640,768]{1,0:T(8,128)(2,1)S(1)} %get-tuple-element.204.att_far.att_ref) | copy-start | bytes 2949124
  82.3 9.7 %copy-start.14 = (bf16[8,240,384]{2,1,0:T(8,128)(2,1)}, bf16[8,240,384]{2,1,0:T(8,128)(2,1)S(1)}, u32[]{:S(2)}) copy-start(bf16[8,240,384]{2,1,0:T(8,128)(2,1)S(1)} %constant_dynamic-update-slice_fusion.12.b0) | copy-start | bytes 4423684
  82.3 9.8 %copy-start.18 = (bf16[192,384]{1,0:T(8,128)(2,1)S(1)}, bf16[192,384]{1,0:T(8,128)(2,1)}, u32[]{:S(2)}) copy-start(bf16[192,384]{1,0:T(8,128)(2,1)} %get-tuple-element.174) | copy-start | bytes 442372
  82.3 9.8 %copy-start.20 = (bf16[192,384]{1,0:T(8,128)(2,1)S(1)}, bf16[192,384]{1,0:T(8,128)(2,1)}, u32[]{:S(2)}) copy-start(bf16[192,384]{1,0:T(8,128)(2,1)} %copy-done.19) | copy-start | bytes 442372
  82.4 9.8 %copy-start.24 = (bf16[2,192,384]{2,1,0:T(8,128)(2,1)S(1)}, bf16[2,192,384]{2,1,0:T(8,128)(2,1)}, u32[]{:S(2)}) copy-start(bf16[2,192,384]{2,1,0:T(8,128)(2,1)} %copy-done.23) | copy-start | bytes 884740
  82.4 14.7 %collective-permute-start.22 = (bf16[8,240,384]{2,1,0:T(8,128)(2,1)S(1)}, bf16[8,240,384]{2,1,0:T(8,128)(2,1)S(1)}, u32[]{:S(2)}, u32[]{:S(2)}) collective-permute-start(bf16[8,240,384]{2,1,0:T(8,128)(2,1)S(1)} %constant_dynamic-update-slice_fusion.12.b0), channel_id=1, source_target_pairs={{0,1},{1,0},{2,3},{3,2},{4,5},{5,4},{6,7},{7,6},{8,9},{9,8},{10,11... | collective-permute-start | bytes 4423688 | tf_op jit(solution)/shard_map/ppermute | solution.py:528
  92.0 6.7 %collective-permute-start.23 = (bf16[8,240,384]{2,1,0:T(8,128)(2,1)S(1)}, bf16[8,240,384]{2,1,0:T(8,128)(2,1)S(1)}, u32[]{:S(2)}, u32[]{:S(2)}) collective-permute-start(bf16[8,240,384]{2,1,0:T(8,128)(2,1)S(1)} %constant_dynamic-update-slice_fusion.18.b1), channel_id=1, source_target_pairs={{0,1},{1,0},{2,3},{3,2},{4,5},{5,4},{6,7},{7,6},{8,9},{9,8},{10,11... | collective-permute-start | bytes 4423688 | tf_op jit(solution)/shard_map/ppermute | solution.py:528
  92.3 7.9 %copy-start.9 = (bf16[8,192,384]{2,1,0:T(8,128)(2,1)}, bf16[8,192,384]{2,1,0:T(8,128)(2,1)S(1)}, u32[]{:S(2)}) copy-start(bf16[8,192,384]{2,1,0:T(8,128)(2,1)S(1)} %pad_maximum_fusion.a0) | copy-start | bytes 3538948
  92.3 4.7 %collective-permute-start.20 = (bf16[8,192,384]{2,1,0:T(8,128)(2,1)S(1)}, bf16[8,192,384]{2,1,0:T(8,128)(2,1)S(1)}, u32[]{:S(2)}, u32[]{:S(2)}) collective-permute-start(bf16[8,192,384]{2,1,0:T(8,128)(2,1)S(1)} %pad_maximum_fusion.a0), channel_id=1, source_target_pairs={{0,1},{1,0},{2,3},{3,2},{4,5},{5,4},{6,7},{7,6},{8,9},{9,8},{10,11... | collective-permute-start | bytes 3538952 | tf_op jit(solution)/shard_map/ppermute | solution.py:528
  93.2 5.5 %copy-start.10 = (bf16[8,192,384]{2,1,0:T(8,128)(2,1)}, bf16[8,192,384]{2,1,0:T(8,128)(2,1)S(1)}, u32[]{:S(2)}) copy-start(bf16[8,192,384]{2,1,0:T(8,128)(2,1)S(1)} %constant_dynamic-update-slice_fusion.10.a1) | copy-start | bytes 3538948
  93.2 5.5 %collective-permute-start.21 = (bf16[8,192,384]{2,1,0:T(8,128)(2,1)S(1)}, bf16[8,192,384]{2,1,0:T(8,128)(2,1)S(1)}, u32[]{:S(2)}, u32[]{:S(2)}) collective-permute-start(bf16[8,192,384]{2,1,0:T(8,128)(2,1)S(1)} %constant_dynamic-update-slice_fusion.10.a1), channel_id=1, source_target_pairs={{0,1},{1,0},{2,3},{3,2},{4,5},{5,4},{6,7},{7,6},{8,9},{9,8},{10,11... | collective-permute-start | bytes 3538952 | tf_op jit(solution)/shard_map/ppermute | solution.py:528
  134.4 3.1 %collective-permute-start.24 = (bf16[8,96,768]{2,1,0:T(8,128)(2,1)}, bf16[8,96,768]{2,1,0:T(8,128)(2,1)S(1)}, u32[]{:S(2)}, u32[]{:S(2)}) collective-permute-start(bf16[8,96,768]{2,1,0:T(8,128)(2,1)} %get-tuple-element.212), channel_id=1, source_target_pairs={{0,1},{1,0},{2,3},{3,2},{4,5},{5,4},{6,7},{7,6},{8,9},{9,8},{10,11... | collective-permute-start | bytes 3538952 | tf_op jit(solution)/shard_map/ppermute | solution.py:528
  139.3 8.9 %collective-permute-start.25 = (bf16[16,24,3072]{2,1,0:T(8,128)(2,1)}, bf16[16,24,3072]{2,1,0:T(8,128)(2,1)S(1)}, u32[]{:S(2)}, u32[]{:S(2)}) collective-permute-start(bf16[16,24,3072]{2,1,0:T(8,128)(2,1)} %get-tuple-element.213), channel_id=1, source_target_pairs={{0,1},{1,0},{2,3},{3,2},{4,5},{5,4},{6,7},{7,6},{8,9},{9,8},{10,11... | collective-permute-start | bytes 7077896 | tf_op jit(solution)/shard_map/ppermute | solution.py:528
  139.5 16.1 %collective-permute-start.27 = (bf16[8,96,768]{2,1,0:T(8,128)(2,1)S(1)}, bf16[8,96,768]{2,1,0:T(8,128)(2,1)S(1)}, u32[]{:S(2)}, u32[]{:S(2)}) collective-permute-start(bf16[8,96,768]{2,1,0:T(8,128)(2,1)S(1)} %copy-done.31), channel_id=1, source_target_pairs={{0,1},{1,0},{2,3},{3,2},{4,5},{5,4},{6,7},{7,6},{8,9},{9,8},{10,11... | collective-permute-start | bytes 3538952 | tf_op jit(solution)/shard_map/ppermute | solution.py:528
  139.9 16.2 %collective-permute-start.28 = (bf16[8,96,768]{2,1,0:T(8,128)(2,1)S(1)}, bf16[8,96,768]{2,1,0:T(8,128)(2,1)S(1)}, u32[]{:S(2)}, u32[]{:S(2)}) collective-permute-start(bf16[8,96,768]{2,1,0:T(8,128)(2,1)S(1)} %add_convert_fusion.1), channel_id=1, source_target_pairs={{0,2},{1,5},{2,0},{3,7},{4,6},{5,1},{6,4},{7,3},{8,10},{9,13},{10,... | collective-permute-start | bytes 3538952 | tf_op jit(solution)/shard_map/ppermute | solution.py:528
  141.6 6.6 %copy-start.5 = (bf16[640,768]{1,0:T(8,128)(2,1)S(1)}, bf16[640,768]{1,0:T(8,128)(2,1)}, u32[]{:S(2)}) copy-start(bf16[640,768]{1,0:T(8,128)(2,1)} %copy-done.4) | copy-start | bytes 2949124
  148.2 5.6 %copy-start.11 = (bf16[16,24,3072]{2,1,0:T(8,128)(2,1)S(1)}, bf16[16,24,3072]{2,1,0:T(8,128)(2,1)}, u32[]{:S(2)}) copy-start(bf16[16,24,3072]{2,1,0:T(8,128)(2,1)} %get-tuple-element.320) | copy-start | bytes 7077892
  153.8 2.3 %collective-permute-start.29 = (bf16[8,24,1920]{2,1,0:T(8,128)(2,1)S(1)}, bf16[8,24,1920]{2,1,0:T(8,128)(2,1)S(1)}, u32[]{:S(2)}, u32[]{:S(2)}) collective-permute-start(bf16[8,24,1920]{2,1,0:T(8,128)(2,1)S(1)} %get-tuple-element.225), channel_id=1, source_target_pairs={{0,1},{1,0},{2,3},{3,2},{4,5},{5,4},{6,7},{7,6},{8,9},{9,8},{10,11... | collective-permute-start | bytes 2211848 | tf_op jit(solution)/shard_map/ppermute | solution.py:528
  154.3 18.0 %collective-permute-start.26 = (bf16[8,24,3072]{2,1,0:T(8,128)(2,1)S(1)}, bf16[8,24,3072]{2,1,0:T(8,128)(2,1)S(1)}, u32[]{:S(2)}, u32[]{:S(2)}) collective-permute-start(bf16[8,24,3072]{2,1,0:T(8,128)(2,1)S(1)} %add_convert_fusion), channel_id=1, source_target_pairs={{0,2},{1,5},{2,0},{3,7},{4,6},{5,1},{6,4},{7,3},{8,10},{9,13},{10,... | collective-permute-start | bytes 3538952 | tf_op jit(solution)/shard_map/ppermute | solution.py:528
  156.3 19.0 %collective-permute-start.31 = (bf16[4,96,768]{2,1,0:T(8,128)(2,1)S(1)}, bf16[4,96,768]{2,1,0:T(8,128)(2,1)S(1)}, u32[]{:S(2)}, u32[]{:S(2)}) collective-permute-start(bf16[4,96,768]{2,1,0:T(8,128)(2,1)S(1)} %add_convert_fusion.5), channel_id=1, source_target_pairs={{0,8},{1,9},{2,10},{3,11},{4,12},{5,13},{6,14},{7,15},{8,0},{9,1},... | collective-permute-start | bytes 1769480 | tf_op jit(solution)/shard_map/ppermute | solution.py:528
  158.0 8.3 %copy-start.2 = (bf16[4,160,768]{2,1,0:T(8,128)(2,1)S(1)}, bf16[4,160,768]{2,1,0:T(8,128)(2,1)}, u32[]{:S(2)}) copy-start(bf16[4,160,768]{2,1,0:T(8,128)(2,1)} %copy-done.1) | copy-start | bytes 2949124
  158.0 20.4 %collective-permute-start.33 = (bf16[8,24,1920]{2,1,0:T(8,128)(2,1)S(1)}, bf16[8,24,1920]{2,1,0:T(8,128)(2,1)S(1)}, u32[]{:S(2)}, u32[]{:S(2)}) collective-permute-start(bf16[8,24,1920]{2,1,0:T(8,128)(2,1)S(1)} %add_convert_fusion.2), channel_id=1, source_target_pairs={{0,2},{1,5},{2,0},{3,7},{4,6},{5,1},{6,4},{7,3},{8,10},{9,13},{10,... | collective-permute-start | bytes 2211848 | tf_op jit(solution)/shard_map/ppermute | solution.py:528
  171.7 12.5 %collective-permute-start.35 = (bf16[8,32,1152]{2,1,0:T(8,128)(2,1)S(1)}, bf16[8,32,1152]{2,1,0:T(8,128)(2,1)S(1)}, u32[]{:S(2)}, u32[]{:S(2)}) collective-permute-start(bf16[8,32,1152]{2,1,0:T(8,128)(2,1)S(1)} %get-tuple-element.261), channel_id=1, source_target_pairs={{0,1},{1,0},{2,3},{3,2},{4,5},{5,4},{6,7},{7,6},{8,9},{9,8},{10,11... | collective-permute-start | bytes 1769480 | tf_op jit(solution)/shard_map/ppermute | solution.py:528
  171.7 2.8 %collective-permute-start.34 = (bf16[8,32,1152]{2,1,0:T(8,128)(2,1)S(1)}, bf16[8,32,1152]{2,1,0:T(8,128)(2,1)S(1)}, u32[]{:S(2)}, u32[]{:S(2)}) collective-permute-start(bf16[8,32,1152]{2,1,0:T(8,128)(2,1)S(1)} %get-tuple-element.246), channel_id=1, source_target_pairs={{0,1},{1,0},{2,3},{3,2},{4,5},{5,4},{6,7},{7,6},{8,9},{9,8},{10,11... | collective-permute-start | bytes 1769480 | tf_op jit(solution)/shard_map/ppermute | solution.py:528
  172.2 3.4 %collective-permute-start.32 = (bf16[8,24,1920]{2,1,0:T(8,128)(2,1)S(1)}, bf16[8,24,1920]{2,1,0:T(8,128)(2,1)S(1)}, u32[]{:S(2)}, u32[]{:S(2)}) collective-permute-start(bf16[8,24,1920]{2,1,0:T(8,128)(2,1)S(1)} %get-tuple-element.243), channel_id=1, source_target_pairs={{0,1},{1,0},{2,3},{3,2},{4,5},{5,4},{6,7},{7,6},{8,9},{9,8},{10,11... | collective-permute-start | bytes 2211848 | tf_op jit(solution)/shard_map/ppermute | solution.py:528
  174.6 15.4 %collective-permute-start.30 = (bf16[4,24,3072]{2,1,0:T(8,128)(2,1)S(1)}, bf16[4,24,3072]{2,1,0:T(8,128)(2,1)S(1)}, u32[]{:S(2)}, u32[]{:S(2)}) collective-permute-start(bf16[4,24,3072]{2,1,0:T(8,128)(2,1)S(1)} %add_convert_fusion.4), channel_id=1, source_target_pairs={{0,8},{1,9},{2,10},{3,11},{4,12},{5,13},{6,14},{7,15},{8,0},{9,1},... | collective-permute-start | bytes 1769480 | tf_op jit(solution)/shard_map/ppermute | solution.py:528
  175.3 11.0 %collective-permute-start.36 = (bf16[8,32,1152]{2,1,0:T(8,128)(2,1)S(1)}, bf16[8,32,1152]{2,1,0:T(8,128)(2,1)S(1)}, u32[]{:S(2)}, u32[]{:S(2)}) collective-permute-start(bf16[8,32,1152]{2,1,0:T(8,128)(2,1)S(1)} %add_convert_fusion.3), channel_id=1, source_target_pairs={{0,2},{1,5},{2,0},{3,7},{4,6},{5,1},{6,4},{7,3},{8,10},{9,13},{10,... | collective-permute-start | bytes 1769480 | tf_op jit(solution)/shard_map/ppermute | solution.py:528
  181.9 10.0 %collective-permute-start.38 = (bf16[2,96,768]{2,1,0:T(8,128)(2,1)S(1)}, bf16[2,96,768]{2,1,0:T(8,128)(2,1)S(1)}, u32[]{:S(2)}, u32[]{:S(2)}) collective-permute-start(bf16[2,96,768]{2,1,0:T(8,128)(2,1)S(1)} %add_convert_fusion.9), channel_id=1, source_target_pairs={{0,4},{1,3},{2,6},{3,1},{4,0},{5,7},{6,2},{7,5},{8,12},{9,11},{10,... | collective-permute-start | bytes 884744 | tf_op jit(solution)/shard_map/ppermute | solution.py:528
  183.6 9.2 %collective-permute-start.37 = (bf16[4,24,1920]{2,1,0:T(8,128)(2,1)S(1)}, bf16[4,24,1920]{2,1,0:T(8,128)(2,1)S(1)}, u32[]{:S(2)}, u32[]{:S(2)}) collective-permute-start(bf16[4,24,1920]{2,1,0:T(8,128)(2,1)S(1)} %add_convert_fusion.6), channel_id=1, source_target_pairs={{0,4},{1,3},{2,6},{3,1},{4,0},{5,7},{6,2},{7,5},{8,12},{9,11},{10,... | collective-permute-start | bytes 1105928 | tf_op jit(solution)/shard_map/ppermute | solution.py:528
  186.4 9.4 %collective-permute-start.41 = (bf16[4,32,1152]{2,1,0:T(8,128)(2,1)S(1)}, bf16[4,32,1152]{2,1,0:T(8,128)(2,1)S(1)}, u32[]{:S(2)}, u32[]{:S(2)}) collective-permute-start(bf16[4,32,1152]{2,1,0:T(8,128)(2,1)S(1)} %add_convert_fusion.8), channel_id=1, source_target_pairs={{0,4},{1,3},{2,6},{3,1},{4,0},{5,7},{6,2},{7,5},{8,12},{9,11},{10,... | collective-permute-start | bytes 884744 | tf_op jit(solution)/shard_map/ppermute | solution.py:528
  190.1 8.9 %collective-permute-start.40 = (bf16[2,24,3072]{2,1,0:T(8,128)(2,1)S(1)}, bf16[2,24,3072]{2,1,0:T(8,128)(2,1)S(1)}, u32[]{:S(2)}, u32[]{:S(2)}) collective-permute-start(bf16[2,24,3072]{2,1,0:T(8,128)(2,1)S(1)} %add_convert_fusion.7), channel_id=1, source_target_pairs={{0,4},{1,3},{2,6},{3,1},{4,0},{5,7},{6,2},{7,5},{8,12},{9,11},{10,... | collective-permute-start | bytes 884744 | tf_op jit(solution)/shard_map/ppermute | solution.py:528
  192.0 15.2 %collective-permute-start.46 = (bf16[1,96,768]{2,1,0:T(8,128)(2,1)S(1)}, bf16[1,96,768]{2,1,0:T(8,128)(2,1)S(1)}, u32[]{:S(2)}, u32[]{:S(2)}) collective-permute-start(bf16[1,96,768]{2,1,0:T(8,128)(2,1)S(1)} %add_convert_fusion.13), channel_id=1, source_target_pairs={{0,16},{1,17},{2,18},{3,19},{4,20},{5,21},{6,22},{7,23},{8,24},{9,... | collective-permute-start | bytes 442376 | tf_op jit(solution)/shard_map/ppermute | solution.py:528
  192.8 9.2 %collective-permute-start.39 = (bf16[2,24,1920]{2,1,0:T(8,128)(2,1)S(1)}, bf16[2,24,1920]{2,1,0:T(8,128)(2,1)S(1)}, u32[]{:S(2)}, u32[]{:S(2)}) collective-permute-start(bf16[2,24,1920]{2,1,0:T(8,128)(2,1)S(1)} %add_convert_fusion.10), channel_id=1, source_target_pairs={{0,8},{1,9},{2,10},{3,11},{4,12},{5,13},{6,14},{7,15},{8,0},{9,1},... | collective-permute-start | bytes 552968 | tf_op jit(solution)/shard_map/ppermute | solution.py:528
  195.9 10.8 %collective-permute-start.43 = (bf16[2,32,1152]{2,1,0:T(8,128)(2,1)S(1)}, bf16[2,32,1152]{2,1,0:T(8,128)(2,1)S(1)}, u32[]{:S(2)}, u32[]{:S(2)}) collective-permute-start(bf16[2,32,1152]{2,1,0:T(8,128)(2,1)S(1)} %add_convert_fusion.12), channel_id=1, source_target_pairs={{0,8},{1,9},{2,10},{3,11},{4,12},{5,13},{6,14},{7,15},{8,0},{9,1},... | collective-permute-start | bytes 442376 | tf_op jit(solution)/shard_map/ppermute | solution.py:528
  199.1 14.4 %collective-permute-start.45 = (bf16[1,24,3072]{2,1,0:T(8,128)(2,1)S(1)}, bf16[1,24,3072]{2,1,0:T(8,128)(2,1)S(1)}, u32[]{:S(2)}, u32[]{:S(2)}) collective-permute-start(bf16[1,24,3072]{2,1,0:T(8,128)(2,1)S(1)} %add_convert_fusion.11), channel_id=1, source_target_pairs={{0,16},{1,17},{2,18},{3,19},{4,20},{5,21},{6,22},{7,23},{8,24},{9,... | collective-permute-start | bytes 442376 | tf_op jit(solution)/shard_map/ppermute | solution.py:528
  202.1 13.1 %collective-permute-start.42 = (bf16[1,24,1920]{2,1,0:T(8,128)(2,1)S(1)}, bf16[1,24,1920]{2,1,0:T(8,128)(2,1)S(1)}, u32[]{:S(2)}, u32[]{:S(2)}) collective-permute-start(bf16[1,24,1920]{2,1,0:T(8,128)(2,1)S(1)} %add_convert_fusion.14), channel_id=1, source_target_pairs={{0,16},{1,17},{2,18},{3,19},{4,20},{5,21},{6,22},{7,23},{8,24},{9,... | collective-permute-start | bytes 276488 | tf_op jit(solution)/shard_map/ppermute | solution.py:528
  206.7 9.2 %collective-permute-start.44 = (bf16[1,32,1152]{2,1,0:T(8,128)(2,1)S(1)}, bf16[1,32,1152]{2,1,0:T(8,128)(2,1)S(1)}, u32[]{:S(2)}, u32[]{:S(2)}) collective-permute-start(bf16[1,32,1152]{2,1,0:T(8,128)(2,1)S(1)} %add_convert_fusion.15), channel_id=1, source_target_pairs={{0,16},{1,17},{2,18},{3,19},{4,20},{5,21},{6,22},{7,23},{8,24},{9,... | collective-permute-start | bytes 221192 | tf_op jit(solution)/shard_map/ppermute | solution.py:528
  (15 other events, 30.4 us)

commit v2 on v1

--- a/solution.py
+++ b/solution.py
@@ -785,7 +785,7 @@
             buffer((2, width, third), BF), buffer((rows, width), BF), buffer((4, 16, BLOCK), F32),
             buffer((32, 16, BLOCK), BF), flag((5,)),
         ],
-        compiler_params=pltpu.CompilerParams(vmem_limit_bytes=30 * MIB),
+        compiler_params=pltpu.CompilerParams(vmem_limit_bytes=18 * MIB),
         cost_estimate=pl.CostEstimate(flops=1, bytes_accessed=1, transcendentals=0),
         name="first",
     )(place, *gathered_a, rows_in, far)

time: 218 us -> 218 us (level)
  no operation moved by 1% of the time
where the time goes in v2:
time: 218 us
  Pallas kernels  76.6 us (35%)
  waiting for transfers between devices  72 us (33%)
  starting transfers between devices  44.8 us (21%)
  local copies, waits for them, and re-layouts  13.4 us (6%)
  other arithmetic  9.2 us (4%)
    ppermute x47, waiting for transfers between devices, move(): return lax.ppermute(value, AXES, pairs)  72 us
    ppermute x47, starting transfers between devices, move(): return lax.ppermute(value, AXES, pairs)  44.8 us
    pallas_call x1, Pallas kernels, shards(): pl.pallas_call(mlp_kernel, grid_spec=pltpu.PrefetchScalarGridSpec(num_sca...  34.2 us
    pallas_call x1, Pallas kernels, shards(): pl.pallas_call(first_kernel, out_shape=(struct((2, 16, BLOCK), F32), stru...  13.4 us
    pallas_call x2, Pallas kernels, call(): pl.pallas_call(kernel, grid=grid, out_shape=out_shape, in_specs=in_specs,...  13 us
    pallas_call x2, Pallas kernels, grad_call(): pl.pallas_call(kernel, out_shape=out_shape, in_specs=[smem] + [vmem] * (l...  10.8 us
    unnamed x76, local copies, waits for them, and re-layouts  6.85 us
  transfers between devices with their start and end apart: 47, of which 24 were waited for; matrix products, arithmetic and copies ran while one was open for 7% of the time, Pallas kernels for 17%

profile of v2, /device:TPU:0, one launch (start us, length us, event | category | flops | bytes accessed | tf_op | source)
XLA Modules:
  0.0 217.5 jit_solution(11446548888112241154)
XLA Ops:
  1.4 1.8 share.1
  3.7 1.2 collective-permute-done.got_ref
  5.6 1.9 pair.1
  7.4 2.9 %collective-permute-start.3 = (bf16[192,384]{1,0:T(8,128)(2,1)}, bf16[192,384]{1,0:T(8,128)(2,1)S(1)}, u32[]{:S(2)}, u32[]{:S(2)}) collective-permute-start(bf16[192,384]{1,0:T(8,128)(2,1)} %get-tuple-element.174), channel_id=1, source_target_pairs={{0,4},{1,3},{2,6},{3,1},{4,0},{5,7},{6,2},{7,5},{8,12},{9,11},{10,... | collective-permute-start | bytes 442376 | tf_op jit(solution)/shard_map/ppermute | solution.py:528
  10.3 3.6 %collective-permute-start.2 = (bf16[160,384]{1,0:T(8,128)(2,1)}, bf16[160,384]{1,0:T(8,128)(2,1)S(1)}, u32[]{:S(2)}, u32[]{:S(2)}) collective-permute-start(bf16[160,384]{1,0:T(8,128)(2,1)} %get-tuple-element.175), channel_id=1, source_target_pairs={{0,24},{1,25},{2,26},{3,27},{4,28},{5,29},{6,30},{7,31},{8,0},{9,1... | collective-permute-start | bytes 368648 | tf_op jit(solution)/shard_map/ppermute | solution.py:528
  13.9 4.0 %collective-permute-done.2 = bf16[160,384]{1,0:T(8,128)(2,1)S(1)} collective-permute-done((bf16[160,384]{1,0:T(8,128)(2,1)}, bf16[160,384]{1,0:T(8,128)(2,1)S(1)}, u32[]{:S(2)}, u32[]{:S(2)}) %collective-permute-start.2) | collective-permute-done | bytes 122912 | tf_op jit(solution)/shard_map/ppermute | solution.py:528
  17.9 2.8 %collective-permute-done.1 = bf16[160,384]{1,0:T(8,128)(2,1)S(1)} collective-permute-done((bf16[160,384]{1,0:T(8,128)(2,1)}, bf16[160,384]{1,0:T(8,128)(2,1)S(1)}, u32[]{:S(2)}, u32[]{:S(2)}) %collective-permute-start.1) | collective-permute-done | bytes 122912 | tf_op jit(solution)/shard_map/ppermute | solution.py:528
  20.8 1.0 pad_maximum_fusion.4
  21.8 1.6 collective-permute-start.5
  23.4 0.9 constant_dynamic-update-slice_fusion.4
  24.4 6.6 %collective-permute-done.4 = bf16[160,384]{1,0:T(8,128)(2,1)S(1)} collective-permute-done((bf16[160,384]{1,0:T(8,128)(2,1)S(1)}, bf16[160,384]{1,0:T(8,128)(2,1)S(1)}, u32[]{:S(2)}, u32[]{:S(2)}) %collective-permute-start.4) | collective-permute-done | bytes 122912 | tf_op jit(solution)/shard_map/ppermute | solution.py:528
  31.0 2.0 collective-permute-start.7
  33.1 1.0 pad_maximum_fusion.3
  34.8 0.8 constant_dynamic-update-slice_fusion.17
  35.6 5.1 %collective-permute-done.8 = bf16[240,384]{1,0:T(8,128)(2,1)S(1)} collective-permute-done((bf16[240,384]{1,0:T(8,128)(2,1)}, bf16[240,384]{1,0:T(8,128)(2,1)S(1)}, u32[]{:S(2)}, u32[]{:S(2)}) %collective-permute-start.8) | collective-permute-done | bytes 184352 | tf_op jit(solution)/shard_map/ppermute | solution.py:528
  40.7 2.3 %collective-permute-done.6 = bf16[4,160,384]{2,1,0:T(8,128)(2,1)} collective-permute-done((bf16[4,160,384]{2,1,0:T(8,128)(2,1)S(1)}, bf16[4,160,384]{2,1,0:T(8,128)(2,1)}, u32[]{:S(2)}, u32[]{:S(2)}) %collective-permute-start.6) | collective-permute-done | bytes 491552 | tf_op jit(solution)/shard_map/ppermute | solution.py:528
  43.3 1.1 constant_dynamic-update-slice_fusion.own0
  44.5 1.6 collective-permute-start.9
  46.1 2.7 %collective-permute-start.12 = (bf16[3,240,384]{2,1,0:T(8,128)(2,1)S(1)}, bf16[3,240,384]{2,1,0:T(8,128)(2,1)S(1)}, u32[]{:S(2)}, u32[]{:S(2)}) collective-permute-start(bf16[3,240,384]{2,1,0:T(8,128)(2,1)S(1)} %pad_maximum_fusion.2), channel_id=1, source_target_pairs={{0,4},{1,3},{2,6},{3,1},{4,0},{5,7},{6,2},{7,5},{8,12},{9,11},{10,... | collective-permute-start | bytes 1658888 | tf_op jit(solution)/shard_map/ppermute | solution.py:528
  49.5 1.1 copy.32
  53.4 7.8 %collective-permute-done.12 = bf16[3,240,384]{2,1,0:T(8,128)(2,1)S(1)} collective-permute-done((bf16[3,240,384]{2,1,0:T(8,128)(2,1)S(1)}, bf16[3,240,384]{2,1,0:T(8,128)(2,1)S(1)}, u32[]{:S(2)}, u32[]{:S(2)}) %collective-permute-start.12) | collective-permute-done | bytes 552992 | tf_op jit(solution)/shard_map/ppermute | solution.py:528
  61.6 1.7 collective-permute-start.15
  63.9 1.5 collective-permute-start.14
  65.9 1.7 collective-permute-start.17
  67.7 1.2 collective-permute-start.16
  68.9 13.4 %first.1 = (f32[2,16,384]{2,1,0:T(8,128)S(1)}, f32[4,1,768]{2,1,0:T(1,128)S(1)}, bf16[768,640]{1,0:T(8,128)(2,1)S(1)}, bf16[2,640,1152]{2,1,0:T(8,128)(2,1)S(1)}...) custom-call(s32[176]{0:T(256)S(1)} %copy-done.6, ...), custom_call_target="tpu_custom_call" | custom-call | flops 1 | bytes 1 | tf_op jit(solution)/shard_map/first/pallas_call | solution.py:776
  82.5 9.3 %collective-permute-done.13 = bf16[4,192,384]{2,1,0:T(8,128)(2,1)S(1)} collective-permute-done((bf16[4,192,384]{2,1,0:T(8,128)(2,1)S(1)}, bf16[4,192,384]{2,1,0:T(8,128)(2,1)S(1)}, u32[]{:S(2)}, u32[]{:S(2)}) %collective-permute-start.13) | collective-permute-done | bytes 589856 | tf_op jit(solution)/shard_map/ppermute | solution.py:528
  93.3 3.7 %collective-permute-done.20.a2 = bf16[8,192,384]{2,1,0:T(8,128)(2,1)S(1)} collective-permute-done((bf16[8,192,384]{2,1,0:T(8,128)(2,1)S(1)}, bf16[8,192,384]{2,1,0:T(8,128)(2,1)S(1)}, u32[]{:S(2)}, u32[]{:S(2)}) %collective-permute-start.20) | collective-permute-done | bytes 1179680 | tf_op jit(solution)/shard_map/ppermute | solution.py:528
  97.0 1.7 collective-permute-done.21.a3
  98.8 1.0 copy-done.22
  100.2 34.2 %mlp.1 = (bf16[640,768]{1,0:T(8,128)(2,1)S(1)}, bf16[640,768]{1,0:T(8,128)(2,1)}, bf16[16,24,3072]{2,1,0:T(8,128)(2,1)}, bf16[16,24,3072]{2,1,0:T(8,128)(2,1)}, ...) custom-call(s32[176]{0:T(256)S(1)} %copy-done.6, ...), custom_call_target="tpu_custom_call" | custom-call | flops 1 | bytes 1 | tf_op jit(solution)/shard_map/mlp/pallas_call | solution.py:801
  134.6 2.9 %collective-permute-done.24 = bf16[8,96,768]{2,1,0:T(8,128)(2,1)S(1)} collective-permute-done((bf16[8,96,768]{2,1,0:T(8,128)(2,1)}, bf16[8,96,768]{2,1,0:T(8,128)(2,1)S(1)}, u32[]{:S(2)}, u32[]{:S(2)}) %collective-permute-start.24) | collective-permute-done | bytes 1179680 | tf_op jit(solution)/shard_map/ppermute | solution.py:528
  137.6 1.7 add_convert_fusion.1
  139.9 1.7 collective-permute-start.28
  141.6 6.5 %attention_back.2.gqkv_ref = bf16[640,1152]{1,0:T(8,128)(2,1)S(1)} custom-call(bf16[2,768,384]{2,1,0:T(8,128)(2,1)S(1)} %copy-done.3, bf16[2,640,1152]{2,1,0:T(8,128)(2,1)S(1)} %get-tuple-element.215.refs_1_, f32[4,160,160]{2,1,0:T(8,128)S(1)} %get-tuple-element.216.refs_2_, bf16[640,768]{1,0:T(8,128)(2,1)S(1)} %copy-done), custom_call_target="tpu_custom_call" | custom-call | flops 1 | bytes 1 | tf_op jit(solution)/shard_map/attention_back/pallas_call | solution.py:748
  148.2 5.5 %qkv_grad.1 = (f32[640,768]{1,0:T(8,128)S(1)}, f32[1,1152]{1,0:T(1,128)S(1)}, bf16[16,24,1920]{2,1,0:T(8,128)(2,1)S(1)}, bf16[8,24,1920]{2,1,0:T(8,128)(2,1)S(1)}, bf16[8,24,1920]{2,1,0:T(8,128)(2,1)S(1)}) custom-call(s32[176]{0:T(256)S(1)} %copy-done.6, bf16[768,640]{1,0:T(8,128)(2,1)S(1)} %get-tuple-element.221.h1_turned, ...), custom_call_target="tpu_custom_call" | custom-call | flops 1 | bytes 1 | tf_op jit(solution)/shard_map/qkv_grad/pallas_call | solution.py:861
  154.3 1.3 collective-permute-start.26
  156.3 1.5 collective-permute-start.31
  158.0 1.8 collective-permute-start.33
  159.8 6.5 %attention_back.3.gqkv_ref = bf16[640,1152]{1,0:T(8,128)(2,1)S(1)} custom-call(bf16[2,768,384]{2,1,0:T(8,128)(2,1)S(1)} %copy-done.3, bf16[2,640,1152]{2,1,0:T(8,128)(2,1)S(1)} %get-tuple-element.215.refs_1_, f32[4,160,160]{2,1,0:T(8,128)S(1)} %get-tuple-element.216.refs_2_, bf16[640,768]{1,0:T(8,128)(2,1)S(1)} %copy-done), custom_call_target="tpu_custom_call" | custom-call | flops 1 | bytes 1 | tf_op jit(solution)/shard_map/attention_back/pallas_call | solution.py:748
  166.4 5.3 %input_grad.1 = (bf16[640,768]{1,0:T(8,128)(2,1)S(1)}, bf16[16,32,1152]{2,1,0:T(8,128)(2,1)S(1)}, bf16[8,32,1152]{2,1,0:T(8,128)(2,1)S(1)}, bf16[8,32,1152]{2,1,0:T(8,128)(2,1)S(1)}) custom-call(s32[176]{0:T(256)S(1)} %copy-done.6, bf16[768,640]{1,0:T(8,128)(2,1)S(1)} %get-tuple-element.221.h1_turned, bf16[640,1152]{1,0:T(8,128)(2,1)S(1)} %attention_back.3.gqkv_ref, ...), custom_call_target="tpu_custom_call" | custom-call | flops 1 | bytes 1 | tf_op jit(solution)/shard_map/input_grad/pallas_call | solution.py:861
  172.5 2.0 collective-permute-done.34
  175.7 2.8 %collective-permute-done.33.refs_2_ = bf16[8,24,1920]{2,1,0:T(8,128)(2,1)S(1)} collective-permute-done((bf16[8,24,1920]{2,1,0:T(8,128)(2,1)S(1)}, bf16[8,24,1920]{2,1,0:T(8,128)(2,1)S(1)}, u32[]{:S(2)}, u32[]{:S(2)}) %collective-permute-start.33) | collective-permute-done | bytes 737312 | tf_op jit(solution)/shard_map/ppermute | solution.py:528
  178.4 1.7 copy.35
  180.1 1.7 copy.36
  181.9 1.5 collective-permute-start.38
  184.2 2.1 collective-permute-done.36.refs_8_
  186.4 1.5 collective-permute-start.41
  187.9 2.0 collective-permute-done.30
  190.1 1.8 collective-permute-start.40
  192.8 1.6 collective-permute-start.39
  194.5 1.3 collective-permute-done.41.refs_9_
  195.9 1.7 collective-permute-start.43
  197.6 1.4 collective-permute-done.40
  199.1 1.3 collective-permute-start.45
  200.4 1.6 collective-permute-done.39.refs_4_
  202.1 1.2 collective-permute-start.42
  203.2 3.4 %collective-permute-done.43.refs_10_ = bf16[2,32,1152]{2,1,0:T(8,128)(2,1)S(1)} collective-permute-done((bf16[2,32,1152]{2,1,0:T(8,128)(2,1)S(1)}, bf16[2,32,1152]{2,1,0:T(8,128)(2,1)S(1)}, u32[]{:S(2)}, u32[]{:S(2)}) %collective-permute-start.43) | collective-permute-done | bytes 147488 | tf_op jit(solution)/shard_map/ppermute | solution.py:528
  207.2 0.8 add_bitcast_fusion.1
  208.0 5.4 %collective-permute-done.45 = bf16[1,24,3072]{2,1,0:T(8,128)(2,1)S(1)} collective-permute-done((bf16[1,24,3072]{2,1,0:T(8,128)(2,1)S(1)}, bf16[1,24,3072]{2,1,0:T(8,128)(2,1)S(1)}, u32[]{:S(2)}, u32[]{:S(2)}) %collective-permute-start.45) | collective-permute-done | bytes 147488 | tf_op jit(solution)/shard_map/ppermute | solution.py:528
  213.4 0.8 add_bitcast_fusion
  214.3 0.9 collective-permute-done.42.refs_5_
  215.1 0.8 collective-permute-done.44.refs_11_
  215.9 1.4 last.1
  (157 shorter events, 17.1 us)
Async XLA Ops:
  3.2 1.7 collective-permute-start
  7.4 27.2 %copy-start.17 = (bf16[192,384]{1,0:T(8,128)(2,1)S(1)}, bf16[192,384]{1,0:T(8,128)(2,1)}, u32[]{:S(2)}) copy-start(bf16[192,384]{1,0:T(8,128)(2,1)} %get-tuple-element.174) | copy-start | bytes 442372
  7.4 13.3 %collective-permute-start.3 = (bf16[192,384]{1,0:T(8,128)(2,1)}, bf16[192,384]{1,0:T(8,128)(2,1)S(1)}, u32[]{:S(2)}, u32[]{:S(2)}) collective-permute-start(bf16[192,384]{1,0:T(8,128)(2,1)} %get-tuple-element.174), channel_id=1, source_target_pairs={{0,4},{1,3},{2,6},{3,1},{4,0},{5,7},{6,2},{7,5},{8,12},{9,11},{10,... | collective-permute-start | bytes 442376 | tf_op jit(solution)/shard_map/ppermute | solution.py:528
  10.3 7.6 %collective-permute-start.2 = (bf16[160,384]{1,0:T(8,128)(2,1)}, bf16[160,384]{1,0:T(8,128)(2,1)S(1)}, u32[]{:S(2)}, u32[]{:S(2)}) collective-permute-start(bf16[160,384]{1,0:T(8,128)(2,1)} %get-tuple-element.175), channel_id=1, source_target_pairs={{0,24},{1,25},{2,26},{3,27},{4,28},{5,29},{6,30},{7,31},{8,0},{9,1... | collective-permute-start | bytes 368648 | tf_op jit(solution)/shard_map/ppermute | solution.py:528
  13.9 6.9 %collective-permute-start.1 = (bf16[160,384]{1,0:T(8,128)(2,1)}, bf16[160,384]{1,0:T(8,128)(2,1)S(1)}, u32[]{:S(2)}, u32[]{:S(2)}) collective-permute-start(bf16[160,384]{1,0:T(8,128)(2,1)} %get-tuple-element.175), channel_id=1, source_target_pairs={{0,8},{1,9},{2,10},{3,11},{4,12},{5,13},{6,14},{7,15},{8,16},{9,17... | collective-permute-start | bytes 368648 | tf_op jit(solution)/shard_map/ppermute | solution.py:528
  20.8 14.0 %copy-start.19 = (bf16[192,384]{1,0:T(8,128)(2,1)}, bf16[192,384]{1,0:T(8,128)(2,1)S(1)}, u32[]{:S(2)}) copy-start(bf16[192,384]{1,0:T(8,128)(2,1)S(1)} %collective-permute-done.3) | copy-start | bytes 442372
  21.8 9.2 %collective-permute-start.5 = (bf16[2,192,384]{2,1,0:T(8,128)(2,1)S(1)}, bf16[2,192,384]{2,1,0:T(8,128)(2,1)S(1)}, u32[]{:S(2)}, u32[]{:S(2)}) collective-permute-start(bf16[2,192,384]{2,1,0:T(8,128)(2,1)S(1)} %pad_maximum_fusion.4), channel_id=1, source_target_pairs={{0,2},{1,5},{2,0},{3,7},{4,6},{5,1},{6,4},{7,3},{8,10},{9,13},{10,... | collective-permute-start | bytes 884744 | tf_op jit(solution)/shard_map/ppermute | solution.py:528
  24.3 10.5 %copy-start.27 = (bf16[240,384]{1,0:T(8,128)(2,1)S(1)}, bf16[240,384]{1,0:T(8,128)(2,1)}, u32[]{:S(2)}) copy-start(bf16[240,384]{1,0:T(8,128)(2,1)} %get-tuple-element.182) | copy-start | bytes 552964
  24.3 6.7 %collective-permute-start.4 = (bf16[160,384]{1,0:T(8,128)(2,1)S(1)}, bf16[160,384]{1,0:T(8,128)(2,1)S(1)}, u32[]{:S(2)}, u32[]{:S(2)}) collective-permute-start(bf16[160,384]{1,0:T(8,128)(2,1)S(1)} %collective-permute-done.1), channel_id=1, source_target_pairs={{0,8},{1,9},{2,10},{3,11},{4,12},{5,13},{6,14},{7,15},{8,16},{9,17... | collective-permute-start | bytes 368648 | tf_op jit(solution)/shard_map/ppermute | solution.py:528
  31.0 9.7 %collective-permute-start.8 = (bf16[240,384]{1,0:T(8,128)(2,1)}, bf16[240,384]{1,0:T(8,128)(2,1)S(1)}, u32[]{:S(2)}, u32[]{:S(2)}) collective-permute-start(bf16[240,384]{1,0:T(8,128)(2,1)} %get-tuple-element.182), channel_id=1, source_target_pairs={{0,24},{1,25},{2,26},{3,27},{4,28},{5,29},{6,30},{7,31},{8,0},{9,1... | collective-permute-start | bytes 552968 | tf_op jit(solution)/shard_map/ppermute | solution.py:528
  31.0 9.7 %collective-permute-start.7 = (bf16[240,384]{1,0:T(8,128)(2,1)}, bf16[240,384]{1,0:T(8,128)(2,1)S(1)}, u32[]{:S(2)}, u32[]{:S(2)}) collective-permute-start(bf16[240,384]{1,0:T(8,128)(2,1)} %get-tuple-element.182), channel_id=1, source_target_pairs={{0,8},{1,9},{2,10},{3,11},{4,12},{5,13},{6,14},{7,15},{8,16},{9,17... | collective-permute-start | bytes 552968 | tf_op jit(solution)/shard_map/ppermute | solution.py:528
  34.0 9.0 %copy-start.7 = (s32[4]{0:T(128)S(1)}, s32[4]{0:T(128)}, u32[]{:S(2)}) copy-start(s32[4]{0:T(128)} %counts.1) | copy-start | bytes 52
  34.1 9.0 %collective-permute-start.6 = (bf16[4,160,384]{2,1,0:T(8,128)(2,1)S(1)}, bf16[4,160,384]{2,1,0:T(8,128)(2,1)}, u32[]{:S(2)}, u32[]{:S(2)}) collective-permute-start(bf16[4,160,384]{2,1,0:T(8,128)(2,1)S(1)} %pad_maximum_fusion.3), channel_id=1, source_target_pairs={{0,4},{1,3},{2,6},{3,1},{4,0},{5,7},{6,2},{7,5},{8,12},{9,11},{10,... | collective-permute-start | bytes 1474568 | tf_op jit(solution)/shard_map/ppermute | solution.py:528
  35.6 13.2 %copy-start.25 = (bf16[4,153,768]{2,0,1:T(4,128)(2,1)S(1)}, bf16[4,153,768]{2,0,1:T(4,128)(2,1)}, u32[]{:S(2)}) copy-start(bf16[4,153,768]{2,0,1:T(4,128)(2,1)} %param.31) | copy-start | bytes 2820100
  43.3 10.1 %collective-permute-start.10 = (bf16[240,384]{1,0:T(8,128)(2,1)S(1)}, bf16[240,384]{1,0:T(8,128)(2,1)S(1)}, u32[]{:S(2)}, u32[]{:S(2)}) collective-permute-start(bf16[240,384]{1,0:T(8,128)(2,1)S(1)} %collective-permute-done.7), channel_id=1, source_target_pairs={{0,8},{1,9},{2,10},{3,11},{4,12},{5,13},{6,14},{7,15},{8,16},{9,17... | collective-permute-start | bytes 552968 | tf_op jit(solution)/shard_map/ppermute | solution.py:528
  44.5 16.8 %collective-permute-start.9 = (bf16[8,160,384]{2,1,0:T(8,128)(2,1)S(1)}, bf16[8,160,384]{2,1,0:T(8,128)(2,1)S(1)}, u32[]{:S(2)}, u32[]{:S(2)}) collective-permute-start(bf16[8,160,384]{2,1,0:T(8,128)(2,1)S(1)} %constant_dynamic-update-slice_fusion.own0), channel_id=1, source_target_pairs={{0,2},{1,5},{2,0},{3,7},{4,6},{5,1},{6,4},{7,3},{8,10},{9,13},{10,... | collective-permute-start | bytes 2949128 | tf_op jit(solution)/shard_map/ppermute | solution.py:528
  46.1 15.0 %collective-permute-start.12 = (bf16[3,240,384]{2,1,0:T(8,128)(2,1)S(1)}, bf16[3,240,384]{2,1,0:T(8,128)(2,1)S(1)}, u32[]{:S(2)}, u32[]{:S(2)}) collective-permute-start(bf16[3,240,384]{2,1,0:T(8,128)(2,1)S(1)} %pad_maximum_fusion.2), channel_id=1, source_target_pairs={{0,4},{1,3},{2,6},{3,1},{4,0},{5,7},{6,2},{7,5},{8,12},{9,11},{10,... | collective-permute-start | bytes 1658888 | tf_op jit(solution)/shard_map/ppermute | solution.py:528
  48.8 12.5 %collective-permute-start.11 = (bf16[4,192,384]{2,1,0:T(8,128)(2,1)S(1)}, bf16[4,192,384]{2,1,0:T(8,128)(2,1)S(1)}, u32[]{:S(2)}, u32[]{:S(2)}) collective-permute-start(bf16[4,192,384]{2,1,0:T(8,128)(2,1)S(1)} %pad_maximum_fusion.1), channel_id=1, source_target_pairs={{0,8},{1,9},{2,10},{3,11},{4,12},{5,13},{6,14},{7,15},{8,16},{9,17... | collective-permute-start | bytes 1769480 | tf_op jit(solution)/shard_map/ppermute | solution.py:528
  51.8 17.1 %copy-start.1 = (bf16[4,160,768]{2,1,0:T(8,128)(2,1)}, bf16[4,160,768]{2,1,0:T(8,128)(2,1)S(1)}, u32[]{:S(2)}) copy-start(bf16[4,160,768]{2,1,0:T(8,128)(2,1)S(1)} %pad.11.clone) | copy-start | bytes 2949124
  61.3 7.6 %copy-start.6 = (s32[176]{0:T(256)S(1)}, s32[176]{0:T(256)}, u32[]{:S(2)}) copy-start(s32[176]{0:T(256)} %concatenate.28.place) | copy-start | bytes 2116
  61.6 30.2 %collective-permute-start.15 = (bf16[7,240,384]{2,1,0:T(8,128)(2,1)S(1)}, bf16[7,240,384]{2,1,0:T(8,128)(2,1)S(1)}, u32[]{:S(2)}, u32[]{:S(2)}) collective-permute-start(bf16[7,240,384]{2,1,0:T(8,128)(2,1)S(1)} %get-tuple-element.329), channel_id=1, source_target_pairs={{0,2},{1,5},{2,0},{3,7},{4,6},{5,1},{6,4},{7,3},{8,10},{9,13},{10,... | collective-permute-start | bytes 3870728 | tf_op jit(solution)/shard_map/ppermute | solution.py:528
  63.4 2.6 %collective-permute-start.18 = (bf16[8,160,384]{2,1,0:T(8,128)(2,1)S(1)}, bf16[8,160,384]{2,1,0:T(8,128)(2,1)S(1)}, u32[]{:S(2)}, u32[]{:S(2)}) collective-permute-start(bf16[8,160,384]{2,1,0:T(8,128)(2,1)S(1)} %constant_dynamic-update-slice_fusion.own0), channel_id=1, source_target_pairs={{0,1},{1,0},{2,3},{3,2},{4,5},{5,4},{6,7},{7,6},{8,9},{9,8},{10,11... | collective-permute-start | bytes 2949128 | tf_op jit(solution)/shard_map/ppermute | solution.py:528
  63.4 4.3 %collective-permute-start.19 = (bf16[8,160,384]{2,1,0:T(8,128)(2,1)S(1)}, bf16[8,160,384]{2,1,0:T(8,128)(2,1)S(1)}, u32[]{:S(2)}, u32[]{:S(2)}) collective-permute-start(bf16[8,160,384]{2,1,0:T(8,128)(2,1)S(1)} %collective-permute-done.9.own1), channel_id=1, source_target_pairs={{0,1},{1,0},{2,3},{3,2},{4,5},{5,4},{6,7},{7,6},{8,9},{9,8},{10,11... | collective-permute-start | bytes 2949128 | tf_op jit(solution)/shard_map/ppermute | solution.py:528
  63.9 18.6 %collective-permute-start.14 = (bf16[4,192,384]{2,1,0:T(8,128)(2,1)S(1)}, bf16[4,192,384]{2,1,0:T(8,128)(2,1)S(1)}, u32[]{:S(2)}, u32[]{:S(2)}) collective-permute-start(bf16[4,192,384]{2,1,0:T(8,128)(2,1)S(1)} %pad_maximum_fusion.1), channel_id=1, source_target_pairs={{0,24},{1,25},{2,26},{3,27},{4,28},{5,29},{6,30},{7,31},{8,0},{9,1... | collective-permute-start | bytes 1769480 | tf_op jit(solution)/shard_map/ppermute | solution.py:528
  65.3 26.5 %collective-permute-start.13 = (bf16[4,192,384]{2,1,0:T(8,128)(2,1)S(1)}, bf16[4,192,384]{2,1,0:T(8,128)(2,1)S(1)}, u32[]{:S(2)}, u32[]{:S(2)}) collective-permute-start(bf16[4,192,384]{2,1,0:T(8,128)(2,1)S(1)} %collective-permute-done.11), channel_id=1, source_target_pairs={{0,8},{1,9},{2,10},{3,11},{4,12},{5,13},{6,14},{7,15},{8,16},{9,17... | collective-permute-start | bytes 1769480 | tf_op jit(solution)/shard_map/ppermute | solution.py:528
  65.9 16.3 %collective-permute-start.17 = (bf16[1,240,384]{2,1,0:T(8,128)(2,1)S(1)}, bf16[1,240,384]{2,1,0:T(8,128)(2,1)S(1)}, u32[]{:S(2)}, u32[]{:S(2)}) collective-permute-start(bf16[1,240,384]{2,1,0:T(8,128)(2,1)S(1)} %bitcast.54), channel_id=1, source_target_pairs={{0,4},{1,3},{2,6},{3,1},{4,0},{5,7},{6,2},{7,5},{8,12},{9,11},{10,... | collective-permute-start | bytes 552968 | tf_op jit(solution)/shard_map/ppermute | solution.py:528
  67.7 14.8 %collective-permute-start.16 = (bf16[1,240,384]{2,1,0:T(8,128)(2,1)S(1)}, bf16[1,240,384]{2,1,0:T(8,128)(2,1)S(1)}, u32[]{:S(2)}, u32[]{:S(2)}) collective-permute-start(bf16[1,240,384]{2,1,0:T(8,128)(2,1)S(1)} %bitcast.55), channel_id=1, source_target_pairs={{0,6},{1,7},{2,4},{3,5},{4,2},{5,3},{6,0},{7,1},{8,14},{9,15},{10,... | collective-permute-start | bytes 552968 | tf_op jit(solution)/shard_map/ppermute | solution.py:528
  82.3 9.7 %copy-start.4 = (bf16[640,768]{1,0:T(8,128)(2,1)}, bf16[640,768]{1,0:T(8,128)(2,1)S(1)}, u32[]{:S(2)}) copy-start(bf16[640,768]{1,0:T(8,128)(2,1)S(1)} %get-tuple-element.204.att_far.att_ref) | copy-start | bytes 2949124
  82.3 9.7 %copy-start.14 = (bf16[8,240,384]{2,1,0:T(8,128)(2,1)}, bf16[8,240,384]{2,1,0:T(8,128)(2,1)S(1)}, u32[]{:S(2)}) copy-start(bf16[8,240,384]{2,1,0:T(8,128)(2,1)S(1)} %constant_dynamic-update-slice_fusion.12.b0) | copy-start | bytes 4423684
  82.3 9.8 %copy-start.18 = (bf16[192,384]{1,0:T(8,128)(2,1)S(1)}, bf16[192,384]{1,0:T(8,128)(2,1)}, u32[]{:S(2)}) copy-start(bf16[192,384]{1,0:T(8,128)(2,1)} %get-tuple-element.174) | copy-start | bytes 442372
  82.3 9.8 %copy-start.20 = (bf16[192,384]{1,0:T(8,128)(2,1)S(1)}, bf16[192,384]{1,0:T(8,128)(2,1)}, u32[]{:S(2)}) copy-start(bf16[192,384]{1,0:T(8,128)(2,1)} %copy-done.19) | copy-start | bytes 442372
  82.4 9.8 %copy-start.24 = (bf16[2,192,384]{2,1,0:T(8,128)(2,1)S(1)}, bf16[2,192,384]{2,1,0:T(8,128)(2,1)}, u32[]{:S(2)}) copy-start(bf16[2,192,384]{2,1,0:T(8,128)(2,1)} %copy-done.23) | copy-start | bytes 884740
  82.4 14.7 %collective-permute-start.22 = (bf16[8,240,384]{2,1,0:T(8,128)(2,1)S(1)}, bf16[8,240,384]{2,1,0:T(8,128)(2,1)S(1)}, u32[]{:S(2)}, u32[]{:S(2)}) collective-permute-start(bf16[8,240,384]{2,1,0:T(8,128)(2,1)S(1)} %constant_dynamic-update-slice_fusion.12.b0), channel_id=1, source_target_pairs={{0,1},{1,0},{2,3},{3,2},{4,5},{5,4},{6,7},{7,6},{8,9},{9,8},{10,11... | collective-permute-start | bytes 4423688 | tf_op jit(solution)/shard_map/ppermute | solution.py:528
  92.0 6.7 %collective-permute-start.23 = (bf16[8,240,384]{2,1,0:T(8,128)(2,1)S(1)}, bf16[8,240,384]{2,1,0:T(8,128)(2,1)S(1)}, u32[]{:S(2)}, u32[]{:S(2)}) collective-permute-start(bf16[8,240,384]{2,1,0:T(8,128)(2,1)S(1)} %constant_dynamic-update-slice_fusion.18.b1), channel_id=1, source_target_pairs={{0,1},{1,0},{2,3},{3,2},{4,5},{5,4},{6,7},{7,6},{8,9},{9,8},{10,11... | collective-permute-start | bytes 4423688 | tf_op jit(solution)/shard_map/ppermute | solution.py:528
  92.3 7.9 %copy-start.9 = (bf16[8,192,384]{2,1,0:T(8,128)(2,1)}, bf16[8,192,384]{2,1,0:T(8,128)(2,1)S(1)}, u32[]{:S(2)}) copy-start(bf16[8,192,384]{2,1,0:T(8,128)(2,1)S(1)} %pad_maximum_fusion.a0) | copy-start | bytes 3538948
  92.3 4.7 %collective-permute-start.20 = (bf16[8,192,384]{2,1,0:T(8,128)(2,1)S(1)}, bf16[8,192,384]{2,1,0:T(8,128)(2,1)S(1)}, u32[]{:S(2)}, u32[]{:S(2)}) collective-permute-start(bf16[8,192,384]{2,1,0:T(8,128)(2,1)S(1)} %pad_maximum_fusion.a0), channel_id=1, source_target_pairs={{0,1},{1,0},{2,3},{3,2},{4,5},{5,4},{6,7},{7,6},{8,9},{9,8},{10,11... | collective-permute-start | bytes 3538952 | tf_op jit(solution)/shard_map/ppermute | solution.py:528
  93.2 5.5 %copy-start.10 = (bf16[8,192,384]{2,1,0:T(8,128)(2,1)}, bf16[8,192,384]{2,1,0:T(8,128)(2,1)S(1)}, u32[]{:S(2)}) copy-start(bf16[8,192,384]{2,1,0:T(8,128)(2,1)S(1)} %constant_dynamic-update-slice_fusion.10.a1) | copy-start | bytes 3538948
  93.2 5.5 %collective-permute-start.21 = (bf16[8,192,384]{2,1,0:T(8,128)(2,1)S(1)}, bf16[8,192,384]{2,1,0:T(8,128)(2,1)S(1)}, u32[]{:S(2)}, u32[]{:S(2)}) collective-permute-start(bf16[8,192,384]{2,1,0:T(8,128)(2,1)S(1)} %constant_dynamic-update-slice_fusion.10.a1), channel_id=1, source_target_pairs={{0,1},{1,0},{2,3},{3,2},{4,5},{5,4},{6,7},{7,6},{8,9},{9,8},{10,11... | collective-permute-start | bytes 3538952 | tf_op jit(solution)/shard_map/ppermute | solution.py:528
  134.4 3.1 %collective-permute-start.24 = (bf16[8,96,768]{2,1,0:T(8,128)(2,1)}, bf16[8,96,768]{2,1,0:T(8,128)(2,1)S(1)}, u32[]{:S(2)}, u32[]{:S(2)}) collective-permute-start(bf16[8,96,768]{2,1,0:T(8,128)(2,1)} %get-tuple-element.212), channel_id=1, source_target_pairs={{0,1},{1,0},{2,3},{3,2},{4,5},{5,4},{6,7},{7,6},{8,9},{9,8},{10,11... | collective-permute-start | bytes 3538952 | tf_op jit(solution)/shard_map/ppermute | solution.py:528
  139.3 8.9 %collective-permute-start.25 = (bf16[16,24,3072]{2,1,0:T(8,128)(2,1)}, bf16[16,24,3072]{2,1,0:T(8,128)(2,1)S(1)}, u32[]{:S(2)}, u32[]{:S(2)}) collective-permute-start(bf16[16,24,3072]{2,1,0:T(8,128)(2,1)} %get-tuple-element.213), channel_id=1, source_target_pairs={{0,1},{1,0},{2,3},{3,2},{4,5},{5,4},{6,7},{7,6},{8,9},{9,8},{10,11... | collective-permute-start | bytes 7077896 | tf_op jit(solution)/shard_map/ppermute | solution.py:528
  139.5 16.1 %collective-permute-start.27 = (bf16[8,96,768]{2,1,0:T(8,128)(2,1)S(1)}, bf16[8,96,768]{2,1,0:T(8,128)(2,1)S(1)}, u32[]{:S(2)}, u32[]{:S(2)}) collective-permute-start(bf16[8,96,768]{2,1,0:T(8,128)(2,1)S(1)} %copy-done.31), channel_id=1, source_target_pairs={{0,1},{1,0},{2,3},{3,2},{4,5},{5,4},{6,7},{7,6},{8,9},{9,8},{10,11... | collective-permute-start | bytes 3538952 | tf_op jit(solution)/shard_map/ppermute | solution.py:528
  139.9 16.2 %collective-permute-start.28 = (bf16[8,96,768]{2,1,0:T(8,128)(2,1)S(1)}, bf16[8,96,768]{2,1,0:T(8,128)(2,1)S(1)}, u32[]{:S(2)}, u32[]{:S(2)}) collective-permute-start(bf16[8,96,768]{2,1,0:T(8,128)(2,1)S(1)} %add_convert_fusion.1), channel_id=1, source_target_pairs={{0,2},{1,5},{2,0},{3,7},{4,6},{5,1},{6,4},{7,3},{8,10},{9,13},{10,... | collective-permute-start | bytes 3538952 | tf_op jit(solution)/shard_map/ppermute | solution.py:528
  141.6 6.6 %copy-start.5 = (bf16[640,768]{1,0:T(8,128)(2,1)S(1)}, bf16[640,768]{1,0:T(8,128)(2,1)}, u32[]{:S(2)}) copy-start(bf16[640,768]{1,0:T(8,128)(2,1)} %copy-done.4) | copy-start | bytes 2949124
  148.2 5.6 %copy-start.11 = (bf16[16,24,3072]{2,1,0:T(8,128)(2,1)S(1)}, bf16[16,24,3072]{2,1,0:T(8,128)(2,1)}, u32[]{:S(2)}) copy-start(bf16[16,24,3072]{2,1,0:T(8,128)(2,1)} %get-tuple-element.320) | copy-start | bytes 7077892
  153.8 2.3 %collective-permute-start.29 = (bf16[8,24,1920]{2,1,0:T(8,128)(2,1)S(1)}, bf16[8,24,1920]{2,1,0:T(8,128)(2,1)S(1)}, u32[]{:S(2)}, u32[]{:S(2)}) collective-permute-start(bf16[8,24,1920]{2,1,0:T(8,128)(2,1)S(1)} %get-tuple-element.225), channel_id=1, source_target_pairs={{0,1},{1,0},{2,3},{3,2},{4,5},{5,4},{6,7},{7,6},{8,9},{9,8},{10,11... | collective-permute-start | bytes 2211848 | tf_op jit(solution)/shard_map/ppermute | solution.py:528
  154.3 18.0 %collective-permute-start.26 = (bf16[8,24,3072]{2,1,0:T(8,128)(2,1)S(1)}, bf16[8,24,3072]{2,1,0:T(8,128)(2,1)S(1)}, u32[]{:S(2)}, u32[]{:S(2)}) collective-permute-start(bf16[8,24,3072]{2,1,0:T(8,128)(2,1)S(1)} %add_convert_fusion), channel_id=1, source_target_pairs={{0,2},{1,5},{2,0},{3,7},{4,6},{5,1},{6,4},{7,3},{8,10},{9,13},{10,... | collective-permute-start | bytes 3538952 | tf_op jit(solution)/shard_map/ppermute | solution.py:528
  156.3 19.0 %collective-permute-start.31 = (bf16[4,96,768]{2,1,0:T(8,128)(2,1)S(1)}, bf16[4,96,768]{2,1,0:T(8,128)(2,1)S(1)}, u32[]{:S(2)}, u32[]{:S(2)}) collective-permute-start(bf16[4,96,768]{2,1,0:T(8,128)(2,1)S(1)} %add_convert_fusion.5), channel_id=1, source_target_pairs={{0,8},{1,9},{2,10},{3,11},{4,12},{5,13},{6,14},{7,15},{8,0},{9,1},... | collective-permute-start | bytes 1769480 | tf_op jit(solution)/shard_map/ppermute | solution.py:528
  158.0 8.3 %copy-start.2 = (bf16[4,160,768]{2,1,0:T(8,128)(2,1)S(1)}, bf16[4,160,768]{2,1,0:T(8,128)(2,1)}, u32[]{:S(2)}) copy-start(bf16[4,160,768]{2,1,0:T(8,128)(2,1)} %copy-done.1) | copy-start | bytes 2949124
  158.0 20.4 %collective-permute-start.33 = (bf16[8,24,1920]{2,1,0:T(8,128)(2,1)S(1)}, bf16[8,24,1920]{2,1,0:T(8,128)(2,1)S(1)}, u32[]{:S(2)}, u32[]{:S(2)}) collective-permute-start(bf16[8,24,1920]{2,1,0:T(8,128)(2,1)S(1)} %add_convert_fusion.2), channel_id=1, source_target_pairs={{0,2},{1,5},{2,0},{3,7},{4,6},{5,1},{6,4},{7,3},{8,10},{9,13},{10,... | collective-permute-start | bytes 2211848 | tf_op jit(solution)/shard_map/ppermute | solution.py:528
  171.7 12.5 %collective-permute-start.35 = (bf16[8,32,1152]{2,1,0:T(8,128)(2,1)S(1)}, bf16[8,32,1152]{2,1,0:T(8,128)(2,1)S(1)}, u32[]{:S(2)}, u32[]{:S(2)}) collective-permute-start(bf16[8,32,1152]{2,1,0:T(8,128)(2,1)S(1)} %get-tuple-element.261), channel_id=1, source_target_pairs={{0,1},{1,0},{2,3},{3,2},{4,5},{5,4},{6,7},{7,6},{8,9},{9,8},{10,11... | collective-permute-start | bytes 1769480 | tf_op jit(solution)/shard_map/ppermute | solution.py:528
  171.7 2.8 %collective-permute-start.34 = (bf16[8,32,1152]{2,1,0:T(8,128)(2,1)S(1)}, bf16[8,32,1152]{2,1,0:T(8,128)(2,1)S(1)}, u32[]{:S(2)}, u32[]{:S(2)}) collective-permute-start(bf16[8,32,1152]{2,1,0:T(8,128)(2,1)S(1)} %get-tuple-element.246), channel_id=1, source_target_pairs={{0,1},{1,0},{2,3},{3,2},{4,5},{5,4},{6,7},{7,6},{8,9},{9,8},{10,11... | collective-permute-start | bytes 1769480 | tf_op jit(solution)/shard_map/ppermute | solution.py:528
  172.2 3.4 %collective-permute-start.32 = (bf16[8,24,1920]{2,1,0:T(8,128)(2,1)S(1)}, bf16[8,24,1920]{2,1,0:T(8,128)(2,1)S(1)}, u32[]{:S(2)}, u32[]{:S(2)}) collective-permute-start(bf16[8,24,1920]{2,1,0:T(8,128)(2,1)S(1)} %get-tuple-element.243), channel_id=1, source_target_pairs={{0,1},{1,0},{2,3},{3,2},{4,5},{5,4},{6,7},{7,6},{8,9},{9,8},{10,11... | collective-permute-start | bytes 2211848 | tf_op jit(solution)/shard_map/ppermute | solution.py:528
  174.6 15.4 %collective-permute-start.30 = (bf16[4,24,3072]{2,1,0:T(8,128)(2,1)S(1)}, bf16[4,24,3072]{2,1,0:T(8,128)(2,1)S(1)}, u32[]{:S(2)}, u32[]{:S(2)}) collective-permute-start(bf16[4,24,3072]{2,1,0:T(8,128)(2,1)S(1)} %add_convert_fusion.4), channel_id=1, source_target_pairs={{0,8},{1,9},{2,10},{3,11},{4,12},{5,13},{6,14},{7,15},{8,0},{9,1},... | collective-permute-start | bytes 1769480 | tf_op jit(solution)/shard_map/ppermute | solution.py:528
  175.3 11.0 %collective-permute-start.36 = (bf16[8,32,1152]{2,1,0:T(8,128)(2,1)S(1)}, bf16[8,32,1152]{2,1,0:T(8,128)(2,1)S(1)}, u32[]{:S(2)}, u32[]{:S(2)}) collective-permute-start(bf16[8,32,1152]{2,1,0:T(8,128)(2,1)S(1)} %add_convert_fusion.3), channel_id=1, source_target_pairs={{0,2},{1,5},{2,0},{3,7},{4,6},{5,1},{6,4},{7,3},{8,10},{9,13},{10,... | collective-permute-start | bytes 1769480 | tf_op jit(solution)/shard_map/ppermute | solution.py:528
  181.9 10.0 %collective-permute-start.38 = (bf16[2,96,768]{2,1,0:T(8,128)(2,1)S(1)}, bf16[2,96,768]{2,1,0:T(8,128)(2,1)S(1)}, u32[]{:S(2)}, u32[]{:S(2)}) collective-permute-start(bf16[2,96,768]{2,1,0:T(8,128)(2,1)S(1)} %add_convert_fusion.9), channel_id=1, source_target_pairs={{0,4},{1,3},{2,6},{3,1},{4,0},{5,7},{6,2},{7,5},{8,12},{9,11},{10,... | collective-permute-start | bytes 884744 | tf_op jit(solution)/shard_map/ppermute | solution.py:528
  183.6 9.2 %collective-permute-start.37 = (bf16[4,24,1920]{2,1,0:T(8,128)(2,1)S(1)}, bf16[4,24,1920]{2,1,0:T(8,128)(2,1)S(1)}, u32[]{:S(2)}, u32[]{:S(2)}) collective-permute-start(bf16[4,24,1920]{2,1,0:T(8,128)(2,1)S(1)} %add_convert_fusion.6), channel_id=1, source_target_pairs={{0,4},{1,3},{2,6},{3,1},{4,0},{5,7},{6,2},{7,5},{8,12},{9,11},{10,... | collective-permute-start | bytes 1105928 | tf_op jit(solution)/shard_map/ppermute | solution.py:528
  186.4 9.4 %collective-permute-start.41 = (bf16[4,32,1152]{2,1,0:T(8,128)(2,1)S(1)}, bf16[4,32,1152]{2,1,0:T(8,128)(2,1)S(1)}, u32[]{:S(2)}, u32[]{:S(2)}) collective-permute-start(bf16[4,32,1152]{2,1,0:T(8,128)(2,1)S(1)} %add_convert_fusion.8), channel_id=1, source_target_pairs={{0,4},{1,3},{2,6},{3,1},{4,0},{5,7},{6,2},{7,5},{8,12},{9,11},{10,... | collective-permute-start | bytes 884744 | tf_op jit(solution)/shard_map/ppermute | solution.py:528
  190.1 8.9 %collective-permute-start.40 = (bf16[2,24,3072]{2,1,0:T(8,128)(2,1)S(1)}, bf16[2,24,3072]{2,1,0:T(8,128)(2,1)S(1)}, u32[]{:S(2)}, u32[]{:S(2)}) collective-permute-start(bf16[2,24,3072]{2,1,0:T(8,128)(2,1)S(1)} %add_convert_fusion.7), channel_id=1, source_target_pairs={{0,4},{1,3},{2,6},{3,1},{4,0},{5,7},{6,2},{7,5},{8,12},{9,11},{10,... | collective-permute-start | bytes 884744 | tf_op jit(solution)/shard_map/ppermute | solution.py:528
  192.0 15.2 %collective-permute-start.46 = (bf16[1,96,768]{2,1,0:T(8,128)(2,1)S(1)}, bf16[1,96,768]{2,1,0:T(8,128)(2,1)S(1)}, u32[]{:S(2)}, u32[]{:S(2)}) collective-permute-start(bf16[1,96,768]{2,1,0:T(8,128)(2,1)S(1)} %add_convert_fusion.13), channel_id=1, source_target_pairs={{0,16},{1,17},{2,18},{3,19},{4,20},{5,21},{6,22},{7,23},{8,24},{9,... | collective-permute-start | bytes 442376 | tf_op jit(solution)/shard_map/ppermute | solution.py:528
  192.8 9.2 %collective-permute-start.39 = (bf16[2,24,1920]{2,1,0:T(8,128)(2,1)S(1)}, bf16[2,24,1920]{2,1,0:T(8,128)(2,1)S(1)}, u32[]{:S(2)}, u32[]{:S(2)}) collective-permute-start(bf16[2,24,1920]{2,1,0:T(8,128)(2,1)S(1)} %add_convert_fusion.10), channel_id=1, source_target_pairs={{0,8},{1,9},{2,10},{3,11},{4,12},{5,13},{6,14},{7,15},{8,0},{9,1},... | collective-permute-start | bytes 552968 | tf_op jit(solution)/shard_map/ppermute | solution.py:528
  195.9 10.8 %collective-permute-start.43 = (bf16[2,32,1152]{2,1,0:T(8,128)(2,1)S(1)}, bf16[2,32,1152]{2,1,0:T(8,128)(2,1)S(1)}, u32[]{:S(2)}, u32[]{:S(2)}) collective-permute-start(bf16[2,32,1152]{2,1,0:T(8,128)(2,1)S(1)} %add_convert_fusion.12), channel_id=1, source_target_pairs={{0,8},{1,9},{2,10},{3,11},{4,12},{5,13},{6,14},{7,15},{8,0},{9,1},... | collective-permute-start | bytes 442376 | tf_op jit(solution)/shard_map/ppermute | solution.py:528
  199.1 14.4 %collective-permute-start.45 = (bf16[1,24,3072]{2,1,0:T(8,128)(2,1)S(1)}, bf16[1,24,3072]{2,1,0:T(8,128)(2,1)S(1)}, u32[]{:S(2)}, u32[]{:S(2)}) collective-permute-start(bf16[1,24,3072]{2,1,0:T(8,128)(2,1)S(1)} %add_convert_fusion.11), channel_id=1, source_target_pairs={{0,16},{1,17},{2,18},{3,19},{4,20},{5,21},{6,22},{7,23},{8,24},{9,... | collective-permute-start | bytes 442376 | tf_op jit(solution)/shard_map/ppermute | solution.py:528
  202.1 13.1 %collective-permute-start.42 = (bf16[1,24,1920]{2,1,0:T(8,128)(2,1)S(1)}, bf16[1,24,1920]{2,1,0:T(8,128)(2,1)S(1)}, u32[]{:S(2)}, u32[]{:S(2)}) collective-permute-start(bf16[1,24,1920]{2,1,0:T(8,128)(2,1)S(1)} %add_convert_fusion.14), channel_id=1, source_target_pairs={{0,16},{1,17},{2,18},{3,19},{4,20},{5,21},{6,22},{7,23},{8,24},{9,... | collective-permute-start | bytes 276488 | tf_op jit(solution)/shard_map/ppermute | solution.py:528
  206.7 9.2 %collective-permute-start.44 = (bf16[1,32,1152]{2,1,0:T(8,128)(2,1)S(1)}, bf16[1,32,1152]{2,1,0:T(8,128)(2,1)S(1)}, u32[]{:S(2)}, u32[]{:S(2)}) collective-permute-start(bf16[1,32,1152]{2,1,0:T(8,128)(2,1)S(1)} %add_convert_fusion.15), channel_id=1, source_target_pairs={{0,16},{1,17},{2,18},{3,19},{4,20},{5,21},{6,22},{7,23},{8,24},{9,... | collective-permute-start | bytes 221192 | tf_op jit(solution)/shard_map/ppermute | solution.py:528
  (15 other events, 30.4 us)
